TPU v7x, 32 devices: a whole 2x2x4 slice. The times are simulated.
32 devices in a mesh: dp: 4 (over y, x), mp: 8 (over z, core).
Axes of the slice: x: 2, y: 2, z: 4, core: 2. Of those that a mesh axis runs over, the one named last changes fastest.
Arguments:
- inputs: bfloat16 [32, 2560], P('dp'), may hold values from -6 to 6
- cotangent: bfloat16 [32, 2560], P('dp'), may hold values from -6 to 6
- w_in: bfloat16 [8, 16, 128, 128], P('mp', 'dp'), may hold values from -0.125 to 0.125
- w_out: bfloat16 [8, 16, 128, 128], P('mp', 'dp'), may hold values from -0.21875 to 0.21875
- block_index: int32 [8, 16], P('mp'), may hold values from 0 to 19, as said below
- block_count: int32 [8], P('mp'), may hold values from 8 to 16, as said below
- drop_seeds: int32 [32], P('dp'), may hold values from 0 to 1073741823
Outputs:
- outputs: bfloat16 [32, 2560], P(('dp', 'mp'))
- input_grad: bfloat16 [32, 2560], P(('dp', 'mp'))
- w_in_grad: float32 [8, 16, 128, 128], P('mp', 'dp')
- w_out_grad: float32 [8, 16, 128, 128], P('mp', 'dp')
Inputs may be any that keep to these rules, and one draw needn't show every extreme that they name: `block_index`: each row holds 16 different feature blocks; the first slots hold a few shared blocks and the blocks of a butterfly over the feature blocks. `block_count`: some hidden block uses all 16 slots and some uses 16 // 2.
All inputs are finite; a program needn't handle non-finite values.
Results may differ from a plain program's by a relative error of at most 0.012.
Values may be sent and summed in bfloat16 or wider, within the bound.
No kernel may reach another device: no remote copies, remote signals or barrier semaphores. Data moves between devices by JAX's collectives and lax.ppermute only.
A program may use at most 64 MiB of HBM per device.

v0:
```python
import math

import jax
import jax.numpy as jnp
from jax import lax
from jax.sharding import PartitionSpec as P

BS = 128
K = 16


def scramble(value):
    value = value ^ lax.shift_right_logical(value, jnp.int32(16))
    value = value * jnp.int32(73244475)
    value = value ^ lax.shift_right_logical(value, jnp.int32(16))
    value = value * jnp.int32(73244475)
    value = value ^ lax.shift_right_logical(value, jnp.int32(16))
    return value


def keep_factor(seeds, first_unit):
    units = first_unit + jnp.arange(BS, dtype=jnp.int32)
    mixed = scramble(seeds[:, None] + units[None, :] * jnp.int32(668265261))
    kept = mixed & jnp.int32(7) != jnp.int32(0)
    return kept.astype(jnp.float32) * jnp.float32(8.0 / 7.0)


def gelu_parts(pre_act):
    coeff = math.sqrt(2.0 / math.pi)
    inner = coeff * (pre_act + 0.044715 * pre_act**3)
    tanh_val = jnp.tanh(inner)
    activation = 0.5 * pre_act * (1.0 + tanh_val)
    slope = 0.5 * (1.0 + tanh_val) + 0.5 * pre_act * (1.0 - tanh_val * tanh_val) * coeff * (
        1.0 + 3.0 * 0.044715 * pre_act * pre_act
    )
    return (activation, slope)


def place_blocks(blocks, idx_row, block_cols):
    tok_rows = blocks.shape[0]
    placed = jnp.zeros((tok_rows, block_cols, BS), jnp.float32).at[:, idx_row].set(blocks)
    return placed.reshape(tok_rows, block_cols * BS)


def spread(partial_value):
    return lax.psum_scatter(partial_value, "mp", scatter_dimension=0, tiled=True).astype(
        jnp.bfloat16
    )


def body(inputs, cotangent, w_in, w_out, block_index, block_count, drop_seeds):
    tok_rows, feat_width = inputs.shape
    block_cols = feat_width // BS
    w_first, w_second = (
        lax.all_gather(w_in, "dp", axis=1, tiled=True),
        lax.all_gather(w_out, "dp", axis=1, tiled=True),
    )
    idx_row = block_index[0]
    valid = jnp.arange(K, dtype=jnp.int32) < block_count[0]
    valid_half = valid.astype(jnp.bfloat16)
    valid_full = valid.astype(jnp.float32)
    w1m = w_first[0] * valid_half[:, None, None]
    w2m = w_second[0] * valid_half[:, None, None]
    selected = jnp.take(inputs.reshape(tok_rows, block_cols, BS), idx_row, axis=1)
    pre_act = jnp.einsum("tkc,kcf->tf", selected, w1m, preferred_element_type=jnp.float32)
    activation, slope = gelu_parts(pre_act)
    keep_scale = keep_factor(drop_seeds, lax.axis_index("mp") * BS)
    dropped = (activation * keep_scale).astype(jnp.bfloat16)
    out_blocks = jnp.einsum("tf,kfc->tkc", dropped, w2m, preferred_element_type=jnp.float32)
    out_part = place_blocks(out_blocks, idx_row, block_cols)
    outputs = spread(out_part)
    cot_sel = jnp.take(cotangent.reshape(tok_rows, block_cols, BS), idx_row, axis=1)
    grad_drop = jnp.einsum("tkc,kfc->tf", cot_sel, w2m, preferred_element_type=jnp.float32)
    grad_pre = (grad_drop * keep_scale * slope).astype(jnp.bfloat16)
    in_blocks = jnp.einsum("tf,kcf->tkc", grad_pre, w1m, preferred_element_type=jnp.float32)
    in_part = place_blocks(in_blocks, idx_row, block_cols)
    input_grad = spread(in_part)
    term_in = (
        jnp.einsum("tkc,tf->kcf", selected, grad_pre, preferred_element_type=jnp.float32)
        * valid_full[:, None, None]
    )
    term_out = (
        jnp.einsum("tf,tkc->kfc", dropped, cot_sel, preferred_element_type=jnp.float32)
        * valid_full[:, None, None]
    )
    grad_in, grad_out = (
        lax.psum_scatter(
            term_in.astype(jnp.bfloat16), "dp", scatter_dimension=0, tiled=True
        ).astype(jnp.float32),
        lax.psum_scatter(
            term_out.astype(jnp.bfloat16), "dp", scatter_dimension=0, tiled=True
        ).astype(jnp.float32),
    )
    return (outputs, input_grad, grad_in[None], grad_out[None])


def solution(mesh):
    placed = (
        P("dp", None),
        P("dp", None),
        P("mp", "dp", None, None),
        P("mp", "dp", None, None),
        P("mp", None),
        P("mp"),
        P("dp"),
    )
    return jax.shard_map(
        body,
        mesh=mesh,
        in_specs=placed,
        out_specs=(
            P(("dp", "mp"), None),
            P(("dp", "mp"), None),
            P("mp", "dp", None, None),
            P("mp", "dp", None, None),
        ),
        check_vma=False,
    )
```

profile of v0, /device:TPU:0, one launch (start us, length us, event | category | flops | bytes accessed | tf_op | source)
XLA Modules:
  0.0 85.9 jit_solution(7901866068238466545)
XLA Ops:
  7.2 0.0 copy-start
  7.2 0.0 reduce-scatter.5.cloned.1.call-start
  7.2 0.7 compare_and_fusion
  8.6 11.8 %all_gather.6 = bf16[1,16,128,128]{3,2,0,1:T(8,128)(2,1)S(1)} all-gather(bf16[1,4,128,128]{3,2,0,1:T(8,128)(2,1)} %bitcast.71), channel_id=1, replica_groups=mesh['dp'=4,'mp'=8] {'dp'}, dimensions={1}, use_global_device_ids=true | all-gather | bytes 655360 | tf_op jit(solution)/shard_map/all_gather | solution.py:55
  20.4 0.0 copy-start.2
  20.5 0.6 gather_fusion
  21.0 0.2 copy-done.2
  21.2 0.6 gather_fusion.1
  21.8 0.2 convolution_bitcast_fusion.3
  22.1 0.7 copy-done.3
  22.7 1.2 %fusion.2 = bf16[16,128,128]{1,2,0:T(8,128)(2,1)} fusion(f32[16]{0:T(128)S(1)} %get-tuple-element.15, bf16[16,8,128]{2,1,0:T(8,128)(2,1)S(1)} %gather_fusion.1, pred[16]{0:T(512)(128)(4,1)S(1)} %compare_and_fusion, f32[8,128]{1,0:T(8,128)S(1)} %convolution_bitcast_fusion.3, s32[128]{0:T(128)S(1)} %add_multiply_fusion, s32[8]{0:T(128)S(1)} %copy-done.3), kind=kOutput, calls=%fused_computation.8 | convolution fusion | flops 4757504 | bytes 561776 | tf_op jit(solution)/shard_map/tf,tkc->kfc/dot_general | solution.py:83
  24.0 0.0 reduce-scatter.5.cloned.1.call-update
  24.0 0.0 reduce-scatter.3.cloned.1.call-start
  24.0 0.8 copy-done.1
  24.9 10.9 %all_gather.7 = bf16[1,16,128,128]{3,2,0,1:T(8,128)(2,1)S(1)} all-gather(bf16[1,4,128,128]{3,2,0,1:T(8,128)(2,1)S(1)} %bitcast.72), channel_id=1, replica_groups=mesh['dp'=4,'mp'=8] {'dp'}, dimensions={1}, use_global_device_ids=true | all-gather | bytes 655360 | tf_op jit(solution)/shard_map/all_gather | solution.py:56
  35.7 0.3 fusion.6
  36.1 1.2 %fusion = bf16[16,128,128]{2,1,0:T(8,128)(2,1)} fusion(bf16[8,128,1]{1,0,2:T(8,128)(2,1)S(1)} %fusion.6, f32[16]{0:T(128)S(1)} %get-tuple-element.15, bf16[16,8,128]{2,1,0:T(8,128)(2,1)S(1)} %gather_fusion, pred[16]{0:T(512)(128)(4,1)S(1)} %compare_and_fusion), kind=kOutput, calls=%fused_computation.6 | convolution fusion | flops 4734976 | bytes 559184 | tf_op jit(solution)/shard_map/tkc,tf->kcf/dot_general | solution.py:79
  37.3 0.0 reduce-scatter.3.cloned.1.call-update
  37.3 0.3 convolution_bitcast_fusion
  37.6 0.3 convolution_bitcast_fusion.1
  37.9 1.0 %scatter_fusion.1 = f32[8,20,128]{2,0,1:T(8,128)S(1)} fusion(f32[8,20,128]{2,0,1:T(8,128)S(1)} %broadcast.72.clone.1, s32[16]{0:T(128)S(1)} %fusion.29, f32[16,8,128]{2,1,0:T(8,128)S(1)} %convolution_bitcast_fusion), kind=kCustom, calls=%fused_computation.3 | custom fusion | bytes 196672 | tf_op jit(solution)/shard_map/scatter | solution.py:41
  38.9 1.0 %scatter_fusion = f32[8,20,128]{2,0,1:T(8,128)S(1)} fusion(f32[8,20,128]{2,0,1:T(8,128)S(1)} %broadcast.72.clone, s32[16]{0:T(128)S(1)} %fusion.29, f32[16,8,128]{2,1,0:T(8,128)S(1)} %convolution_bitcast_fusion.1), kind=kCustom, calls=%fused_computation.2 | custom fusion | bytes 196672 | tf_op jit(solution)/shard_map/scatter | solution.py:41
  40.0 0.0 copy-start.5
  40.0 0.6 copy-done.5
  40.6 0.6 dynamic-slice
  41.2 27.6 %all-reduce.4 = (bf16[8,2560]{1,0:T(8,128)(2,1)S(1)}, bf16[8,2560]{1,0:T(8,128)(2,1)S(1)}) all-reduce(f32[8,2560]{1,0:T(8,128)S(1)} %bitcast.69, f32[8,2560]{1,0:T(8,128)S(1)} %bitcast.70), channel_id=2, replica_groups=mesh['dp'=4,'mp'=8] {'mp'}, use_global_device_ids=true, to_apply=%region_1.3.clone | all-reduce | flops 40960 | bytes 245760
  68.8 1.3 %dynamic-slice_convert_fusion = bf16[1,2560]{1,0:T(2,128)(2,1)} fusion(bf16[8,2560]{1,0:T(8,128)(2,1)S(1)} %get-tuple-element.14, u32[]{:T(128)} %bitcast.23), kind=kLoop, calls=%fused_computation.31 | loop fusion | bytes 10244 | tf_op jit(solution)/shard_map/convert_element_type | solution.py:46
  70.1 1.3 %dynamic-slice_convert_fusion.1 = bf16[1,2560]{1,0:T(2,128)(2,1)} fusion(bf16[8,2560]{1,0:T(8,128)(2,1)S(1)} %get-tuple-element.13, u32[]{:T(128)} %bitcast.23), kind=kLoop, calls=%fused_computation.32 | loop fusion | bytes 10244 | tf_op jit(solution)/shard_map/convert_element_type | solution.py:46
  71.3 0.9 %bitcast_convert_fusion = f32[1,4,128,128]{2,3,1,0:T(8,128)S(1)} fusion(bf16[4,128,128]{1,2,0:T(8,128)(2,1)} %reduce-scatter.5.cloned.1.call-done), kind=kLoop, calls=%fused_computation.23 | loop fusion | flops 65536 | bytes 393216 | tf_op jit(solution)/shard_map/broadcast_in_dim | solution.py:94
  72.2 0.8 copy.14
  73.1 4.4 %reduce-scatter.3.cloned.1.call-done = bf16[4,128,128]{2,1,0:T(8,128)(2,1)} async-done(((bf16[16,128,128]{2,1,0:T(8,128)(2,1)}), bf16[4,128,128]{2,1,0:T(8,128)(2,1)}) %reduce-scatter.3.cloned.1.call-update) | async-done | bytes 131088 | tf_op jit(solution)/shard_map/reduce_scatter | solution.py:87
  77.5 1.6 %bitcast_convert_fusion.1 = f32[1,4,128,128]{3,2,1,0:T(8,128)} fusion(bf16[4,128,128]{2,1,0:T(8,128)(2,1)} %reduce-scatter.3.cloned.1.call-done), kind=kLoop, calls=%fused_computation.24 | loop fusion | flops 65536 | bytes 393216 | tf_op jit(solution)/shard_map/broadcast_in_dim | solution.py:94
  (13 shorter events, 0.0 us)
Async XLA Ops:
  7.2 13.3 %copy-start = (bf16[8,2560]{1,0:T(8,128)(2,1)S(1)}, bf16[8,2560]{1,0:T(8,128)(2,1)}, u32[]{:S(2)}) copy-start(bf16[8,2560]{1,0:T(8,128)(2,1)} %param.9) | copy-start | bytes 122884
  7.2 0.7 copy-start.4
  7.2 64.1 %reduce-scatter.5.cloned.1.call-start = ((), (), s32[]{:S(2)}) async-start(), calls=%async_computation.3 | async-start | bytes 655360 | tf_op jit(solution)/shard_map/reduce_scatter | solution.py:90
  20.4 0.8 copy-start.2
  22.1 0.7 copy-start.3
  23.9 0.9 %copy-start.1 = (bf16[1,4,128,128]{3,2,1,0:T(8,128)(2,1)S(1)}, bf16[1,4,128,128]{3,2,1,0:T(8,128)(2,1)}, u32[]{:S(2)}) copy-start(bf16[1,4,128,128]{3,2,1,0:T(8,128)(2,1)} %param.12) | copy-start | bytes 393220
  24.0 53.5 %reduce-scatter.3.cloned.1.call-start = ((), (), s32[]{:S(2)}) async-start(), calls=%async_computation.2 | async-start | bytes 655360 | tf_op jit(solution)/shard_map/reduce_scatter | solution.py:87
  40.0 0.7 copy-start.5
Sparse Core Ops, SparseCore 0:
  24.1 25.4 reduce-scatter.4
  52.7 24.7 reduce-scatter.2
where the time goes:
time: 86.3 us; the launch traced here: 85.9 us
  blocking collectives  50.3 us (58%)
  between operations  14.8 us (17%)
  local copies, waits for them, and re-layouts  9.49 us (11%)
  waiting for transfers between devices  4.43 us (5%)
  matrix products  3.58 us (4%)
  other arithmetic  3.25 us (4%)
    unnamed x1, blocking collectives  27.6 us
    all_gather x1, blocking collectives, body(): lax.all_gather(w_in, 'dp', axis=1, tiled=True)  11.8 us
    all_gather x1, blocking collectives, body(): lax.all_gather(w_out, 'dp', axis=1, tiled=True)  10.9 us
    reduce_scatter x1, waiting for transfers between devices, body(): lax.psum_scatter(term_in.astype(jnp.bfloat16), 'dp', scatter_dimension=0,...  4.4 us
    unnamed x14, local copies, waits for them, and re-layouts  3.78 us
    broadcast_in_dim x2, other arithmetic, body(): return (outputs, input_grad, grad_in[None], grad_out[None])  2.55 us
    convert_element_type x2, local copies, waits for them, and re-layouts, spread(): lax.psum_scatter(partial_value, 'mp', scatter_dimension=0, tiled=True)  2.52 us
    scatter x2, local copies, waits for them, and re-layouts, place_blocks(): jnp.zeros((tok_rows, block_cols, BS), jnp.float32).at[:, idx_row]  2.03 us
  transfers between devices with their start and end apart: 2, of which 1 were waited for; matrix products, arithmetic and copies ran while one was open for 11% of the time, Pallas kernels for 0%

commit v1 on v0

v1 whole, which is shorter than its diff:
```python
import functools
import math

import jax
import jax.numpy as jnp
from jax import lax
from jax.experimental import pallas as pl
from jax.experimental.pallas import tpu as pltpu
from jax.sharding import Mesh, PartitionSpec as P

BS = 128
F32 = jnp.float32
BF16 = jnp.bfloat16
VMEM_LIMIT = 48 * 2**20


def scramble(value):
    value = value ^ lax.shift_right_logical(value, jnp.int32(16))
    value = value * jnp.int32(73244475)
    value = value ^ lax.shift_right_logical(value, jnp.int32(16))
    value = value * jnp.int32(73244475)
    value = value ^ lax.shift_right_logical(value, jnp.int32(16))
    return value


def keep_factor(seeds, first_unit):
    units = first_unit + jnp.arange(BS, dtype=jnp.int32)
    mixed = scramble(seeds[:, None] + units[None, :] * jnp.int32(668265261))
    kept = mixed & jnp.int32(7) != jnp.int32(0)
    return kept.astype(F32) * jnp.float32(8.0 / 7.0)


def gelu_parts(pre_act):
    coeff = math.sqrt(2.0 / math.pi)
    inner = coeff * (pre_act + 0.044715 * pre_act**3)
    tanh_val = jnp.tanh(inner)
    activation = 0.5 * pre_act * (1.0 + tanh_val)
    slope = 0.5 * (1.0 + tanh_val) + 0.5 * pre_act * (1.0 - tanh_val * tanh_val) * coeff * (
        1.0 + 3.0 * 0.044715 * pre_act * pre_act
    )
    return (activation, slope)


def dot(left, right, dims):
    return lax.dot_general(left, right, (dims, ((), ())), preferred_element_type=F32)


def feature_block(pieces, index, used):
    at = pl.ds(pl.multiple_of(index * BS, BS), BS)
    rows = [piece[:, at].astype(F32) for piece in pieces]
    return (jnp.concatenate(rows, axis=0) * used).astype(BF16)


def slot(meta, which, slots):
    return meta[which], meta[2 * slots + which].astype(F32)


def partial_kernel(groups, slots, meta, *refs):
    toks, cots = refs[:groups], refs[groups : 2 * groups]
    keep, w1_own, w1_far, w2_own, w2_far, out = refs[2 * groups :]
    tokens = groups * toks[0].shape[0]
    pre = jnp.zeros((tokens, BS), F32)
    grad = jnp.zeros((tokens, BS), F32)
    for side, w1, w2 in ((0, w1_own, w2_own), (1, w1_far, w2_far)):
        for j in range(slots):
            index, used = slot(meta, side * slots + j, slots)
            pre += dot(feature_block(toks, index, used), w1[0, j], ((1,), (0,)))
            grad += dot(feature_block(cots, index, used), w2[0, j], ((1,), (1,)))
    out[:tokens] = pre
    out[tokens : 2 * tokens] = grad
    out[2 * tokens :] = keep[...]


def swap_halves(value):
    half = value.shape[0] // 2
    return jnp.concatenate([value[half:], value[:half]], axis=0)


def hidden_kernel(groups, slots, blocks, meta, *refs):
    toks, cots = refs[:groups], refs[groups : 2 * groups]
    mine, theirs, w1_own, w1_far, w2_own, w2_far, away, home, rows_far, rows_own, acc = refs[2 * groups :]
    tokens = groups * toks[0].shape[0]
    half = tokens // 2
    acc[...] = jnp.zeros_like(acc)
    pre = mine[:tokens] + swap_halves(theirs[:tokens])
    grad = mine[tokens : 2 * tokens] + swap_halves(theirs[tokens : 2 * tokens])
    keep = jnp.concatenate([mine[2 * tokens :], theirs[2 * tokens :]], axis=0)
    activation, slope = gelu_parts(pre)
    dropped = (activation * keep).astype(BF16)
    grad_pre = (grad * keep * slope).astype(BF16)
    for side, w1, w2 in ((0, w1_own, w2_own), (1, w1_far, w2_far)):
        for j in range(slots):
            index, used = slot(meta, side * slots + j, slots)
            out_block = dot(dropped, w2[0, j], ((1,), (0,))) * used
            in_block = dot(grad_pre, w1[0, j], ((1,), (1,))) * used
            acc[:, pl.ds(index, 1), :] = out_block.reshape(tokens, 1, BS)
            acc[:, pl.ds(blocks + index, 1), :] = in_block.reshape(tokens, 1, BS)
    away[...] = acc[half:].astype(BF16)
    home[...] = acc[:half]
    for side, rows in ((0, rows_own), (1, rows_far)):
        rows[:, :BS] = dropped
        rows[:, BS : 2 * BS] = grad_pre
        for j in range(slots):
            index, used = slot(meta, side * slots + j, slots)
            rows[:, (2 + j) * BS : (3 + j) * BS] = feature_block(toks, index, used)
            at = 2 + slots + j
            rows[:, at * BS : (at + 1) * BS] = feature_block(cots, index, used)


def grad_kernel(slots, own, far, grad_in, grad_out):
    def column(at):
        cut = slice(at * BS, (at + 1) * BS)
        return jnp.concatenate([own[:, cut], far[:, cut]], axis=0)

    dropped, grad_pre = column(0), column(1)
    for j in range(slots):
        grad_in[0, j] = dot(column(2 + j), grad_pre, ((0,), (0,)))
        grad_out[0, j] = dot(dropped, column(2 + slots + j), ((0,), (0,)))


def call(kernel, n_vmem, out_shape, flops, nbytes, scalars=True, scratch=()):
    vmem = pl.BlockSpec(memory_space=pltpu.VMEM)
    head = [pl.BlockSpec(memory_space=pltpu.SMEM)] if scalars else []
    return pl.pallas_call(
        kernel,
        out_shape=out_shape,
        in_specs=head + [vmem] * n_vmem,
        out_specs=jax.tree.map(lambda _: vmem, out_shape),
        scratch_shapes=list(scratch),
        compiler_params=pltpu.CompilerParams(vmem_limit_bytes=VMEM_LIMIT),
        cost_estimate=pl.CostEstimate(flops=flops, bytes_accessed=nbytes, transcendentals=0),
    )


def flip(value, axis, size, bit):
    return lax.ppermute(value, axis, [(i, i ^ bit) for i in range(size)])


def body(n_dy, n_mp, inputs, cotangent, w_in, w_out, block_index, block_count, drop_seeds):
    local, width = inputs.shape
    blocks = width // BS
    slots = w_in.shape[1]
    tokens = n_dy * local
    rank = lax.axis_index("mp")
    dx = lax.axis_index("dx")
    first = (lax.axis_index("dy") * 2 + dx) * slots

    w1_far = flip(w_in, "dx", 2, 1)
    w2_far = flip(w_out, "dx", 2, 1)
    toks, cots = [inputs], [cotangent]
    bit = 1
    while bit < n_dy:
        toks += [flip(piece, "dy", n_dy, bit) for piece in toks]
        cots += [flip(piece, "dy", n_dy, bit) for piece in cots]
        bit *= 2

    own_slots = first + jnp.arange(slots, dtype=jnp.int32)
    far_slots = own_slots + (1 - 2 * dx) * slots
    both = jnp.concatenate([own_slots, far_slots])
    used = (both < block_count[0]).astype(jnp.int32)
    meta = jnp.concatenate([block_index[0][both], used])
    keep = keep_factor(drop_seeds, rank * BS)

    shape = jax.ShapeDtypeStruct
    work = 2 * tokens * 2 * slots * 2 * BS * BS
    moved = 4 * slots * BS * BS * 2
    mine = call(
        functools.partial(partial_kernel, n_dy, slots),
        2 * n_dy + 5,
        shape((2 * tokens + local, BS), F32),
        work,
        moved,
    )(meta, *toks, *cots, keep, w_in, w1_far, w_out, w2_far)

    bit = 1
    while bit < n_dy:
        theirs = flip(mine, "dy", n_dy, bit)
        if 2 * bit < n_dy:

            def swapped(value):
                parts = value.reshape(n_dy // (2 * bit), 2, bit * local, BS)
                return parts[:, ::-1].reshape(tokens, BS)

            mine = jnp.concatenate(
                [
                    mine[:tokens] + swapped(theirs[:tokens]),
                    mine[tokens : 2 * tokens] + swapped(theirs[tokens : 2 * tokens]),
                    mine[2 * tokens :],
                    theirs[2 * tokens :],
                ]
            )
        bit *= 2

    half = tokens // 2
    away, total, rows_far, rows_own = call(
        functools.partial(hidden_kernel, n_dy, slots, blocks),
        2 * n_dy + 6,
        (
            shape((half, 2 * blocks, BS), BF16),
            shape((half, 2 * blocks, BS), F32),
            shape((tokens, (2 + 2 * slots) * BS), BF16),
            shape((tokens, (2 + 2 * slots) * BS), BF16),
        ),
        work,
        moved,
        scratch=[pltpu.VMEM((tokens, 2 * blocks, BS), F32)],
    )(meta, *toks, *cots, mine, theirs, w_in, w1_far, w_out, w2_far)

    bit = n_dy // 2
    total = total + flip(away, "dy", n_dy, bit).astype(F32)
    while bit > 1:
        bit //= 2
        cut = bit * local
        total = total[:cut] + flip(total[cut:].astype(BF16), "dy", n_dy, bit).astype(F32)

    rows_got = flip(rows_far, "dx", 2, 1)
    grad_in, grad_out = call(
        functools.partial(grad_kernel, slots),
        2,
        (shape((1, slots, BS, BS), F32), shape((1, slots, BS, BS), F32)),
        4 * tokens * slots * 2 * BS * BS,
        2 * slots * BS * BS * 4,
        scalars=False,
    )(rows_own, rows_got)

    bit = 1
    while bit < n_mp:
        mine_bit = (rank // bit) % 2
        pairs = total.reshape(total.shape[0] // 2, 2, 2 * blocks, BS)
        away = lax.dynamic_index_in_dim(pairs, 1 - mine_bit, 1, keepdims=False)
        total = lax.dynamic_index_in_dim(pairs, mine_bit, 1, keepdims=False)
        sent = F32 if bit == 1 else BF16
        total = total + flip(away.astype(sent), "mp", n_mp, bit).astype(F32)
        bit *= 2
    total = total.astype(BF16)
    rows = total.shape[0]
    outputs = total[:, :blocks].reshape(rows, width)
    input_grad = total[:, blocks:].reshape(rows, width)
    return (outputs, input_grad, grad_in, grad_out)


def solution(mesh):
    n_dp, n_mp = mesh.shape["dp"], mesh.shape["mp"]
    fine = Mesh(mesh.devices.reshape(n_dp // 2, 2, n_mp), ("dy", "dx", "mp"))
    dp = ("dy", "dx")
    placed = (
        P(dp, None),
        P(dp, None),
        P("mp", dp, None, None),
        P("mp", dp, None, None),
        P("mp", None),
        P("mp"),
        P(dp),
    )
    return jax.shard_map(
        functools.partial(body, n_dp // 2, n_mp),
        mesh=fine,
        in_specs=placed,
        out_specs=(
            P(("dy", "dx", "mp"), None),
            P(("dy", "dx", "mp"), None),
            P("mp", dp, None, None),
            P("mp", dp, None, None),
        ),
        check_vma=False,
    )
```

time: 86.3 us -> 33.2 us (0.38)
  blocking collectives: 50.3 us -> 0 us
  starting transfers between devices: 0.08 us -> 14.7 us
  between operations: 14.8 us -> 1.43 us
  local copies, waits for them, and re-layouts: 9.49 us -> 2.57 us
  waiting for transfers between devices: 4.43 us -> 11.1 us
  matrix products: 3.58 us -> 0 us
  other arithmetic: 3.25 us -> 0.37 us
  Pallas kernels: 0 us -> 2.8 us
    unnamed x1 -> x0, blocking collectives: 27.6 us -> none
    all_gather x2 -> x0, blocking collectives: 22.7 us -> none  [the longest x1 11.8 us: body(): lax.all_gather(w_in, 'dp', axis=1, tiled=True)]
    ppermute x0 -> x10, starting transfers between devices: none -> 14.7 us  [flip(): return lax.ppermute(value, axis, [(i, i ^ bit) for i in range(size)])]
    ppermute x0 -> x10, waiting for transfers between devices: none -> 11.1 us  [flip(): return lax.ppermute(value, axis, [(i, i ^ bit) for i in range(size)])]
    reduce_scatter x2 -> x0, waiting for transfers between devices: 4.4 us -> none  [the longest x1 4.4 us: body(): lax.psum_scatter(term_in.astype(jnp.bfloat16), 'dp', scatter_dimension=0,...]
    dot_general x6 -> x0, matrix products: 3.58 us -> none  [the longest x1 1.22 us: body(): jnp.einsum('tkc,tf->kcf', selected, grad_pre, preferred_element_type=jnp....]
    pallas_call x0 -> x3, Pallas kernels: none -> 2.8 us  [the longest x1 1.05 us: body(): call(functools.partial(grad_kernel, slots), 2, (shape((1, slots, BS, BS),...]
    broadcast_in_dim x2 -> x0, other arithmetic: 2.55 us -> none  [body(): return (outputs, input_grad, grad_in[None], grad_out[None])]
  transfers between devices with their start and end apart: 2 -> 10, of which waited for: 1 -> 7; matrix products, arithmetic and copies ran while one was open for 11% -> 3% of each run, Pallas kernels for 0% -> 3%
where the time goes in v1:
time: 33.2 us; the launch traced here: 33 us
  starting transfers between devices  14.7 us (44%)
  waiting for transfers between devices  11.1 us (33%)
  Pallas kernels  2.8 us (8%)
  local copies, waits for them, and re-layouts  2.57 us (8%)
  between operations  1.43 us (4%)
  other arithmetic  0.37 us (1%)
    ppermute x10, starting transfers between devices, flip(): return lax.ppermute(value, axis, [(i, i ^ bit) for i in range(size)])  14.7 us
    ppermute x10, waiting for transfers between devices, flip(): return lax.ppermute(value, axis, [(i, i ^ bit) for i in range(size)])  11.1 us
    unnamed x15, local copies, waits for them, and re-layouts  1.89 us
    pallas_call x1, Pallas kernels, body(): call(functools.partial(grad_kernel, slots), 2, (shape((1, slots, BS, BS),...  1.05 us
    pallas_call x1, Pallas kernels, body(): call(functools.partial(hidden_kernel, n_dy, slots, blocks), 2 * n_dy + 6,...  0.91 us
    pallas_call x1, Pallas kernels, body(): call(functools.partial(partial_kernel, n_dy, slots), 2 * n_dy + 5, shape(...  0.84 us
  transfers between devices with their start and end apart: 10, of which 7 were waited for; matrix products, arithmetic and copies ran while one was open for 3% of the time, Pallas kernels for 3%

profile of v1, /device:TPU:0, one launch (start us, length us, event | category | flops | bytes accessed | tf_op | source)
XLA Modules:
  0.0 33.0 jit_solution(4534485304519681181)
XLA Ops:
  0.6 0.0 copy-start
  0.6 3.0 %collective-permute-start = (bf16[8,2560]{1,0:T(8,128)(2,1)}, bf16[8,2560]{1,0:T(8,128)(2,1)S(1)}, u32[]{:S(2)}, u32[]{:S(2)}) collective-permute-start(bf16[8,2560]{1,0:T(8,128)(2,1)} %refs_0_.3), channel_id=1, source_target_pairs={{0,16},{16,0},{1,17},{17,1},{2,18},{18,2},{3,19},{19,3},{4,20},{20... | collective-permute-start | bytes 122888 | tf_op jit(solution)/shard_map/ppermute | solution.py:136
  3.7 0.1 collective-permute-start.1
  3.8 1.9 %collective-permute-start.2 = (bf16[1,4,128,128]{3,2,1,0:T(8,128)(2,1)}, bf16[1,4,128,128]{3,2,1,0:T(8,128)(2,1)S(1)}, u32[]{:S(2)}, u32[]{:S(2)}) collective-permute-start(bf16[1,4,128,128]{3,2,1,0:T(8,128)(2,1)} %refs_6_.1), channel_id=1, source_target_pairs={{0,8},{8,0},{1,9},{9,1},{2,10},{10,2},{3,11},{11,3},{4,12},{12,4},... | collective-permute-start | bytes 393224 | tf_op jit(solution)/shard_map/ppermute | solution.py:136
  5.7 0.1 collective-permute-start.3
  6.4 0.1 fusion.6
  6.5 0.6 %copy-done.5 = s32[8]{0:T(128)S(1)} copy-done((s32[8]{0:T(128)S(1)}, s32[8]{0:T(128)}, u32[]{:S(2)}) %copy-start.5) | copy-done | bytes 56
  7.2 0.1 fusion.5.refs_4_
  7.3 0.1 compare_convert_fusion
  7.4 0.0 copy-start.4
  7.4 0.6 %gather_fusion = s32[8]{0:T(128)S(1)} fusion(s32[16]{0:T(128)S(1)} %bitcast.28, s32[1024]{0:T(1024)S(1)} %pad_clamp_fusion), kind=kCustom, calls=%fused_computation | custom fusion | bytes 96 | tf_op jit(solution)/shard_map/gather | solution.py:161
  8.0 0.1 pad_add_fusion.meta
  8.1 0.0 collective-permute-done.refs_1_
  8.1 0.0 collective-permute-done.1.refs_3_
  8.1 2.2 %collective-permute-done.2.refs_6_.refs_7_ = bf16[1,4,128,128]{3,2,1,0:T(8,128)(2,1)S(1)} collective-permute-done((bf16[1,4,128,128]{3,2,1,0:T(8,128)(2,1)}, bf16[1,4,128,128]{3,2,1,0:T(8,128)(2,1)S(1)}, u32[]{:S(2)}, u32[]{:S(2)}) %collective-permute-start.2) | collective-permute-done | bytes 131104 | tf_op jit(solution)/shard_map/ppermute | solution.py:136
  10.3 1.4 %collective-permute-done.3.refs_8_.refs_9_ = bf16[1,4,128,128]{3,2,1,0:T(8,128)(2,1)S(1)} collective-permute-done((bf16[1,4,128,128]{3,2,1,0:T(8,128)(2,1)}, bf16[1,4,128,128]{3,2,1,0:T(8,128)(2,1)S(1)}, u32[]{:S(2)}, u32[]{:S(2)}) %collective-permute-start.3) | collective-permute-done | bytes 131104 | tf_op jit(solution)/shard_map/ppermute | solution.py:136
  11.8 0.8 %shard_map.102.refs_4_ = f32[40,128]{1,0:T(8,128)S(1)} custom-call(s32[16]{0:T(128)S(1)} %pad_add_fusion.meta, bf16[8,2560]{1,0:T(8,128)(2,1)S(1)} %copy-done.3, bf16[8,2560]{1,0:T(8,128)(2,1)S(1)} %collective-permute-done.refs_1_, bf16[8,2560]{1,0:T(8,128)(2,1)S(1)} %copy-done.4, bf16[8,2560]{1,0:T(8,128)(2,1)S(1)} %collective-permute-done.1.refs_3_, ...), custom_call_target="tpu_custom_call" | custom-call | flops 8388608 | bytes 524288 | tf_op jit(solution)/shard_map/pallas_call | solution.py:167
  12.6 1.7 %collective-permute-start.4 = (f32[40,128]{1,0:T(8,128)S(1)}, f32[40,128]{1,0:T(8,128)S(1)}, u32[]{:S(2)}, u32[]{:S(2)}) collective-permute-start(f32[40,128]{1,0:T(8,128)S(1)} %shard_map.102.refs_4_), channel_id=1, source_target_pairs={{0,16},{16,0},{1,17},{17,1},{2,18},{18,2},{3,19},{19,3},{4,20},{20... | collective-permute-start | bytes 61448 | tf_op jit(solution)/shard_map/ppermute | solution.py:136
  14.3 2.1 %collective-permute-done.4.refs_5_ = f32[40,128]{1,0:T(8,128)S(1)} collective-permute-done((f32[40,128]{1,0:T(8,128)S(1)}, f32[40,128]{1,0:T(8,128)S(1)}, u32[]{:S(2)}, u32[]{:S(2)}) %collective-permute-start.4) | collective-permute-done | bytes 20512 | tf_op jit(solution)/shard_map/ppermute | solution.py:136
  16.4 0.9 %shard_map.103 = (bf16[8,40,128]{2,1,0:T(8,128)(2,1)S(1)}, f32[8,40,128]{2,1,0:T(8,128)S(1)}, bf16[16,1280]{1,0:T(8,128)(2,1)S(1)}, bf16[16,1280]{1,0:T(8,128)(2,1)S(1)}) custom-call(s32[16]{0:T(128)S(1)} %pad_add_fusion.meta, bf16[8,2560]{1,0:T(8,128)(2,1)S(1)} %copy-done.3, bf16[8,2560]{1,0:T(8,128)(2,1)S(1)} %collective-permute-done.refs_1_, ...), custom_call_target="tpu_custom_call" | custom-call | flops 8388608 | bytes 524288 | tf_op jit(solution)/shard_map/pallas_call | solution.py:195
  17.3 1.7 %collective-permute-start.5 = (bf16[8,40,128]{2,1,0:T(8,128)(2,1)S(1)}, bf16[8,40,128]{2,1,0:T(8,128)(2,1)S(1)}, u32[]{:S(2)}, u32[]{:S(2)}) collective-permute-start(bf16[8,40,128]{2,1,0:T(8,128)(2,1)S(1)} %get-tuple-element.11), channel_id=1, source_target_pairs={{0,16},{16,0},{1,17},{17,1},{2,18},{18,2},{3,19},{19,3},{4,20},{20... | collective-permute-start | bytes 245768 | tf_op jit(solution)/shard_map/ppermute | solution.py:136
  19.1 2.8 %collective-permute-done.5 = bf16[8,40,128]{2,1,0:T(8,128)(2,1)S(1)} collective-permute-done((bf16[8,40,128]{2,1,0:T(8,128)(2,1)S(1)}, bf16[8,40,128]{2,1,0:T(8,128)(2,1)S(1)}, u32[]{:S(2)}, u32[]{:S(2)}) %collective-permute-start.5) | collective-permute-done | bytes 81952 | tf_op jit(solution)/shard_map/ppermute | solution.py:136
  21.9 0.1 collective-permute-start.6
  22.0 1.2 %collective-permute-done.6 = f32[4,40,128]{2,1,0:T(8,128)S(1)} collective-permute-done((f32[4,40,128]{2,1,0:T(8,128)S(1)}, f32[4,40,128]{2,1,0:T(8,128)S(1)}, u32[]{:S(2)}, u32[]{:S(2)}) %collective-permute-start.6) | collective-permute-done | bytes 81952 | tf_op jit(solution)/shard_map/ppermute | solution.py:136
  23.3 1.8 %collective-permute-start.7 = (bf16[2,40,128]{2,1,0:T(8,128)(2,1)S(1)}, bf16[2,40,128]{2,1,0:T(8,128)(2,1)S(1)}, u32[]{:S(2)}, u32[]{:S(2)}) collective-permute-start(bf16[2,40,128]{2,1,0:T(8,128)(2,1)S(1)} %fusion), channel_id=1, source_target_pairs={{0,2},{1,3},{2,0},{3,1},{4,6},{5,7},{6,4},{7,5},{8,10},{9,11},{10,... | collective-permute-start | bytes 61448 | tf_op jit(solution)/shard_map/ppermute | solution.py:136
  25.0 1.5 %collective-permute-start.9 = (bf16[16,1280]{1,0:T(8,128)(2,1)S(1)}, bf16[16,1280]{1,0:T(8,128)(2,1)S(1)}, u32[]{:S(2)}, u32[]{:S(2)}) collective-permute-start(bf16[16,1280]{1,0:T(8,128)(2,1)S(1)} %get-tuple-element.13), channel_id=1, source_target_pairs={{0,8},{8,0},{1,9},{9,1},{2,10},{10,2},{3,11},{11,3},{4,12},{12,4},... | collective-permute-start | bytes 122888 | tf_op jit(solution)/shard_map/ppermute | solution.py:136
  26.5 0.6 %collective-permute-done.7 = bf16[2,40,128]{2,1,0:T(8,128)(2,1)S(1)} collective-permute-done((bf16[2,40,128]{2,1,0:T(8,128)(2,1)S(1)}, bf16[2,40,128]{2,1,0:T(8,128)(2,1)S(1)}, u32[]{:S(2)}, u32[]{:S(2)}) %collective-permute-start.7) | collective-permute-done | bytes 20512 | tf_op jit(solution)/shard_map/ppermute | solution.py:136
  27.1 2.8 %collective-permute-start.8 = (bf16[1,40,128]{2,1,0:T(8,128)(2,1)S(1)}, bf16[1,40,128]{2,1,0:T(8,128)(2,1)S(1)}, u32[]{:S(2)}, u32[]{:S(2)}) collective-permute-start(bf16[1,40,128]{2,1,0:T(8,128)(2,1)S(1)} %dynamic-slice_convert_fusion.1), channel_id=1, source_target_pairs={{0,4},{1,5},{2,6},{3,7},{4,0},{5,1},{6,2},{7,3},{8,12},{9,13},{10,... | collective-permute-start | bytes 30728 | tf_op jit(solution)/shard_map/ppermute | solution.py:136
  29.9 1.0 %shard_map.104 = (f32[1,4,128,128]{3,2,1,0:T(8,128)}, f32[1,4,128,128]{3,2,1,0:T(8,128)}) custom-call(bf16[16,1280]{1,0:T(8,128)(2,1)S(1)} %get-tuple-element.12.own, bf16[16,1280]{1,0:T(8,128)(2,1)S(1)} %collective-permute-done.9.far), custom_call_target="tpu_custom_call" | custom-call | flops 8388608 | bytes 524288 | tf_op jit(solution)/shard_map/pallas_call | solution.py:217
  31.0 0.8 %collective-permute-done.8 = bf16[1,40,128]{2,1,0:T(8,128)(2,1)S(1)} collective-permute-done((bf16[1,40,128]{2,1,0:T(8,128)(2,1)S(1)}, bf16[1,40,128]{2,1,0:T(8,128)(2,1)S(1)}, u32[]{:S(2)}, u32[]{:S(2)}) %collective-permute-start.8) | collective-permute-done | bytes 10272 | tf_op jit(solution)/shard_map/ppermute | solution.py:136
  31.8 0.6 %copy.16 = bf16[1,1,20,128]{3,1,2,0:T(2,128)(2,1)} copy(bf16[1,1,20,128]{3,2,1,0:T(8,128)(2,1)S(1)} %get-tuple-element.17) | data formatting | bytes 10240
  32.4 0.6 %copy.15 = bf16[1,1,20,128]{3,1,2,0:T(2,128)(2,1)} copy(bf16[1,1,20,128]{3,2,1,0:T(8,128)(2,1)S(1)} %get-tuple-element.16) | data formatting | bytes 10240
  (22 shorter events, 0.1 us)
Async XLA Ops:
  0.6 6.7 %copy-start = (s32[1,16]{1,0:T(1,128)S(1)}, s32[1,16]{1,0:T(1,128)}, u32[]{:S(2)}) copy-start(s32[1,16]{1,0:T(1,128)} %param.11) | copy-start | bytes 196
  0.6 7.5 %collective-permute-start = (bf16[8,2560]{1,0:T(8,128)(2,1)}, bf16[8,2560]{1,0:T(8,128)(2,1)S(1)}, u32[]{:S(2)}, u32[]{:S(2)}) collective-permute-start(bf16[8,2560]{1,0:T(8,128)(2,1)} %refs_0_.3), channel_id=1, source_target_pairs={{0,16},{16,0},{1,17},{17,1},{2,18},{18,2},{3,19},{19,3},{4,20},{20... | collective-permute-start | bytes 122888 | tf_op jit(solution)/shard_map/ppermute | solution.py:136
  3.7 4.4 %collective-permute-start.1 = (bf16[8,2560]{1,0:T(8,128)(2,1)}, bf16[8,2560]{1,0:T(8,128)(2,1)S(1)}, u32[]{:S(2)}, u32[]{:S(2)}) collective-permute-start(bf16[8,2560]{1,0:T(8,128)(2,1)} %refs_2_.3), channel_id=1, source_target_pairs={{0,16},{16,0},{1,17},{17,1},{2,18},{18,2},{3,19},{19,3},{4,20},{20... | collective-permute-start | bytes 122888 | tf_op jit(solution)/shard_map/ppermute | solution.py:136
  3.8 6.6 %collective-permute-start.2 = (bf16[1,4,128,128]{3,2,1,0:T(8,128)(2,1)}, bf16[1,4,128,128]{3,2,1,0:T(8,128)(2,1)S(1)}, u32[]{:S(2)}, u32[]{:S(2)}) collective-permute-start(bf16[1,4,128,128]{3,2,1,0:T(8,128)(2,1)} %refs_6_.1), channel_id=1, source_target_pairs={{0,8},{8,0},{1,9},{9,1},{2,10},{10,2},{3,11},{11,3},{4,12},{12,4},... | collective-permute-start | bytes 393224 | tf_op jit(solution)/shard_map/ppermute | solution.py:136
  5.7 6.1 %collective-permute-start.3 = (bf16[1,4,128,128]{3,2,1,0:T(8,128)(2,1)}, bf16[1,4,128,128]{3,2,1,0:T(8,128)(2,1)S(1)}, u32[]{:S(2)}, u32[]{:S(2)}) collective-permute-start(bf16[1,4,128,128]{3,2,1,0:T(8,128)(2,1)} %refs_8_.1), channel_id=1, source_target_pairs={{0,8},{8,0},{1,9},{9,1},{2,10},{10,2},{3,11},{11,3},{4,12},{12,4},... | collective-permute-start | bytes 393224 | tf_op jit(solution)/shard_map/ppermute | solution.py:136
  6.5 0.7 %copy-start.5 = (s32[8]{0:T(128)S(1)}, s32[8]{0:T(128)}, u32[]{:S(2)}) copy-start(s32[8]{0:T(128)} %param.13) | copy-start | bytes 100
  7.3 4.4 %copy-start.1 = (bf16[1,4,128,128]{3,2,1,0:T(8,128)(2,1)S(1)}, bf16[1,4,128,128]{3,2,1,0:T(8,128)(2,1)}, u32[]{:S(2)}) copy-start(bf16[1,4,128,128]{3,2,1,0:T(8,128)(2,1)} %refs_6_.1) | copy-start | bytes 393220
  7.4 4.4 %copy-start.2 = (bf16[1,4,128,128]{3,2,1,0:T(8,128)(2,1)S(1)}, bf16[1,4,128,128]{3,2,1,0:T(8,128)(2,1)}, u32[]{:S(2)}) copy-start(bf16[1,4,128,128]{3,2,1,0:T(8,128)(2,1)} %refs_8_.1) | copy-start | bytes 393220
  7.4 4.4 %copy-start.3 = (bf16[8,2560]{1,0:T(8,128)(2,1)S(1)}, bf16[8,2560]{1,0:T(8,128)(2,1)}, u32[]{:S(2)}) copy-start(bf16[8,2560]{1,0:T(8,128)(2,1)} %refs_0_.3) | copy-start | bytes 122884
  7.4 4.4 %copy-start.4 = (bf16[8,2560]{1,0:T(8,128)(2,1)S(1)}, bf16[8,2560]{1,0:T(8,128)(2,1)}, u32[]{:S(2)}) copy-start(bf16[8,2560]{1,0:T(8,128)(2,1)} %refs_2_.3) | copy-start | bytes 122884
  12.6 3.8 %collective-permute-start.4 = (f32[40,128]{1,0:T(8,128)S(1)}, f32[40,128]{1,0:T(8,128)S(1)}, u32[]{:S(2)}, u32[]{:S(2)}) collective-permute-start(f32[40,128]{1,0:T(8,128)S(1)} %shard_map.102.refs_4_), channel_id=1, source_target_pairs={{0,16},{16,0},{1,17},{17,1},{2,18},{18,2},{3,19},{19,3},{4,20},{20... | collective-permute-start | bytes 61448 | tf_op jit(solution)/shard_map/ppermute | solution.py:136
  17.3 4.5 %collective-permute-start.5 = (bf16[8,40,128]{2,1,0:T(8,128)(2,1)S(1)}, bf16[8,40,128]{2,1,0:T(8,128)(2,1)S(1)}, u32[]{:S(2)}, u32[]{:S(2)}) collective-permute-start(bf16[8,40,128]{2,1,0:T(8,128)(2,1)S(1)} %get-tuple-element.11), channel_id=1, source_target_pairs={{0,16},{16,0},{1,17},{17,1},{2,18},{18,2},{3,19},{19,3},{4,20},{20... | collective-permute-start | bytes 245768 | tf_op jit(solution)/shard_map/ppermute | solution.py:136
  21.9 1.3 %collective-permute-start.6 = (f32[4,40,128]{2,1,0:T(8,128)S(1)}, f32[4,40,128]{2,1,0:T(8,128)S(1)}, u32[]{:S(2)}, u32[]{:S(2)}) collective-permute-start(f32[4,40,128]{2,1,0:T(8,128)S(1)} %dynamic-slice_bitcast_fusion), channel_id=1, source_target_pairs={{0,1},{1,0},{2,3},{3,2},{4,5},{5,4},{6,7},{7,6},{8,9},{9,8},{10,11... | collective-permute-start | bytes 245768 | tf_op jit(solution)/shard_map/ppermute | solution.py:136
  23.3 3.8 %collective-permute-start.7 = (bf16[2,40,128]{2,1,0:T(8,128)(2,1)S(1)}, bf16[2,40,128]{2,1,0:T(8,128)(2,1)S(1)}, u32[]{:S(2)}, u32[]{:S(2)}) collective-permute-start(bf16[2,40,128]{2,1,0:T(8,128)(2,1)S(1)} %fusion), channel_id=1, source_target_pairs={{0,2},{1,3},{2,0},{3,1},{4,6},{5,7},{6,4},{7,5},{8,10},{9,11},{10,... | collective-permute-start | bytes 61448 | tf_op jit(solution)/shard_map/ppermute | solution.py:136
  25.0 4.9 %collective-permute-start.9 = (bf16[16,1280]{1,0:T(8,128)(2,1)S(1)}, bf16[16,1280]{1,0:T(8,128)(2,1)S(1)}, u32[]{:S(2)}, u32[]{:S(2)}) collective-permute-start(bf16[16,1280]{1,0:T(8,128)(2,1)S(1)} %get-tuple-element.13), channel_id=1, source_target_pairs={{0,8},{8,0},{1,9},{9,1},{2,10},{10,2},{3,11},{11,3},{4,12},{12,4},... | collective-permute-start | bytes 122888 | tf_op jit(solution)/shard_map/ppermute | solution.py:136
  27.1 4.6 %collective-permute-start.8 = (bf16[1,40,128]{2,1,0:T(8,128)(2,1)S(1)}, bf16[1,40,128]{2,1,0:T(8,128)(2,1)S(1)}, u32[]{:S(2)}, u32[]{:S(2)}) collective-permute-start(bf16[1,40,128]{2,1,0:T(8,128)(2,1)S(1)} %dynamic-slice_convert_fusion.1), channel_id=1, source_target_pairs={{0,4},{1,5},{2,6},{3,7},{4,0},{5,1},{6,2},{7,3},{8,12},{9,13},{10,... | collective-permute-start | bytes 30728 | tf_op jit(solution)/shard_map/ppermute | solution.py:136

commit v2 on v0

v2 whole, which is shorter than its diff:
```python
import functools
import math

import jax
import jax.numpy as jnp
from jax import lax
from jax.experimental import pallas as pl
from jax.experimental.pallas import tpu as pltpu
from jax.sharding import PartitionSpec as P

BS = 128
F32 = jnp.float32
BF16 = jnp.bfloat16
VMEM_LIMIT = 48 * 2**20


def scramble(value):
    value = value ^ lax.shift_right_logical(value, jnp.int32(16))
    value = value * jnp.int32(73244475)
    value = value ^ lax.shift_right_logical(value, jnp.int32(16))
    value = value * jnp.int32(73244475)
    value = value ^ lax.shift_right_logical(value, jnp.int32(16))
    return value


def keep_factor(seeds, first_unit):
    units = first_unit + jnp.arange(BS, dtype=jnp.int32)
    mixed = scramble(seeds[:, None] + units[None, :] * jnp.int32(668265261))
    kept = mixed & jnp.int32(7) != jnp.int32(0)
    return kept.astype(F32) * jnp.float32(8.0 / 7.0)


def gelu_parts(pre_act):
    coeff = math.sqrt(2.0 / math.pi)
    inner = coeff * (pre_act + 0.044715 * pre_act**3)
    tanh_val = jnp.tanh(inner)
    activation = 0.5 * pre_act * (1.0 + tanh_val)
    slope = 0.5 * (1.0 + tanh_val) + 0.5 * pre_act * (1.0 - tanh_val * tanh_val) * coeff * (
        1.0 + 3.0 * 0.044715 * pre_act * pre_act
    )
    return (activation, slope)


def dot(left, right, dims):
    return lax.dot_general(left, right, (dims, ((), ())), preferred_element_type=F32)


def slot(block_index, block_count, first, at):
    number = first ^ at
    return block_index[0, number], (number < block_count[0]).astype(F32)


def block_of(picks, half, place):
    local = picks.shape[0] // 2
    rows = picks[:, place * BS : (place + 1) * BS].astype(F32)
    return rows[half * local : (half + 1) * local].astype(BF16)


def add_slots(slots, picks, pre, grad, masks_in, masks_out, weights):
    firsts, seconds = weights[: len(masks_in)], weights[len(masks_in) :]
    for mask, first in zip(masks_in, firsts):
        for j in range(slots):
            pre += dot(block_of(picks, 0, mask * slots + j), first[0, j], ((1,), (0,)))
    for mask, second in zip(masks_out, seconds):
        for j in range(slots):
            grad += dot(block_of(picks, 1, mask * slots + j), second[0, j], ((1,), (1,)))
    return pre, grad


def select_kernel(slots, masks_in, masks_out, block_index, block_count, tokens, *refs):
    *weights, picks, table, sums = refs
    first = lax.axis_index("dp") * slots
    local = sums.shape[0] // 2
    row = lax.broadcasted_iota(jnp.int32, table.shape, 0)
    lane = lax.broadcasted_iota(jnp.int32, table.shape, 1)
    entries = jnp.zeros(table.shape, jnp.int32)
    for place in range(picks.shape[1] // BS):
        index, used = slot(block_index, block_count, first, place)
        at = pl.ds(pl.multiple_of(index * BS, BS), BS)
        picks[:, place * BS : (place + 1) * BS] = (tokens[:, at].astype(F32) * used).astype(BF16)
        entry = jnp.where(row == 0, index, used.astype(jnp.int32))
        entries = jnp.where(lane == place, entry, entries)
    table[...] = entries
    zero = jnp.zeros((local, BS), F32)
    pre, grad = add_slots(slots, picks, zero, zero, masks_in, masks_out, weights)
    sums[:local] = pre
    sums[local:] = grad


def hold_kernel(first, second, held_first, held_second, sems):
    copies = [
        pltpu.make_async_copy(first, held_first, sems.at[0]),
        pltpu.make_async_copy(second, held_second, sems.at[1]),
    ]
    for copy in copies:
        copy.start()
    for copy in copies:
        copy.wait()


def partial_kernel(slots, masks_in, masks_out, picks, *refs):
    *weights, sums, out = refs
    local = picks.shape[0] // 2
    pre, grad = add_slots(slots, picks, sums[:local], sums[local:], masks_in, masks_out, weights)
    out[:local] = pre
    out[local:] = grad


def hidden_kernel(slots, blocks, masks_in, masks_out, late, picks, table, keep, sums, *refs):
    count = len(masks_in)
    firsts = dict(zip(masks_in, refs[:count]))
    seconds = dict(zip(masks_out, refs[count : 2 * count]))
    away, home, *rows = refs[2 * count : -1]
    acc = refs[-1]
    local = keep.shape[0]
    half = local // 2
    odd = lax.axis_index("mp") % 2
    acc[...] = jnp.zeros_like(acc)
    entries = table[...]
    pre, grad = add_slots(
        slots, picks, sums[:local], sums[local:], late, late, [firsts[m] for m in late] + [seconds[m] for m in late]
    )
    activation, slope = gelu_parts(pre)
    dropped_full = activation * keep[...]
    grad_full = grad * keep[...] * slope
    dropped, grad_pre = dropped_full.astype(BF16), grad_full.astype(BF16)
    for mask in range(count):
        for j in range(slots):
            at = mask * slots + j
            index, used = entries[0, at], entries[1, at].astype(F32)
            out_block = dot(dropped, seconds[mask][0, j], ((1,), (0,))) * used
            in_block = dot(grad_pre, firsts[mask][0, j], ((1,), (1,))) * used
            acc[:, :, pl.ds(index, 1), :] = out_block.reshape(half, 2, 1, BS)
            acc[:, :, pl.ds(blocks + index, 1), :] = in_block.reshape(half, 2, 1, BS)
    even_rows, odd_rows = acc[:, 0], acc[:, 1]
    away[...] = jnp.where(odd == 1, even_rows, odd_rows).astype(BF16)
    home[...] = jnp.where(odd == 1, odd_rows, even_rows)
    hidden = jnp.concatenate([dropped_full, grad_full], axis=0).astype(BF16)
    for mask, message in enumerate(rows):
        message[:, :BS] = hidden
        message[:, BS:] = picks[:, mask * slots * BS : (mask + 1) * slots * BS]


def all_rows(messages, half, place):
    return jnp.concatenate([block_of(message, half, place) for message in messages], axis=0)


def grad_kernel(slots, *refs):
    *messages, grad_in, grad_out, order = refs
    order[...] = jnp.zeros_like(order)
    dropped, grad_pre = all_rows(messages, 0, 0), all_rows(messages, 1, 0)
    for j in range(slots):
        grad_in[0, j] = dot(all_rows(messages, 0, 1 + j), grad_pre, ((0,), (0,)))
        grad_out[0, j] = dot(dropped, all_rows(messages, 1, 1 + j), ((0,), (0,)))


def last_kernel(blocks, kept, got, order, outputs, input_grad):
    for row in range(kept.shape[0]):
        total = kept[row] + got[row].astype(F32)
        for result, start in ((outputs, 0), (input_grad, blocks)):
            line = [total[start + i : start + i + 1] for i in range(blocks)]
            result[row : row + 1] = jnp.concatenate(line, axis=1).astype(BF16)


def call(kernel, n_vmem, out_shape, flops, nbytes, scalars=0, scratch=()):
    vmem = pl.BlockSpec(memory_space=pltpu.VMEM)
    head = [pl.BlockSpec(memory_space=pltpu.SMEM)] * scalars
    return pl.pallas_call(
        kernel,
        out_shape=out_shape,
        in_specs=head + [vmem] * n_vmem,
        out_specs=jax.tree.map(lambda _: vmem, out_shape),
        scratch_shapes=list(scratch),
        compiler_params=pltpu.CompilerParams(vmem_limit_bytes=VMEM_LIMIT),
        cost_estimate=pl.CostEstimate(flops=flops, bytes_accessed=nbytes, transcendentals=0),
    )


def flip(value, axis, size, mask):
    return lax.ppermute(value, axis, [(i, i ^ mask) for i in range(size)]) if mask else value


def gather(values, held, n_dp, orders):
    pieces = [{0: value} for value in values]
    for step, bits in enumerate(zip(*orders)):
        pieces = [
            {**parts, **{mask | bit: flip(part, "dp", n_dp, bit) for mask, part in parts.items()}}
            for parts, bit in zip(pieces, bits)
        ]
        if step == 0:
            for parts, own in zip(pieces, held):
                parts[0] = own
    return pieces


def exchange(messages, n_dp, bits):
    for bit in bits:
        size = messages[0].shape[1]
        leaving = jnp.concatenate([message for mask, message in enumerate(messages) if mask & bit], axis=1)
        arrived = flip(leaving, "dp", n_dp, bit)
        place = 0
        for mask in range(len(messages)):
            if mask & bit:
                messages[mask] = arrived[:, place * size : (place + 1) * size]
                place += 1
    return messages


def body(n_dp, n_mp, inputs, cotangent, w_in, w_out, block_index, block_count, drop_seeds):
    local, width = inputs.shape
    blocks = width // BS
    slots = w_in.shape[1]
    shape = jax.ShapeDtypeStruct
    piece_flops = 2 * local * slots * BS * BS
    piece_bytes = slots * BS * BS * 2

    bits = [1 << i for i in range(n_dp.bit_length() - 1)]
    held = pl.pallas_call(
        hold_kernel,
        out_shape=[shape(w_in.shape, BF16), shape(w_out.shape, BF16)],
        in_specs=[pl.BlockSpec(memory_space=pl.ANY)] * 2,
        out_specs=[pl.BlockSpec(memory_space=pltpu.VMEM)] * 2,
        scratch_shapes=[pltpu.SemaphoreType.DMA((2,))],
    )(w_in, w_out)
    firsts, seconds = gather([w_in, w_out], held, n_dp, [bits, bits[::-1]])

    rank = lax.axis_index("mp")
    keep = keep_factor(drop_seeds, rank * BS)
    steps = [([0, bits[0]], [0, bits[-1]])]
    late = [n_dp - 1]
    steps.append([[mask for mask in range(n_dp - 1) if mask not in done] for done in steps[0]])
    weights = [[firsts[m] for m in masks_in] + [seconds[m] for m in masks_out] for masks_in, masks_out in steps]
    picks, table, sums = call(
        functools.partial(select_kernel, slots, *steps[0]),
        1 + len(weights[0]),
        [
            shape((2 * local, n_dp * slots * BS), BF16),
            shape((8, BS), jnp.int32),
            shape((2 * local, BS), F32),
        ],
        0,
        0,
        scalars=2,
    )(block_index, block_count, jnp.concatenate([inputs, cotangent]), *weights[0])
    sums = call(
        functools.partial(partial_kernel, slots, *steps[1]),
        2 + len(weights[1]),
        shape((2 * local, BS), F32),
        0,
        0,
    )(picks, *weights[1], sums)

    half = local // 2
    masks_in, masks_out = sorted(firsts), sorted(seconds)
    away, home, *rows = call(
        functools.partial(hidden_kernel, slots, blocks, masks_in, masks_out, late),
        4 + 2 * n_dp,
        [shape((half, 2 * blocks, BS), BF16), shape((half, 2 * blocks, BS), F32)]
        + [shape((2 * local, (1 + slots) * BS), BF16)] * n_dp,
        (2 * n_dp + 2) * piece_flops,
        2 * n_dp * piece_bytes,
        scratch=[pltpu.VMEM((half, 2, 2 * blocks, BS), F32)],
    )(picks, table, keep, sums, *[firsts[m] for m in masks_in], *[seconds[m] for m in masks_out])

    total = home + flip(away, "mp", n_mp, 1).astype(F32)
    messages = exchange(rows, n_dp, bits)
    bit = 2
    while bit < n_mp:
        mine_bit = (rank // bit) % 2
        pairs = total.reshape(total.shape[0] // 2, 2, 2 * blocks, BS)
        away = lax.dynamic_index_in_dim(pairs, 1 - mine_bit, 1, keepdims=False)
        home = lax.dynamic_index_in_dim(pairs, mine_bit, 1, keepdims=False)
        got = flip(away.astype(BF16), "mp", n_mp, bit)
        total = home + got.astype(F32)
        bit *= 2

    grad_shape = shape((1, slots, BS, BS), F32)
    grad_in, grad_out, order = call(
        functools.partial(grad_kernel, slots),
        n_dp,
        [grad_shape, grad_shape, shape((8, BS), F32)],
        2 * n_dp * piece_flops,
        4 * piece_bytes,
    )(*messages)
    done = home.shape[0]
    outputs, input_grad = call(
        functools.partial(last_kernel, blocks),
        3,
        [shape((done, width), BF16), shape((done, width), BF16)],
        done * 2 * width,
        done * 2 * width * 8,
    )(home, got, order)
    return (outputs, input_grad, grad_in, grad_out)


def solution(mesh):
    placed = (
        P("dp", None),
        P("dp", None),
        P("mp", "dp", None, None),
        P("mp", "dp", None, None),
        P("mp", None),
        P("mp"),
        P("dp"),
    )
    return jax.shard_map(
        functools.partial(body, mesh.shape["dp"], mesh.shape["mp"]),
        mesh=mesh,
        in_specs=placed,
        out_specs=(
            P(("dp", "mp"), None),
            P(("dp", "mp"), None),
            P("mp", "dp", None, None),
            P("mp", "dp", None, None),
        ),
        check_vma=False,
    )
```

time: 86.3 us -> 27.2 us (0.32)
  blocking collectives: 50.3 us -> 0 us
  starting transfers between devices: 0.08 us -> 15.5 us
  between operations: 14.8 us -> 1.48 us
  local copies, waits for them, and re-layouts: 9.49 us -> 0.06 us
  Pallas kernels: 0 us -> 5.25 us
  matrix products: 3.58 us -> 0 us
  other arithmetic: 3.25 us -> 0.12 us
    unnamed x1 -> x0, blocking collectives: 27.6 us -> none
    all_gather x2 -> x0, blocking collectives: 22.7 us -> none  [the longest x1 11.8 us: body(): lax.all_gather(w_in, 'dp', axis=1, tiled=True)]
    ppermute x0 -> x11, starting transfers between devices: none -> 15.5 us  [flip(): lax.ppermute(value, axis, [(i, i ^ mask) for i in range(size)])]
    pallas_call x0 -> x6, Pallas kernels: none -> 5.25 us  [the longest x1 1.69 us: body(): pl.pallas_call(hold_kernel, out_shape=[shape(w_in.shape, BF16), shape(w_o...]
    ppermute x0 -> x11, waiting for transfers between devices: none -> 4.56 us  [flip(): lax.ppermute(value, axis, [(i, i ^ mask) for i in range(size)])]
    reduce_scatter x2 -> x0, waiting for transfers between devices: 4.4 us -> none  [the longest x1 4.4 us: body(): lax.psum_scatter(term_in.astype(jnp.bfloat16), 'dp', scatter_dimension=0,...]
    unnamed x14 -> x12, local copies, waits for them, and re-layouts: 3.78 us -> 0.03 us
    dot_general x6 -> x0, matrix products: 3.58 us -> none  [the longest x1 1.22 us: body(): jnp.einsum('tkc,tf->kcf', selected, grad_pre, preferred_element_type=jnp....]
  transfers between devices with their start and end apart: 2 -> 11, of which waited for: 1 -> 8; matrix products, arithmetic and copies ran while one was open for 11% -> 1% of each run, Pallas kernels for 0% -> 14%
where the time goes in v2:
time: 27.2 us; the launch traced here: 27 us
  starting transfers between devices  15.5 us (57%)
  Pallas kernels  5.25 us (19%)
  waiting for transfers between devices  4.56 us (17%)
  between operations  1.48 us (5%)
    ppermute x11, starting transfers between devices, flip(): lax.ppermute(value, axis, [(i, i ^ mask) for i in range(size)])  15.5 us
    ppermute x11, waiting for transfers between devices, flip(): lax.ppermute(value, axis, [(i, i ^ mask) for i in range(size)])  4.56 us
    pallas_call x1, Pallas kernels, body(): pl.pallas_call(hold_kernel, out_shape=[shape(w_in.shape, BF16), shape(w_o...  1.69 us
    pallas_call x1, Pallas kernels, body(): call(functools.partial(grad_kernel, slots), n_dp, [grad_shape, grad_shape...  1.04 us
    pallas_call x1, Pallas kernels, body(): call(functools.partial(hidden_kernel, slots, blocks, masks_in, masks_out,...  0.86 us
    pallas_call x1, Pallas kernels, body(): call(functools.partial(select_kernel, slots, *steps[0]), 1 + len(weights[...  0.84 us
    pallas_call x1, Pallas kernels, body(): call(functools.partial(last_kernel, blocks), 3, [shape((done, width), BF1...  0.62 us
  transfers between devices with their start and end apart: 11, of which 8 were waited for; matrix products, arithmetic and copies ran while one was open for 1% of the time, Pallas kernels for 14%

profile of v2, /device:TPU:0, one launch (start us, length us, event | category | flops | bytes accessed | tf_op | source)
XLA Modules:
  0.0 27.0 jit_solution(5410569563333094634)
XLA Ops:
  0.7 3.0 %collective-permute-start = (bf16[1,4,128,128]{3,2,1,0:T(8,128)(2,1)}, bf16[1,4,128,128]{3,2,1,0:T(8,128)(2,1)S(1)}, u32[]{:S(2)}, u32[]{:S(2)}) collective-permute-start(bf16[1,4,128,128]{3,2,1,0:T(8,128)(2,1)} %first.1), channel_id=1, source_target_pairs={{0,8},{8,0},{16,24},{24,16},{1,9},{9,1},{17,25},{25,17},{2,10},{10... | collective-permute-start | bytes 393224 | tf_op jit(solution)/shard_map/ppermute | solution.py:180
  3.7 1.5 %collective-permute-start.1 = (bf16[1,4,128,128]{3,2,1,0:T(8,128)(2,1)}, bf16[1,4,128,128]{3,2,1,0:T(8,128)(2,1)S(1)}, u32[]{:S(2)}, u32[]{:S(2)}) collective-permute-start(bf16[1,4,128,128]{3,2,1,0:T(8,128)(2,1)} %second.1), channel_id=1, source_target_pairs={{0,16},{8,24},{16,0},{24,8},{1,17},{9,25},{17,1},{25,9},{2,18},{10... | collective-permute-start | bytes 393224 | tf_op jit(solution)/shard_map/ppermute | solution.py:180
  5.2 1.7 %shard_map.102 = (bf16[1,4,128,128]{3,2,1,0:T(8,128)(2,1)}, bf16[1,4,128,128]{3,2,1,0:T(8,128)(2,1)}) custom-call(bf16[1,4,128,128]{3,2,1,0:T(8,128)(2,1)} %first.1, bf16[1,4,128,128]{3,2,1,0:T(8,128)(2,1)} %second.1), custom_call_target="tpu_custom_call" | custom-call | tf_op jit(solution)/shard_map/pallas_call | solution.py:218
  6.9 0.6 %collective-permute-start.2 = (bf16[1,4,128,128]{3,2,1,0:T(8,128)(2,1)}, bf16[1,4,128,128]{3,2,1,0:T(8,128)(2,1)S(1)}, u32[]{:S(2)}, u32[]{:S(2)}) collective-permute-start(bf16[1,4,128,128]{3,2,1,0:T(8,128)(2,1)} %get-tuple-element.20.refs_0_), channel_id=1, source_target_pairs={{0,16},{8,24},{16,0},{24,8},{1,17},{9,25},{17,1},{25,9},{2,18},{10... | collective-permute-start | bytes 393224 | tf_op jit(solution)/shard_map/ppermute | solution.py:180
  7.4 0.1 collective-permute-start.3
  8.3 0.0 copy-start.5
  8.3 0.0 copy-start.2
  8.3 0.0 collective-permute-done.refs_1_
  8.4 2.0 %collective-permute-start.4 = (bf16[1,4,128,128]{3,2,1,0:T(8,128)(2,1)S(1)}, bf16[1,4,128,128]{3,2,1,0:T(8,128)(2,1)S(1)}, u32[]{:S(2)}, u32[]{:S(2)}) collective-permute-start(bf16[1,4,128,128]{3,2,1,0:T(8,128)(2,1)S(1)} %collective-permute-done.refs_1_), channel_id=1, source_target_pairs={{0,16},{8,24},{16,0},{24,8},{1,17},{9,25},{17,1},{25,9},{2,18},{10... | collective-permute-start | bytes 393224 | tf_op jit(solution)/shard_map/ppermute | solution.py:180
  10.3 0.0 collective-permute-done.1.refs_3_.refs_6_
  10.4 1.5 %collective-permute-start.5 = (bf16[1,4,128,128]{3,2,1,0:T(8,128)(2,1)S(1)}, bf16[1,4,128,128]{3,2,1,0:T(8,128)(2,1)S(1)}, u32[]{:S(2)}, u32[]{:S(2)}) collective-permute-start(bf16[1,4,128,128]{3,2,1,0:T(8,128)(2,1)S(1)} %collective-permute-done.1.refs_3_.refs_6_), channel_id=1, source_target_pairs={{0,8},{8,0},{16,24},{24,16},{1,9},{9,1},{17,25},{25,17},{2,10},{10... | collective-permute-start | bytes 393224 | tf_op jit(solution)/shard_map/ppermute | solution.py:180
  11.8 0.0 copy-done.5
  11.8 0.1 fusion.5.keep
  11.9 0.8 %shard_map.103 = (bf16[16,2048]{1,0:T(8,128)(2,1)S(1)}, s32[8,128]{1,0:T(8,128)S(1)}, f32[16,128]{1,0:T(8,128)S(1)}) custom-call(s32[1,16]{1,0:T(1,128)S(1)} %copy-done.2, s32[1]{0:T(128)S(6)} %copy.13.block_count, bf16[16,2560]{1,0:T(8,128)(2,1)S(1)} %pad_maximum_fusion.tokens, bf16[1,4,128,128]{3,2,1,0:T(8,128)(2,1)S(1)} %copy-done, ...), custom_call_target="tpu_custom_call" | custom-call | tf_op jit(solution)/shard_map/pallas_call | solution.py:233
  12.8 0.4 %collective-permute-done.2.refs_0_.refs_2_ = bf16[1,4,128,128]{3,2,1,0:T(8,128)(2,1)S(1)} collective-permute-done((bf16[1,4,128,128]{3,2,1,0:T(8,128)(2,1)}, bf16[1,4,128,128]{3,2,1,0:T(8,128)(2,1)S(1)}, u32[]{:S(2)}, u32[]{:S(2)}) %collective-permute-start.2) | collective-permute-done | bytes 131104 | tf_op jit(solution)/shard_map/ppermute | solution.py:180
  13.2 0.6 %collective-permute-done.3.refs_1_.refs_5_ = bf16[1,4,128,128]{3,2,1,0:T(8,128)(2,1)S(1)} collective-permute-done((bf16[1,4,128,128]{3,2,1,0:T(8,128)(2,1)}, bf16[1,4,128,128]{3,2,1,0:T(8,128)(2,1)S(1)}, u32[]{:S(2)}, u32[]{:S(2)}) %collective-permute-start.3) | collective-permute-done | bytes 131104 | tf_op jit(solution)/shard_map/ppermute | solution.py:180
  13.9 0.2 shard_map.104.sums
  14.1 0.6 %collective-permute-done.4.refs_3_ = bf16[1,4,128,128]{3,2,1,0:T(8,128)(2,1)S(1)} collective-permute-done((bf16[1,4,128,128]{3,2,1,0:T(8,128)(2,1)S(1)}, bf16[1,4,128,128]{3,2,1,0:T(8,128)(2,1)S(1)}, u32[]{:S(2)}, u32[]{:S(2)}) %collective-permute-start.4) | collective-permute-done | bytes 131104 | tf_op jit(solution)/shard_map/ppermute | solution.py:180
  14.6 0.8 %collective-permute-done.5.refs_7_ = bf16[1,4,128,128]{3,2,1,0:T(8,128)(2,1)S(1)} collective-permute-done((bf16[1,4,128,128]{3,2,1,0:T(8,128)(2,1)S(1)}, bf16[1,4,128,128]{3,2,1,0:T(8,128)(2,1)S(1)}, u32[]{:S(2)}, u32[]{:S(2)}) %collective-permute-start.5) | collective-permute-done | bytes 131104 | tf_op jit(solution)/shard_map/ppermute | solution.py:180
  15.4 0.9 %shard_map.105 = (bf16[4,40,128]{2,1,0:T(8,128)(2,1)S(1)}, f32[4,40,128]{2,1,0:T(8,128)S(1)}, bf16[16,640]{1,0:T(8,128)(2,1)S(1)}, bf16[16,640]{1,0:T(8,128)(2,1...) custom-call(bf16[16,2048]{1,0:T(8,128)(2,1)S(1)} %get-tuple-element.22.picks, ...), custom_call_target="tpu_custom_call" | custom-call | flops 10485760 | bytes 1048576 | tf_op jit(solution)/shard_map/pallas_call | solution.py:255
  16.3 0.1 collective-permute-start.6
  16.4 1.4 %collective-permute-start.9 = (bf16[16,1280]{1,0:T(8,128)(2,1)S(1)}, bf16[16,1280]{1,0:T(8,128)(2,1)S(1)}, u32[]{:S(2)}, u32[]{:S(2)}) collective-permute-start(bf16[16,1280]{1,0:T(8,128)(2,1)S(1)} %pad_maximum_fusion.1), channel_id=1, source_target_pairs={{0,8},{8,0},{16,24},{24,16},{1,9},{9,1},{17,25},{25,17},{2,10},{10... | collective-permute-start | bytes 122888 | tf_op jit(solution)/shard_map/ppermute | solution.py:180
  17.8 0.0 collective-permute-done.6
  17.9 1.6 %collective-permute-start.7 = (bf16[2,40,128]{2,1,0:T(8,128)(2,1)S(1)}, bf16[2,40,128]{2,1,0:T(8,128)(2,1)S(1)}, u32[]{:S(2)}, u32[]{:S(2)}) collective-permute-start(bf16[2,40,128]{2,1,0:T(8,128)(2,1)S(1)} %fusion), channel_id=1, source_target_pairs={{0,2},{1,3},{2,0},{3,1},{4,6},{5,7},{6,4},{7,5},{8,10},{9,11},{10,... | collective-permute-start | bytes 61448 | tf_op jit(solution)/shard_map/ppermute | solution.py:180
  19.5 0.9 %collective-permute-done.9 = bf16[16,1280]{1,0:T(8,128)(2,1)S(1)} collective-permute-done((bf16[16,1280]{1,0:T(8,128)(2,1)S(1)}, bf16[16,1280]{1,0:T(8,128)(2,1)S(1)}, u32[]{:S(2)}, u32[]{:S(2)}) %collective-permute-start.9) | collective-permute-done | bytes 40992 | tf_op jit(solution)/shard_map/ppermute | solution.py:180
  20.5 1.0 %collective-permute-start.10 = (bf16[16,1280]{1,0:T(8,128)(2,1)S(1)}, bf16[16,1280]{1,0:T(8,128)(2,1)S(1)}, u32[]{:S(2)}, u32[]{:S(2)}) collective-permute-start(bf16[16,1280]{1,0:T(8,128)(2,1)S(1)} %pad_maximum_fusion.2), channel_id=1, source_target_pairs={{0,16},{8,24},{16,0},{24,8},{1,17},{9,25},{17,1},{25,9},{2,18},{10... | collective-permute-start | bytes 122888 | tf_op jit(solution)/shard_map/ppermute | solution.py:180
  21.5 0.2 collective-permute-done.7
  21.7 2.7 %collective-permute-start.8 = (bf16[1,40,128]{2,1,0:T(8,128)(2,1)S(1)}, bf16[1,40,128]{2,1,0:T(8,128)(2,1)S(1)}, u32[]{:S(2)}, u32[]{:S(2)}) collective-permute-start(bf16[1,40,128]{2,1,0:T(8,128)(2,1)S(1)} %dynamic-slice_convert_fusion), channel_id=1, source_target_pairs={{0,4},{1,5},{2,6},{3,7},{4,0},{5,1},{6,2},{7,3},{8,12},{9,13},{10,... | collective-permute-start | bytes 30728 | tf_op jit(solution)/shard_map/ppermute | solution.py:180
  24.4 0.1 collective-permute-done.10
  24.6 1.0 %shard_map.106 = (f32[1,4,128,128]{3,2,1,0:T(8,128)}, f32[1,4,128,128]{3,2,1,0:T(8,128)}, f32[8,128]{1,0:T(8,128)S(1)}) custom-call(bf16[16,640]{1,0:T(8,128)(2,1)S(1)} %get-tuple-element.27.refs_0_, bf16[16,640]{1,0:T(8,128)(2,1)S(1)} %get-tuple-element.39.refs_1_, bf16[16,640]{1,0:T(8,128)(2,1)S(1)} %get-tuple-element.37.refs_2_, ...), custom_call_target="tpu_custom_call" | custom-call | flops 8388608 | bytes 524288 | tf_op jit(solution)/shard_map/pallas_call | solution.py:278
  25.6 0.8 %collective-permute-done.8.got = bf16[1,40,128]{2,1,0:T(8,128)(2,1)S(1)} collective-permute-done((bf16[1,40,128]{2,1,0:T(8,128)(2,1)S(1)}, bf16[1,40,128]{2,1,0:T(8,128)(2,1)S(1)}, u32[]{:S(2)}, u32[]{:S(2)}) %collective-permute-start.8) | collective-permute-done | bytes 10272 | tf_op jit(solution)/shard_map/ppermute | solution.py:180
  26.4 0.6 %shard_map.107 = (bf16[1,2560]{1,0:T(2,128)(2,1)}, bf16[1,2560]{1,0:T(2,128)(2,1)}) custom-call(f32[1,40,128]{2,1,0:T(8,128)S(1)} %constant_dynamic-slice_fusion.kept, bf16[1,40,128]{2,1,0:T(8,128)(2,1)S(1)} %collective-permute-done.8.got, f32[8,128]{1,0:T(8,128)S(1)} %get-tuple-element.31.order), custom_call_target="tpu_custom_call" | custom-call | flops 5120 | bytes 40960 | tf_op jit(solution)/shard_map/pallas_call | solution.py:286
  (20 shorter events, 0.1 us)
Async XLA Ops:
  0.6 6.9 %copy-start.4 = (bf16[8,2560]{1,0:T(8,128)(2,1)S(1)}, bf16[8,2560]{1,0:T(8,128)(2,1)}, u32[]{:S(2)}) copy-start(bf16[8,2560]{1,0:T(8,128)(2,1)} %param.7) | copy-start | bytes 122884
  0.6 6.9 %copy-start.3 = (bf16[8,2560]{1,0:T(8,128)(2,1)S(1)}, bf16[8,2560]{1,0:T(8,128)(2,1)}, u32[]{:S(2)}) copy-start(bf16[8,2560]{1,0:T(8,128)(2,1)} %param.8) | copy-start | bytes 122884
  0.7 7.7 %collective-permute-start = (bf16[1,4,128,128]{3,2,1,0:T(8,128)(2,1)}, bf16[1,4,128,128]{3,2,1,0:T(8,128)(2,1)S(1)}, u32[]{:S(2)}, u32[]{:S(2)}) collective-permute-start(bf16[1,4,128,128]{3,2,1,0:T(8,128)(2,1)} %first.1), channel_id=1, source_target_pairs={{0,8},{8,0},{16,24},{24,16},{1,9},{9,1},{17,25},{25,17},{2,10},{10... | collective-permute-start | bytes 393224 | tf_op jit(solution)/shard_map/ppermute | solution.py:180
  3.7 6.7 %collective-permute-start.1 = (bf16[1,4,128,128]{3,2,1,0:T(8,128)(2,1)}, bf16[1,4,128,128]{3,2,1,0:T(8,128)(2,1)S(1)}, u32[]{:S(2)}, u32[]{:S(2)}) collective-permute-start(bf16[1,4,128,128]{3,2,1,0:T(8,128)(2,1)} %second.1), channel_id=1, source_target_pairs={{0,16},{8,24},{16,0},{24,8},{1,17},{9,25},{17,1},{25,9},{2,18},{10... | collective-permute-start | bytes 393224 | tf_op jit(solution)/shard_map/ppermute | solution.py:180
  6.9 6.4 %collective-permute-start.2 = (bf16[1,4,128,128]{3,2,1,0:T(8,128)(2,1)}, bf16[1,4,128,128]{3,2,1,0:T(8,128)(2,1)S(1)}, u32[]{:S(2)}, u32[]{:S(2)}) collective-permute-start(bf16[1,4,128,128]{3,2,1,0:T(8,128)(2,1)} %get-tuple-element.20.refs_0_), channel_id=1, source_target_pairs={{0,16},{8,24},{16,0},{24,8},{1,17},{9,25},{17,1},{25,9},{2,18},{10... | collective-permute-start | bytes 393224 | tf_op jit(solution)/shard_map/ppermute | solution.py:180
  7.4 4.5 %copy-start = (bf16[1,4,128,128]{3,2,1,0:T(8,128)(2,1)S(1)}, bf16[1,4,128,128]{3,2,1,0:T(8,128)(2,1)}, u32[]{:S(2)}) copy-start(bf16[1,4,128,128]{3,2,1,0:T(8,128)(2,1)} %get-tuple-element.20.refs_0_) | copy-start | bytes 393220
  7.4 4.5 %copy-start.1 = (bf16[1,4,128,128]{3,2,1,0:T(8,128)(2,1)S(1)}, bf16[1,4,128,128]{3,2,1,0:T(8,128)(2,1)}, u32[]{:S(2)}) copy-start(bf16[1,4,128,128]{3,2,1,0:T(8,128)(2,1)} %get-tuple-element.21.refs_2_.refs_4_) | copy-start | bytes 393220
  7.4 6.4 %collective-permute-start.3 = (bf16[1,4,128,128]{3,2,1,0:T(8,128)(2,1)}, bf16[1,4,128,128]{3,2,1,0:T(8,128)(2,1)S(1)}, u32[]{:S(2)}, u32[]{:S(2)}) collective-permute-start(bf16[1,4,128,128]{3,2,1,0:T(8,128)(2,1)} %get-tuple-element.21.refs_2_.refs_4_), channel_id=1, source_target_pairs={{0,8},{8,0},{16,24},{24,16},{1,9},{9,1},{17,25},{25,17},{2,10},{10... | collective-permute-start | bytes 393224 | tf_op jit(solution)/shard_map/ppermute | solution.py:180
  8.3 3.5 %copy-start.5 = (s32[8]{0:T(128)S(1)}, s32[8]{0:T(128)}, u32[]{:S(2)}) copy-start(s32[8]{0:T(128)} %param.13) | copy-start | bytes 100
  8.3 3.6 %copy-start.2 = (s32[1,16]{1,0:T(1,128)S(1)}, s32[1,16]{1,0:T(1,128)}, u32[]{:S(2)}) copy-start(s32[1,16]{1,0:T(1,128)} %block_index.1) | copy-start | bytes 196
  8.4 6.3 %collective-permute-start.4 = (bf16[1,4,128,128]{3,2,1,0:T(8,128)(2,1)S(1)}, bf16[1,4,128,128]{3,2,1,0:T(8,128)(2,1)S(1)}, u32[]{:S(2)}, u32[]{:S(2)}) collective-permute-start(bf16[1,4,128,128]{3,2,1,0:T(8,128)(2,1)S(1)} %collective-permute-done.refs_1_), channel_id=1, source_target_pairs={{0,16},{8,24},{16,0},{24,8},{1,17},{9,25},{17,1},{25,9},{2,18},{10... | collective-permute-start | bytes 393224 | tf_op jit(solution)/shard_map/ppermute | solution.py:180
  10.4 5.1 %collective-permute-start.5 = (bf16[1,4,128,128]{3,2,1,0:T(8,128)(2,1)S(1)}, bf16[1,4,128,128]{3,2,1,0:T(8,128)(2,1)S(1)}, u32[]{:S(2)}, u32[]{:S(2)}) collective-permute-start(bf16[1,4,128,128]{3,2,1,0:T(8,128)(2,1)S(1)} %collective-permute-done.1.refs_3_.refs_6_), channel_id=1, source_target_pairs={{0,8},{8,0},{16,24},{24,16},{1,9},{9,1},{17,25},{25,17},{2,10},{10... | collective-permute-start | bytes 393224 | tf_op jit(solution)/shard_map/ppermute | solution.py:180
  16.3 1.5 %collective-permute-start.6 = (bf16[4,40,128]{2,1,0:T(8,128)(2,1)S(1)}, bf16[4,40,128]{2,1,0:T(8,128)(2,1)S(1)}, u32[]{:S(2)}, u32[]{:S(2)}) collective-permute-start(bf16[4,40,128]{2,1,0:T(8,128)(2,1)S(1)} %get-tuple-element.26), channel_id=1, source_target_pairs={{0,1},{1,0},{2,3},{3,2},{4,5},{5,4},{6,7},{7,6},{8,9},{9,8},{10,11... | collective-permute-start | bytes 122888 | tf_op jit(solution)/shard_map/ppermute | solution.py:180
  16.4 4.1 %collective-permute-start.9 = (bf16[16,1280]{1,0:T(8,128)(2,1)S(1)}, bf16[16,1280]{1,0:T(8,128)(2,1)S(1)}, u32[]{:S(2)}, u32[]{:S(2)}) collective-permute-start(bf16[16,1280]{1,0:T(8,128)(2,1)S(1)} %pad_maximum_fusion.1), channel_id=1, source_target_pairs={{0,8},{8,0},{16,24},{24,16},{1,9},{9,1},{17,25},{25,17},{2,10},{10... | collective-permute-start | bytes 122888 | tf_op jit(solution)/shard_map/ppermute | solution.py:180
  17.9 3.8 %collective-permute-start.7 = (bf16[2,40,128]{2,1,0:T(8,128)(2,1)S(1)}, bf16[2,40,128]{2,1,0:T(8,128)(2,1)S(1)}, u32[]{:S(2)}, u32[]{:S(2)}) collective-permute-start(bf16[2,40,128]{2,1,0:T(8,128)(2,1)S(1)} %fusion), channel_id=1, source_target_pairs={{0,2},{1,3},{2,0},{3,1},{4,6},{5,7},{6,4},{7,5},{8,10},{9,11},{10,... | collective-permute-start | bytes 61448 | tf_op jit(solution)/shard_map/ppermute | solution.py:180
  20.5 4.1 %collective-permute-start.10 = (bf16[16,1280]{1,0:T(8,128)(2,1)S(1)}, bf16[16,1280]{1,0:T(8,128)(2,1)S(1)}, u32[]{:S(2)}, u32[]{:S(2)}) collective-permute-start(bf16[16,1280]{1,0:T(8,128)(2,1)S(1)} %pad_maximum_fusion.2), channel_id=1, source_target_pairs={{0,16},{8,24},{16,0},{24,8},{1,17},{9,25},{17,1},{25,9},{2,18},{10... | collective-permute-start | bytes 122888 | tf_op jit(solution)/shard_map/ppermute | solution.py:180
  21.7 4.6 %collective-permute-start.8 = (bf16[1,40,128]{2,1,0:T(8,128)(2,1)S(1)}, bf16[1,40,128]{2,1,0:T(8,128)(2,1)S(1)}, u32[]{:S(2)}, u32[]{:S(2)}) collective-permute-start(bf16[1,40,128]{2,1,0:T(8,128)(2,1)S(1)} %dynamic-slice_convert_fusion), channel_id=1, source_target_pairs={{0,4},{1,5},{2,6},{3,7},{4,0},{5,1},{6,2},{7,3},{8,12},{9,13},{10,... | collective-permute-start | bytes 30728 | tf_op jit(solution)/shard_map/ppermute | solution.py:180

commit v3 on v2

--- a/solution.py
+++ b/solution.py
@@ -45,9 +45,9 @@
     return lax.dot_general(left, right, (dims, ((), ())), preferred_element_type=F32)
 
 
-def slot(block_index, block_count, first, at):
+def slot(listed, count, first, at):
     number = first ^ at
-    return block_index[0, number], (number < block_count[0]).astype(F32)
+    return listed[number], (number < listed[count]).astype(F32)
 
 
 def block_of(picks, half, place):
@@ -56,52 +56,53 @@
     return rows[half * local : (half + 1) * local].astype(BF16)
 
 
-def add_slots(slots, picks, pre, grad, masks_in, masks_out, weights):
-    firsts, seconds = weights[: len(masks_in)], weights[len(masks_in) :]
+def side_by_side(weights, slots):
+    return jnp.concatenate([weights[0, j] for j in range(slots)], axis=1)
+
+
+def stacked(weights, slots):
+    return weights[0].reshape(slots * BS, BS)
+
+
+def add_slots(slots, picks, pre, grad, masks_in, masks_out, firsts, seconds):
+    local = picks.shape[0] // 2
+    span = slots * BS
     for mask, first in zip(masks_in, firsts):
-        for j in range(slots):
-            pre += dot(block_of(picks, 0, mask * slots + j), first[0, j], ((1,), (0,)))
+        rows = picks[:, mask * span : (mask + 1) * span].astype(F32)[:local].astype(BF16)
+        pre += dot(rows, stacked(first, slots), ((1,), (0,)))
     for mask, second in zip(masks_out, seconds):
-        for j in range(slots):
-            grad += dot(block_of(picks, 1, mask * slots + j), second[0, j], ((1,), (1,)))
+        rows = picks[:, mask * span : (mask + 1) * span].astype(F32)[local:].astype(BF16)
+        grad += dot(rows, side_by_side(second, slots), ((1,), (1,)))
     return pre, grad
 
 
-def select_kernel(slots, masks_in, masks_out, block_index, block_count, tokens, *refs):
+def select_kernel(slots, masks_in, masks_out, listed, tokens, *refs):
     *weights, picks, table, sums = refs
     first = lax.axis_index("dp") * slots
     local = sums.shape[0] // 2
     row = lax.broadcasted_iota(jnp.int32, table.shape, 0)
     lane = lax.broadcasted_iota(jnp.int32, table.shape, 1)
     entries = jnp.zeros(table.shape, jnp.int32)
-    for place in range(picks.shape[1] // BS):
-        index, used = slot(block_index, block_count, first, place)
+    count = picks.shape[1] // BS
+    for place in range(count):
+        index, used = slot(listed, count, first, place)
         at = pl.ds(pl.multiple_of(index * BS, BS), BS)
         picks[:, place * BS : (place + 1) * BS] = (tokens[:, at].astype(F32) * used).astype(BF16)
         entry = jnp.where(row == 0, index, used.astype(jnp.int32))
         entries = jnp.where(lane == place, entry, entries)
     table[...] = entries
     zero = jnp.zeros((local, BS), F32)
-    pre, grad = add_slots(slots, picks, zero, zero, masks_in, masks_out, weights)
+    firsts, seconds = weights[: len(masks_in)], weights[len(masks_in) :]
+    pre, grad = add_slots(slots, picks, zero, zero, masks_in, masks_out, firsts, seconds)
     sums[:local] = pre
     sums[local:] = grad
-
-
-def hold_kernel(first, second, held_first, held_second, sems):
-    copies = [
-        pltpu.make_async_copy(first, held_first, sems.at[0]),
-        pltpu.make_async_copy(second, held_second, sems.at[1]),
-    ]
-    for copy in copies:
-        copy.start()
-    for copy in copies:
-        copy.wait()
 
 
 def partial_kernel(slots, masks_in, masks_out, picks, *refs):
     *weights, sums, out = refs
     local = picks.shape[0] // 2
-    pre, grad = add_slots(slots, picks, sums[:local], sums[local:], masks_in, masks_out, weights)
+    seconds, firsts = weights[: len(masks_out)], weights[len(masks_out) :]
+    pre, grad = add_slots(slots, picks, sums[:local], sums[local:], masks_in, masks_out, firsts, seconds)
     out[:local] = pre
     out[local:] = grad
 
@@ -118,20 +119,21 @@
     acc[...] = jnp.zeros_like(acc)
     entries = table[...]
     pre, grad = add_slots(
-        slots, picks, sums[:local], sums[local:], late, late, [firsts[m] for m in late] + [seconds[m] for m in late]
+        slots, picks, sums[:local], sums[local:], late, late, [firsts[m] for m in late], [seconds[m] for m in late]
     )
     activation, slope = gelu_parts(pre)
     dropped_full = activation * keep[...]
     grad_full = grad * keep[...] * slope
     dropped, grad_pre = dropped_full.astype(BF16), grad_full.astype(BF16)
     for mask in range(count):
+        out_row = dot(dropped, side_by_side(seconds[mask], slots), ((1,), (0,)))
+        in_row = dot(grad_pre, stacked(firsts[mask], slots), ((1,), (1,)))
         for j in range(slots):
             at = mask * slots + j
             index, used = entries[0, at], entries[1, at].astype(F32)
-            out_block = dot(dropped, seconds[mask][0, j], ((1,), (0,))) * used
-            in_block = dot(grad_pre, firsts[mask][0, j], ((1,), (1,))) * used
-            acc[:, :, pl.ds(index, 1), :] = out_block.reshape(half, 2, 1, BS)
-            acc[:, :, pl.ds(blocks + index, 1), :] = in_block.reshape(half, 2, 1, BS)
+            cut = slice(j * BS, (j + 1) * BS)
+            acc[:, :, pl.ds(index, 1), :] = (out_row[:, cut] * used).reshape(half, 2, 1, BS)
+            acc[:, :, pl.ds(blocks + index, 1), :] = (in_row[:, cut] * used).reshape(half, 2, 1, BS)
     even_rows, odd_rows = acc[:, 0], acc[:, 1]
     away[...] = jnp.where(odd == 1, even_rows, odd_rows).astype(BF16)
     home[...] = jnp.where(odd == 1, odd_rows, even_rows)
@@ -190,6 +192,8 @@
         if step == 0:
             for parts, own in zip(pieces, held):
                 parts[0] = own
+    for parts, value in zip(pieces, values):
+        parts[0] = value
     return pieces
 
 
@@ -215,21 +219,18 @@
     piece_bytes = slots * BS * BS * 2
 
     bits = [1 << i for i in range(n_dp.bit_length() - 1)]
-    held = pl.pallas_call(
-        hold_kernel,
-        out_shape=[shape(w_in.shape, BF16), shape(w_out.shape, BF16)],
-        in_specs=[pl.BlockSpec(memory_space=pl.ANY)] * 2,
-        out_specs=[pl.BlockSpec(memory_space=pltpu.VMEM)] * 2,
-        scratch_shapes=[pltpu.SemaphoreType.DMA((2,))],
-    )(w_in, w_out)
+    *held, inputs, cotangent, block_index, block_count, seeds = lax.optimization_barrier(
+        (w_in, w_out, inputs, cotangent, block_index, block_count, flip(drop_seeds, "mp", n_mp, 1))
+    )
     firsts, seconds = gather([w_in, w_out], held, n_dp, [bits, bits[::-1]])
 
     rank = lax.axis_index("mp")
-    keep = keep_factor(drop_seeds, rank * BS)
+    keep = keep_factor(seeds, rank * BS)
     steps = [([0, bits[0]], [0, bits[-1]])]
     late = [n_dp - 1]
     steps.append([[mask for mask in range(n_dp - 1) if mask not in done] for done in steps[0]])
-    weights = [[firsts[m] for m in masks_in] + [seconds[m] for m in masks_out] for masks_in, masks_out in steps]
+    weights = [[firsts[m] for m in masks_in] + [seconds[m] for m in masks_out] for masks_in, masks_out in steps[:1]]
+    weights.append([seconds[m] for m in steps[1][1]] + [firsts[m] for m in steps[1][0]])
     picks, table, sums = call(
         functools.partial(select_kernel, slots, *steps[0]),
         1 + len(weights[0]),
@@ -240,8 +241,8 @@
         ],
         0,
         0,
-        scalars=2,
-    )(block_index, block_count, jnp.concatenate([inputs, cotangent]), *weights[0])
+        scalars=1,
+    )(jnp.concatenate([block_index[0], block_count]), jnp.concatenate([inputs, cotangent]), *weights[0])
     sums = call(
         functools.partial(partial_kernel, slots, *steps[1]),
         2 + len(weights[1]),
@@ -264,15 +265,15 @@
 
     total = home + flip(away, "mp", n_mp, 1).astype(F32)
     messages = exchange(rows, n_dp, bits)
-    bit = 2
-    while bit < n_mp:
+    bit = n_mp // 2
+    while bit > 1:
         mine_bit = (rank // bit) % 2
-        pairs = total.reshape(total.shape[0] // 2, 2, 2 * blocks, BS)
-        away = lax.dynamic_index_in_dim(pairs, 1 - mine_bit, 1, keepdims=False)
-        home = lax.dynamic_index_in_dim(pairs, mine_bit, 1, keepdims=False)
+        cut = total.shape[0] // 2
+        away = lax.dynamic_slice_in_dim(total, (1 - mine_bit) * cut, cut, 0)
+        home = lax.dynamic_slice_in_dim(total, mine_bit * cut, cut, 0)
         got = flip(away.astype(BF16), "mp", n_mp, bit)
         total = home + got.astype(F32)
-        bit *= 2
+        bit //= 2
 
     grad_shape = shape((1, slots, BS, BS), F32)
     grad_in, grad_out, order = call(

time: 27.2 us -> 26.8 us (0.985)
  Pallas kernels: 5.25 us -> 3.08 us
  other arithmetic: 0.12 us -> 0.99 us
  starting transfers between devices: 15.5 us -> 16.3 us
  local copies, waits for them, and re-layouts: 0.06 us -> 0.69 us
  waiting for transfers between devices: 4.56 us -> 4.06 us
    pallas_call x1 -> x0, Pallas kernels: 1.69 us -> none  [body(): pl.pallas_call(hold_kernel, out_shape=[shape(w_in.shape, BF16), shape(w_o...]
    concatenate x1, other arithmetic: 0.01 us -> 0.8 us  [body(): jnp.concatenate([inputs, cotangent])]
    ppermute x11 -> x12, starting transfers between devices: 15.5 us -> 16.3 us  [flip(): lax.ppermute(value, axis, [(i, i ^ mask) for i in range(size)])]
    unnamed x12 -> x6, local copies, waits for them, and re-layouts: 0.03 us -> 0.66 us
    ppermute x11 -> x12, waiting for transfers between devices: 4.56 us -> 4.06 us  [flip(): lax.ppermute(value, axis, [(i, i ^ mask) for i in range(size)])]
    pallas_call x1, Pallas kernels: 0.86 us -> 0.5 us  [body(): call(functools.partial(hidden_kernel, slots, blocks, masks_in, masks_out,...]
  transfers between devices with their start and end apart: 11 -> 12, of which waited for: 8 -> 6; matrix products, arithmetic and copies ran while one was open for 1% -> 4% of each run, Pallas kernels for 14% -> 7%
where the time goes in v3:
time: 26.8 us; the launch traced here: 26.6 us
  starting transfers between devices  16.3 us (61%)
  waiting for transfers between devices  4.06 us (15%)
  Pallas kernels  3.08 us (11%)
  between operations  1.44 us (5%)
  other arithmetic  0.99 us (4%)
  local copies, waits for them, and re-layouts  0.69 us (3%)
    ppermute x12, starting transfers between devices, flip(): lax.ppermute(value, axis, [(i, i ^ mask) for i in range(size)])  16.3 us
    ppermute x12, waiting for transfers between devices, flip(): lax.ppermute(value, axis, [(i, i ^ mask) for i in range(size)])  4.06 us
    pallas_call x1, Pallas kernels, body(): call(functools.partial(grad_kernel, slots), n_dp, [grad_shape, grad_shape...  1.05 us
    concatenate x1, other arithmetic, body(): jnp.concatenate([inputs, cotangent])  0.8 us
    pallas_call x1, Pallas kernels, body(): call(functools.partial(select_kernel, slots, *steps[0]), 1 + len(weights[...  0.75 us
    unnamed x6, local copies, waits for them, and re-layouts  0.66 us
    pallas_call x1, Pallas kernels, body(): call(functools.partial(last_kernel, blocks), 3, [shape((done, width), BF1...  0.62 us
  transfers between devices with their start and end apart: 12, of which 6 were waited for; matrix products, arithmetic and copies ran while one was open for 4% of the time, Pallas kernels for 7%

profile of v3, /device:TPU:0, one launch (start us, length us, event | category | flops | bytes accessed | tf_op | source)
XLA Modules:
  0.0 26.6 jit_solution(17059889902046950618)
XLA Ops:
  0.6 0.5 %collective-permute-start = (s32[8]{0:T(128)}, s32[8]{0:T(128)S(1)}, u32[]{:S(2)}, u32[]{:S(2)}) collective-permute-start(s32[8]{0:T(128)} %param.13), channel_id=1, source_target_pairs={{0,1},{1,0},{2,3},{3,2},{4,5},{5,4},{6,7},{7,6},{8,9},{9,8},{10,11... | collective-permute-start | bytes 104 | tf_op jit(solution)/shard_map/ppermute | solution.py:182
  1.2 2.6 %collective-permute-start.1 = (bf16[1,4,128,128]{3,2,1,0:T(8,128)(2,1)}, bf16[1,4,128,128]{3,2,1,0:T(8,128)(2,1)S(1)}, u32[]{:S(2)}, u32[]{:S(2)}) collective-permute-start(bf16[1,4,128,128]{3,2,1,0:T(8,128)(2,1)} %refs_0_.3), channel_id=1, source_target_pairs={{0,8},{8,0},{16,24},{24,16},{1,9},{9,1},{17,25},{25,17},{2,10},{10... | collective-permute-start | bytes 393224 | tf_op jit(solution)/shard_map/ppermute | solution.py:182
  3.7 1.5 %collective-permute-start.2 = (bf16[1,4,128,128]{3,2,1,0:T(8,128)(2,1)}, bf16[1,4,128,128]{3,2,1,0:T(8,128)(2,1)S(1)}, u32[]{:S(2)}, u32[]{:S(2)}) collective-permute-start(bf16[1,4,128,128]{3,2,1,0:T(8,128)(2,1)} %refs_4_.1), channel_id=1, source_target_pairs={{0,16},{8,24},{16,0},{24,8},{1,17},{9,25},{17,1},{25,9},{2,18},{10... | collective-permute-start | bytes 393224 | tf_op jit(solution)/shard_map/ppermute | solution.py:182
  6.0 0.0 collective-permute-done
  6.0 0.6 %collective-permute-start.3 = (bf16[1,4,128,128]{3,2,1,0:T(8,128)(2,1)}, bf16[1,4,128,128]{3,2,1,0:T(8,128)(2,1)S(1)}, u32[]{:S(2)}, u32[]{:S(2)}) collective-permute-start(bf16[1,4,128,128]{3,2,1,0:T(8,128)(2,1)} %refs_4_.1), channel_id=1, source_target_pairs={{0,8},{8,0},{16,24},{24,16},{1,9},{9,1},{17,25},{25,17},{2,10},{10... | collective-permute-start | bytes 393224 | tf_op jit(solution)/shard_map/ppermute | solution.py:182
  6.6 0.1 collective-permute-start.4
  6.6 0.8 %pad_maximum_fusion.tokens = bf16[16,2560]{1,0:T(8,128)(2,1)S(1)} fusion(bf16[8,2560]{1,0:T(8,128)(2,1)} %param.8, bf16[8,2560]{1,0:T(8,128)(2,1)} %param.7), kind=kLoop, calls=%fused_computation | loop fusion | flops 163840 | bytes 163840 | tf_op jit(solution)/shard_map/concatenate | solution.py:245
  7.5 0.6 %collective-permute-done.1.refs_1_ = bf16[1,4,128,128]{3,2,1,0:T(8,128)(2,1)S(1)} collective-permute-done((bf16[1,4,128,128]{3,2,1,0:T(8,128)(2,1)}, bf16[1,4,128,128]{3,2,1,0:T(8,128)(2,1)S(1)}, u32[]{:S(2)}, u32[]{:S(2)}) %collective-permute-start.1) | collective-permute-done | bytes 131104 | tf_op jit(solution)/shard_map/ppermute | solution.py:182
  8.0 2.2 %collective-permute-start.5 = (bf16[1,4,128,128]{3,2,1,0:T(8,128)(2,1)S(1)}, bf16[1,4,128,128]{3,2,1,0:T(8,128)(2,1)S(1)}, u32[]{:S(2)}, u32[]{:S(2)}) collective-permute-start(bf16[1,4,128,128]{3,2,1,0:T(8,128)(2,1)S(1)} %collective-permute-done.1.refs_1_), channel_id=1, source_target_pairs={{0,16},{8,24},{16,0},{24,8},{1,17},{9,25},{17,1},{25,9},{2,18},{10... | collective-permute-start | bytes 393224 | tf_op jit(solution)/shard_map/ppermute | solution.py:182
  10.3 0.0 collective-permute-done.2.refs_3_.refs_6_
  10.3 1.5 %collective-permute-start.6 = (bf16[1,4,128,128]{3,2,1,0:T(8,128)(2,1)S(1)}, bf16[1,4,128,128]{3,2,1,0:T(8,128)(2,1)S(1)}, u32[]{:S(2)}, u32[]{:S(2)}) collective-permute-start(bf16[1,4,128,128]{3,2,1,0:T(8,128)(2,1)S(1)} %collective-permute-done.2.refs_3_.refs_6_), channel_id=1, source_target_pairs={{0,8},{8,0},{16,24},{24,16},{1,9},{9,1},{17,25},{25,17},{2,10},{10... | collective-permute-start | bytes 393224 | tf_op jit(solution)/shard_map/ppermute | solution.py:182
  11.8 0.1 fusion.4.keep
  11.8 0.7 %copy-done.2 = s32[1,16]{1,0:T(1,128)S(1)} copy-done((s32[1,16]{1,0:T(1,128)S(1)}, s32[1,16]{1,0:T(1,128)}, u32[]{:S(2)}) %copy-start.2) | copy-done | bytes 88
  12.5 0.1 pad_add_fusion.listed
  12.6 0.7 %shard_map.102 = (bf16[16,2048]{1,0:T(8,128)(2,1)S(1)}, s32[8,128]{1,0:T(8,128)S(1)}, f32[16,128]{1,0:T(8,128)S(1)}) custom-call(s32[17]{0:T(128)S(1)} %pad_add_fusion.listed, bf16[16,2560]{1,0:T(8,128)(2,1)S(1)} %pad_maximum_fusion.tokens, bf16[1,4,128,128]{3,2,1,0:T(8,128)(2,1)S(1)} %copy-done, ...), custom_call_target="tpu_custom_call" | custom-call | tf_op jit(solution)/shard_map/pallas_call | solution.py:234
  13.3 0.0 collective-permute-done.3.refs_0_.refs_5_
  13.3 0.0 collective-permute-done.4.refs_1_.refs_2_
  13.4 0.2 shard_map.103.sums
  13.5 1.6 %collective-permute-done.5.refs_3_ = bf16[1,4,128,128]{3,2,1,0:T(8,128)(2,1)S(1)} collective-permute-done((bf16[1,4,128,128]{3,2,1,0:T(8,128)(2,1)S(1)}, bf16[1,4,128,128]{3,2,1,0:T(8,128)(2,1)S(1)}, u32[]{:S(2)}, u32[]{:S(2)}) %collective-permute-start.5) | collective-permute-done | bytes 131104 | tf_op jit(solution)/shard_map/ppermute | solution.py:182
  15.1 0.1 collective-permute-done.6.refs_7_
  15.2 0.5 %shard_map.104 = (bf16[4,40,128]{2,1,0:T(8,128)(2,1)S(1)}, f32[4,40,128]{2,1,0:T(8,128)S(1)}, bf16[16,640]{1,0:T(8,128)(2,1)S(1)}, bf16[16,640]{1,0:T(8,128)(2,1...) custom-call(bf16[16,2048]{1,0:T(8,128)(2,1)S(1)} %get-tuple-element.29.picks, ...), custom_call_target="tpu_custom_call" | custom-call | flops 10485760 | bytes 1048576 | tf_op jit(solution)/shard_map/pallas_call | solution.py:256
  15.7 0.1 collective-permute-start.7
  15.8 1.6 %collective-permute-start.10 = (bf16[16,1280]{1,0:T(8,128)(2,1)S(1)}, bf16[16,1280]{1,0:T(8,128)(2,1)S(1)}, u32[]{:S(2)}, u32[]{:S(2)}) collective-permute-start(bf16[16,1280]{1,0:T(8,128)(2,1)S(1)} %pad_maximum_fusion.1), channel_id=1, source_target_pairs={{0,8},{8,0},{16,24},{24,16},{1,9},{9,1},{17,25},{25,17},{2,10},{10... | collective-permute-start | bytes 122888 | tf_op jit(solution)/shard_map/ppermute | solution.py:182
  17.4 2.7 %collective-permute-start.8 = (bf16[2,40,128]{2,1,0:T(8,128)(2,1)S(1)}, bf16[2,40,128]{2,1,0:T(8,128)(2,1)S(1)}, u32[]{:S(2)}, u32[]{:S(2)}) collective-permute-start(bf16[2,40,128]{2,1,0:T(8,128)(2,1)S(1)} %dynamic-slice_convert_fusion), channel_id=1, source_target_pairs={{0,4},{1,5},{2,6},{3,7},{4,0},{5,1},{6,2},{7,3},{8,12},{9,13},{10,... | collective-permute-start | bytes 61448 | tf_op jit(solution)/shard_map/ppermute | solution.py:182
  20.1 0.0 collective-permute-done.10
  20.1 1.4 %collective-permute-start.11 = (bf16[16,1280]{1,0:T(8,128)(2,1)S(1)}, bf16[16,1280]{1,0:T(8,128)(2,1)S(1)}, u32[]{:S(2)}, u32[]{:S(2)}) collective-permute-start(bf16[16,1280]{1,0:T(8,128)(2,1)S(1)} %pad_maximum_fusion.2), channel_id=1, source_target_pairs={{0,16},{8,24},{16,0},{24,8},{1,17},{9,25},{17,1},{25,9},{2,18},{10... | collective-permute-start | bytes 122888 | tf_op jit(solution)/shard_map/ppermute | solution.py:182
  21.5 0.7 %collective-permute-done.8 = bf16[2,40,128]{2,1,0:T(8,128)(2,1)S(1)} collective-permute-done((bf16[2,40,128]{2,1,0:T(8,128)(2,1)S(1)}, bf16[2,40,128]{2,1,0:T(8,128)(2,1)S(1)}, u32[]{:S(2)}, u32[]{:S(2)}) %collective-permute-start.8) | collective-permute-done | bytes 20512 | tf_op jit(solution)/shard_map/ppermute | solution.py:182
  22.2 1.6 %collective-permute-start.9 = (bf16[1,40,128]{2,1,0:T(8,128)(2,1)S(1)}, bf16[1,40,128]{2,1,0:T(8,128)(2,1)S(1)}, u32[]{:S(2)}, u32[]{:S(2)}) collective-permute-start(bf16[1,40,128]{2,1,0:T(8,128)(2,1)S(1)} %dynamic-slice_convert_fusion.1), channel_id=1, source_target_pairs={{0,2},{1,3},{2,0},{3,1},{4,6},{5,7},{6,4},{7,5},{8,10},{9,11},{10,... | collective-permute-start | bytes 30728 | tf_op jit(solution)/shard_map/ppermute | solution.py:182
  23.8 0.3 %collective-permute-done.11 = bf16[16,1280]{1,0:T(8,128)(2,1)S(1)} collective-permute-done((bf16[16,1280]{1,0:T(8,128)(2,1)S(1)}, bf16[16,1280]{1,0:T(8,128)(2,1)S(1)}, u32[]{:S(2)}, u32[]{:S(2)}) %collective-permute-start.11) | collective-permute-done | bytes 40992 | tf_op jit(solution)/shard_map/ppermute | solution.py:182
  24.2 1.0 %shard_map.105 = (f32[1,4,128,128]{3,2,1,0:T(8,128)}, f32[1,4,128,128]{3,2,1,0:T(8,128)}, f32[8,128]{1,0:T(8,128)S(1)}) custom-call(bf16[16,640]{1,0:T(8,128)(2,1)S(1)} %get-tuple-element.37.refs_0_, bf16[16,640]{1,0:T(8,128)(2,1)S(1)} %get-tuple-element.49.refs_1_, bf16[16,640]{1,0:T(8,128)(2,1)S(1)} %get-tuple-element.47.refs_2_, ...), custom_call_target="tpu_custom_call" | custom-call | flops 8388608 | bytes 524288 | tf_op jit(solution)/shard_map/pallas_call | solution.py:279
  25.2 0.7 %collective-permute-done.9.got = bf16[1,40,128]{2,1,0:T(8,128)(2,1)S(1)} collective-permute-done((bf16[1,40,128]{2,1,0:T(8,128)(2,1)S(1)}, bf16[1,40,128]{2,1,0:T(8,128)(2,1)S(1)}, u32[]{:S(2)}, u32[]{:S(2)}) %collective-permute-start.9) | collective-permute-done | bytes 10272 | tf_op jit(solution)/shard_map/ppermute | solution.py:182
  26.0 0.6 %shard_map.106 = (bf16[1,2560]{1,0:T(2,128)(2,1)}, bf16[1,2560]{1,0:T(2,128)(2,1)}) custom-call(f32[1,40,128]{2,1,0:T(8,128)S(1)} %constant_dynamic-slice_fusion.kept, bf16[1,40,128]{2,1,0:T(8,128)(2,1)S(1)} %collective-permute-done.9.got, f32[8,128]{1,0:T(8,128)S(1)} %get-tuple-element.41.order), custom_call_target="tpu_custom_call" | custom-call | flops 5120 | bytes 40960 | tf_op jit(solution)/shard_map/pallas_call | solution.py:287
  (16 shorter events, 0.1 us)
Async XLA Ops:
  0.6 6.0 %copy-start = (bf16[1,4,128,128]{3,2,1,0:T(8,128)(2,1)S(1)}, bf16[1,4,128,128]{3,2,1,0:T(8,128)(2,1)}, u32[]{:S(2)}) copy-start(bf16[1,4,128,128]{3,2,1,0:T(8,128)(2,1)} %refs_0_.3) | copy-start | bytes 393220
  0.6 5.3 %collective-permute-start = (s32[8]{0:T(128)}, s32[8]{0:T(128)S(1)}, u32[]{:S(2)}, u32[]{:S(2)}) collective-permute-start(s32[8]{0:T(128)} %param.13), channel_id=1, source_target_pairs={{0,1},{1,0},{2,3},{3,2},{4,5},{5,4},{6,7},{7,6},{8,9},{9,8},{10,11... | collective-permute-start | bytes 104 | tf_op jit(solution)/shard_map/ppermute | solution.py:182
  1.2 6.9 %collective-permute-start.1 = (bf16[1,4,128,128]{3,2,1,0:T(8,128)(2,1)}, bf16[1,4,128,128]{3,2,1,0:T(8,128)(2,1)S(1)}, u32[]{:S(2)}, u32[]{:S(2)}) collective-permute-start(bf16[1,4,128,128]{3,2,1,0:T(8,128)(2,1)} %refs_0_.3), channel_id=1, source_target_pairs={{0,8},{8,0},{16,24},{24,16},{1,9},{9,1},{17,25},{25,17},{2,10},{10... | collective-permute-start | bytes 393224 | tf_op jit(solution)/shard_map/ppermute | solution.py:182
  3.7 6.5 %collective-permute-start.2 = (bf16[1,4,128,128]{3,2,1,0:T(8,128)(2,1)}, bf16[1,4,128,128]{3,2,1,0:T(8,128)(2,1)S(1)}, u32[]{:S(2)}, u32[]{:S(2)}) collective-permute-start(bf16[1,4,128,128]{3,2,1,0:T(8,128)(2,1)} %refs_4_.1), channel_id=1, source_target_pairs={{0,16},{8,24},{16,0},{24,8},{1,17},{9,25},{17,1},{25,9},{2,18},{10... | collective-permute-start | bytes 393224 | tf_op jit(solution)/shard_map/ppermute | solution.py:182
  5.2 7.3 %copy-start.1 = (bf16[1,4,128,128]{3,2,1,0:T(8,128)(2,1)S(1)}, bf16[1,4,128,128]{3,2,1,0:T(8,128)(2,1)}, u32[]{:S(2)}) copy-start(bf16[1,4,128,128]{3,2,1,0:T(8,128)(2,1)} %refs_4_.1) | copy-start | bytes 393220
  6.0 7.3 %collective-permute-start.3 = (bf16[1,4,128,128]{3,2,1,0:T(8,128)(2,1)}, bf16[1,4,128,128]{3,2,1,0:T(8,128)(2,1)S(1)}, u32[]{:S(2)}, u32[]{:S(2)}) collective-permute-start(bf16[1,4,128,128]{3,2,1,0:T(8,128)(2,1)} %refs_4_.1), channel_id=1, source_target_pairs={{0,8},{8,0},{16,24},{24,16},{1,9},{9,1},{17,25},{25,17},{2,10},{10... | collective-permute-start | bytes 393224 | tf_op jit(solution)/shard_map/ppermute | solution.py:182
  6.6 6.8 %collective-permute-start.4 = (bf16[1,4,128,128]{3,2,1,0:T(8,128)(2,1)S(1)}, bf16[1,4,128,128]{3,2,1,0:T(8,128)(2,1)S(1)}, u32[]{:S(2)}, u32[]{:S(2)}) collective-permute-start(bf16[1,4,128,128]{3,2,1,0:T(8,128)(2,1)S(1)} %copy-done), channel_id=1, source_target_pairs={{0,16},{8,24},{16,0},{24,8},{1,17},{9,25},{17,1},{25,9},{2,18},{10... | collective-permute-start | bytes 393224 | tf_op jit(solution)/shard_map/ppermute | solution.py:182
  8.0 7.1 %collective-permute-start.5 = (bf16[1,4,128,128]{3,2,1,0:T(8,128)(2,1)S(1)}, bf16[1,4,128,128]{3,2,1,0:T(8,128)(2,1)S(1)}, u32[]{:S(2)}, u32[]{:S(2)}) collective-permute-start(bf16[1,4,128,128]{3,2,1,0:T(8,128)(2,1)S(1)} %collective-permute-done.1.refs_1_), channel_id=1, source_target_pairs={{0,16},{8,24},{16,0},{24,8},{1,17},{9,25},{17,1},{25,9},{2,18},{10... | collective-permute-start | bytes 393224 | tf_op jit(solution)/shard_map/ppermute | solution.py:182
  10.3 5.0 %collective-permute-start.6 = (bf16[1,4,128,128]{3,2,1,0:T(8,128)(2,1)S(1)}, bf16[1,4,128,128]{3,2,1,0:T(8,128)(2,1)S(1)}, u32[]{:S(2)}, u32[]{:S(2)}) collective-permute-start(bf16[1,4,128,128]{3,2,1,0:T(8,128)(2,1)S(1)} %collective-permute-done.2.refs_3_.refs_6_), channel_id=1, source_target_pairs={{0,8},{8,0},{16,24},{24,16},{1,9},{9,1},{17,25},{25,17},{2,10},{10... | collective-permute-start | bytes 393224 | tf_op jit(solution)/shard_map/ppermute | solution.py:182
  11.8 0.7 %copy-start.2 = (s32[1,16]{1,0:T(1,128)S(1)}, s32[1,16]{1,0:T(1,128)}, u32[]{:S(2)}) copy-start(s32[1,16]{1,0:T(1,128)} %param.11) | copy-start | bytes 196
  15.7 1.7 %collective-permute-start.7 = (bf16[4,40,128]{2,1,0:T(8,128)(2,1)S(1)}, bf16[4,40,128]{2,1,0:T(8,128)(2,1)S(1)}, u32[]{:S(2)}, u32[]{:S(2)}) collective-permute-start(bf16[4,40,128]{2,1,0:T(8,128)(2,1)S(1)} %get-tuple-element.36), channel_id=1, source_target_pairs={{0,1},{1,0},{2,3},{3,2},{4,5},{5,4},{6,7},{7,6},{8,9},{9,8},{10,11... | collective-permute-start | bytes 122888 | tf_op jit(solution)/shard_map/ppermute | solution.py:182
  15.8 4.3 %collective-permute-start.10 = (bf16[16,1280]{1,0:T(8,128)(2,1)S(1)}, bf16[16,1280]{1,0:T(8,128)(2,1)S(1)}, u32[]{:S(2)}, u32[]{:S(2)}) collective-permute-start(bf16[16,1280]{1,0:T(8,128)(2,1)S(1)} %pad_maximum_fusion.1), channel_id=1, source_target_pairs={{0,8},{8,0},{16,24},{24,16},{1,9},{9,1},{17,25},{25,17},{2,10},{10... | collective-permute-start | bytes 122888 | tf_op jit(solution)/shard_map/ppermute | solution.py:182
  17.4 4.8 %collective-permute-start.8 = (bf16[2,40,128]{2,1,0:T(8,128)(2,1)S(1)}, bf16[2,40,128]{2,1,0:T(8,128)(2,1)S(1)}, u32[]{:S(2)}, u32[]{:S(2)}) collective-permute-start(bf16[2,40,128]{2,1,0:T(8,128)(2,1)S(1)} %dynamic-slice_convert_fusion), channel_id=1, source_target_pairs={{0,4},{1,5},{2,6},{3,7},{4,0},{5,1},{6,2},{7,3},{8,12},{9,13},{10,... | collective-permute-start | bytes 61448 | tf_op jit(solution)/shard_map/ppermute | solution.py:182
  20.1 4.1 %collective-permute-start.11 = (bf16[16,1280]{1,0:T(8,128)(2,1)S(1)}, bf16[16,1280]{1,0:T(8,128)(2,1)S(1)}, u32[]{:S(2)}, u32[]{:S(2)}) collective-permute-start(bf16[16,1280]{1,0:T(8,128)(2,1)S(1)} %pad_maximum_fusion.2), channel_id=1, source_target_pairs={{0,16},{8,24},{16,0},{24,8},{1,17},{9,25},{17,1},{25,9},{2,18},{10... | collective-permute-start | bytes 122888 | tf_op jit(solution)/shard_map/ppermute | solution.py:182
  22.2 3.7 %collective-permute-start.9 = (bf16[1,40,128]{2,1,0:T(8,128)(2,1)S(1)}, bf16[1,40,128]{2,1,0:T(8,128)(2,1)S(1)}, u32[]{:S(2)}, u32[]{:S(2)}) collective-permute-start(bf16[1,40,128]{2,1,0:T(8,128)(2,1)S(1)} %dynamic-slice_convert_fusion.1), channel_id=1, source_target_pairs={{0,2},{1,3},{2,0},{3,1},{4,6},{5,7},{6,4},{7,5},{8,10},{9,11},{10,... | collective-permute-start | bytes 30728 | tf_op jit(solution)/shard_map/ppermute | solution.py:182

commit v4 on v3

--- a/solution.py
+++ b/solution.py
@@ -194,6 +194,8 @@
                 parts[0] = own
     for parts, value in zip(pieces, values):
         parts[0] = value
+        for mask in parts:
+            parts[mask] = parts[mask].reshape(value.shape)
     return pieces
 
 
@@ -219,13 +221,10 @@
     piece_bytes = slots * BS * BS * 2
 
     bits = [1 << i for i in range(n_dp.bit_length() - 1)]
-    *held, inputs, cotangent, block_index, block_count, seeds = lax.optimization_barrier(
-        (w_in, w_out, inputs, cotangent, block_index, block_count, flip(drop_seeds, "mp", n_mp, 1))
-    )
-    firsts, seconds = gather([w_in, w_out], held, n_dp, [bits, bits[::-1]])
+    firsts, seconds = gather([w_in, w_out], [w_in[0], w_out[0]], n_dp, [bits, bits[::-1]])
 
     rank = lax.axis_index("mp")
-    keep = keep_factor(seeds, rank * BS)
+    keep = keep_factor(drop_seeds, rank * BS)
     steps = [([0, bits[0]], [0, bits[-1]])]
     late = [n_dp - 1]
     steps.append([[mask for mask in range(n_dp - 1) if mask not in done] for done in steps[0]])

time: 26.8 us -> 26.7 us (level)
    ppermute x12 -> x11, waiting for transfers between devices: 4.06 us -> 4.03 us  [flip(): lax.ppermute(value, axis, [(i, i ^ mask) for i in range(size)])]
    ppermute x12 -> x11, starting transfers between devices: 16.3 us -> 16.3 us  [flip(): lax.ppermute(value, axis, [(i, i ^ mask) for i in range(size)])]
    unnamed x6 -> x8, local copies, waits for them, and re-layouts: 0.66 us -> 0.66 us
  transfers between devices with their start and end apart: 12 -> 11, of which waited for: 6 -> 6; matrix products, arithmetic and copies ran while one was open for 4% -> 4% of each run, Pallas kernels for 7% -> 7%
where the time goes in v4:
time: 26.7 us; the launch traced here: 26.6 us
  starting transfers between devices  16.3 us (61%)
  waiting for transfers between devices  4.03 us (15%)
  Pallas kernels  3.07 us (11%)
  between operations  1.38 us (5%)
  other arithmetic  1.07 us (4%)
  local copies, waits for them, and re-layouts  0.69 us (3%)
    ppermute x11, starting transfers between devices, flip(): lax.ppermute(value, axis, [(i, i ^ mask) for i in range(size)])  16.3 us
    ppermute x11, waiting for transfers between devices, flip(): lax.ppermute(value, axis, [(i, i ^ mask) for i in range(size)])  4.03 us
    pallas_call x1, Pallas kernels, body(): call(functools.partial(grad_kernel, slots), n_dp, [grad_shape, grad_shape...  1.04 us
    concatenate x1, other arithmetic, body(): jnp.concatenate([inputs, cotangent])  0.88 us
    pallas_call x1, Pallas kernels, body(): call(functools.partial(select_kernel, slots, *steps[0]), 1 + len(weights[...  0.75 us
    unnamed x8, local copies, waits for them, and re-layouts  0.66 us
    pallas_call x1, Pallas kernels, body(): call(functools.partial(last_kernel, blocks), 3, [shape((done, width), BF1...  0.62 us
  transfers between devices with their start and end apart: 11, of which 6 were waited for; matrix products, arithmetic and copies ran while one was open for 4% of the time, Pallas kernels for 7%

profile of v4, /device:TPU:0, one launch (start us, length us, event | category | flops | bytes accessed | tf_op | source)
XLA Modules:
  0.0 26.6 jit_solution(15257188371863576147)
XLA Ops:
  0.6 3.0 %collective-permute-start = (bf16[1,4,128,128]{3,2,1,0:T(8,128)(2,1)}, bf16[1,4,128,128]{3,2,1,0:T(8,128)(2,1)S(1)}, u32[]{:S(2)}, u32[]{:S(2)}) collective-permute-start(bf16[1,4,128,128]{3,2,1,0:T(8,128)(2,1)} %refs_0_.3), channel_id=1, source_target_pairs={{0,8},{8,0},{16,24},{24,16},{1,9},{9,1},{17,25},{25,17},{2,10},{10... | collective-permute-start | bytes 393224 | tf_op jit(solution)/shard_map/ppermute | solution.py:182
  3.6 1.5 %collective-permute-start.1 = (bf16[1,4,128,128]{3,2,1,0:T(8,128)(2,1)}, bf16[1,4,128,128]{3,2,1,0:T(8,128)(2,1)S(1)}, u32[]{:S(2)}, u32[]{:S(2)}) collective-permute-start(bf16[1,4,128,128]{3,2,1,0:T(8,128)(2,1)} %refs_4_.1), channel_id=1, source_target_pairs={{0,16},{8,24},{16,0},{24,8},{1,17},{9,25},{17,1},{25,9},{2,18},{10... | collective-permute-start | bytes 393224 | tf_op jit(solution)/shard_map/ppermute | solution.py:182
  5.2 0.5 %collective-permute-start.2 = (bf16[4,128,128]{2,1,0:T(8,128)(2,1)}, bf16[4,128,128]{2,1,0:T(8,128)(2,1)S(1)}, u32[]{:S(2)}, u32[]{:S(2)}) collective-permute-start(bf16[4,128,128]{2,1,0:T(8,128)(2,1)} %bitcast.10), channel_id=1, source_target_pairs={{0,8},{8,0},{16,24},{24,16},{1,9},{9,1},{17,25},{25,17},{2,10},{10... | collective-permute-start | bytes 393224 | tf_op jit(solution)/shard_map/ppermute | solution.py:182
  5.7 0.1 collective-permute-start.3
  5.8 0.9 %pad_maximum_fusion.tokens = bf16[16,2560]{1,0:T(8,128)(2,1)S(1)} fusion(bf16[8,2560]{1,0:T(8,128)(2,1)} %param.8, bf16[8,2560]{1,0:T(8,128)(2,1)} %param.7), kind=kLoop, calls=%fused_computation | loop fusion | flops 163840 | bytes 163840 | tf_op jit(solution)/shard_map/concatenate | solution.py:244
  6.6 1.2 %collective-permute-done.refs_1_ = bf16[1,4,128,128]{3,2,1,0:T(8,128)(2,1)S(1)} collective-permute-done((bf16[1,4,128,128]{3,2,1,0:T(8,128)(2,1)}, bf16[1,4,128,128]{3,2,1,0:T(8,128)(2,1)S(1)}, u32[]{:S(2)}, u32[]{:S(2)}) %collective-permute-start) | collective-permute-done | bytes 131104 | tf_op jit(solution)/shard_map/ppermute | solution.py:182
  7.9 2.4 %collective-permute-start.4 = (bf16[1,4,128,128]{3,2,1,0:T(8,128)(2,1)S(1)}, bf16[1,4,128,128]{3,2,1,0:T(8,128)(2,1)S(1)}, u32[]{:S(2)}, u32[]{:S(2)}) collective-permute-start(bf16[1,4,128,128]{3,2,1,0:T(8,128)(2,1)S(1)} %collective-permute-done.refs_1_), channel_id=1, source_target_pairs={{0,16},{8,24},{16,0},{24,8},{1,17},{9,25},{17,1},{25,9},{2,18},{10... | collective-permute-start | bytes 393224 | tf_op jit(solution)/shard_map/ppermute | solution.py:182
  10.3 0.0 collective-permute-done.1.refs_3_.refs_6_
  10.3 1.5 %collective-permute-start.5 = (bf16[1,4,128,128]{3,2,1,0:T(8,128)(2,1)S(1)}, bf16[1,4,128,128]{3,2,1,0:T(8,128)(2,1)S(1)}, u32[]{:S(2)}, u32[]{:S(2)}) collective-permute-start(bf16[1,4,128,128]{3,2,1,0:T(8,128)(2,1)S(1)} %collective-permute-done.1.refs_3_.refs_6_), channel_id=1, source_target_pairs={{0,8},{8,0},{16,24},{24,16},{1,9},{9,1},{17,25},{25,17},{2,10},{10... | collective-permute-start | bytes 393224 | tf_op jit(solution)/shard_map/ppermute | solution.py:182
  11.8 0.1 fusion.4.keep
  12.5 0.0 copy-start.3
  12.5 0.6 %copy-done.3 = s32[1,16]{1,0:T(1,128)S(1)} copy-done((s32[1,16]{1,0:T(1,128)S(1)}, s32[1,16]{1,0:T(1,128)}, u32[]{:S(2)}) %copy-start.3) | copy-done | bytes 88
  13.2 0.1 pad_add_fusion.listed
  13.2 0.7 %shard_map.102 = (bf16[16,2048]{1,0:T(8,128)(2,1)S(1)}, s32[8,128]{1,0:T(8,128)S(1)}, f32[16,128]{1,0:T(8,128)S(1)}) custom-call(s32[17]{0:T(128)S(1)} %pad_add_fusion.listed, bf16[16,2560]{1,0:T(8,128)(2,1)S(1)} %pad_maximum_fusion.tokens, bf16[1,4,128,128]{3,2,1,0:T(8,128)(2,1)S(1)} %copy-done, bf16[1,4,128,128]{3,2,1,0:T(8,128)(2,1)S(1)} %collective-permute-done.refs_1_, ...), custom_call_target="tpu_custom_call" | custom-call | tf_op jit(solution)/shard_map/pallas_call | solution.py:233
  14.0 0.0 collective-permute-done.2
  14.0 0.0 collective-permute-done.3
  14.0 0.2 shard_map.103.sums
  14.2 0.2 collective-permute-done.4.refs_3_
  14.4 0.8 %collective-permute-done.5.refs_7_ = bf16[1,4,128,128]{3,2,1,0:T(8,128)(2,1)S(1)} collective-permute-done((bf16[1,4,128,128]{3,2,1,0:T(8,128)(2,1)S(1)}, bf16[1,4,128,128]{3,2,1,0:T(8,128)(2,1)S(1)}, u32[]{:S(2)}, u32[]{:S(2)}) %collective-permute-start.5) | collective-permute-done | bytes 131104 | tf_op jit(solution)/shard_map/ppermute | solution.py:182
  15.2 0.5 %shard_map.104 = (bf16[4,40,128]{2,1,0:T(8,128)(2,1)S(1)}, f32[4,40,128]{2,1,0:T(8,128)S(1)}, bf16[16,640]{1,0:T(8,128)(2,1)S(1)}, bf16[16,640]{1,0:T(8,128)(2,1...) custom-call(bf16[16,2048]{1,0:T(8,128)(2,1)S(1)} %get-tuple-element.18.picks, ...), custom_call_target="tpu_custom_call" | custom-call | flops 10485760 | bytes 1048576 | tf_op jit(solution)/shard_map/pallas_call | solution.py:255
  15.7 0.1 collective-permute-start.6
  15.8 1.6 %collective-permute-start.9 = (bf16[16,1280]{1,0:T(8,128)(2,1)S(1)}, bf16[16,1280]{1,0:T(8,128)(2,1)S(1)}, u32[]{:S(2)}, u32[]{:S(2)}) collective-permute-start(bf16[16,1280]{1,0:T(8,128)(2,1)S(1)} %pad_maximum_fusion.1), channel_id=1, source_target_pairs={{0,8},{8,0},{16,24},{24,16},{1,9},{9,1},{17,25},{25,17},{2,10},{10... | collective-permute-start | bytes 122888 | tf_op jit(solution)/shard_map/ppermute | solution.py:182
  17.4 0.0 collective-permute-done.6
  17.4 2.7 %collective-permute-start.7 = (bf16[2,40,128]{2,1,0:T(8,128)(2,1)S(1)}, bf16[2,40,128]{2,1,0:T(8,128)(2,1)S(1)}, u32[]{:S(2)}, u32[]{:S(2)}) collective-permute-start(bf16[2,40,128]{2,1,0:T(8,128)(2,1)S(1)} %dynamic-slice_convert_fusion), channel_id=1, source_target_pairs={{0,4},{1,5},{2,6},{3,7},{4,0},{5,1},{6,2},{7,3},{8,12},{9,13},{10,... | collective-permute-start | bytes 61448 | tf_op jit(solution)/shard_map/ppermute | solution.py:182
  20.1 0.0 collective-permute-done.9
  20.1 1.4 %collective-permute-start.10 = (bf16[16,1280]{1,0:T(8,128)(2,1)S(1)}, bf16[16,1280]{1,0:T(8,128)(2,1)S(1)}, u32[]{:S(2)}, u32[]{:S(2)}) collective-permute-start(bf16[16,1280]{1,0:T(8,128)(2,1)S(1)} %pad_maximum_fusion.2), channel_id=1, source_target_pairs={{0,16},{8,24},{16,0},{24,8},{1,17},{9,25},{17,1},{25,9},{2,18},{10... | collective-permute-start | bytes 122888 | tf_op jit(solution)/shard_map/ppermute | solution.py:182
  21.5 0.7 %collective-permute-done.7 = bf16[2,40,128]{2,1,0:T(8,128)(2,1)S(1)} collective-permute-done((bf16[2,40,128]{2,1,0:T(8,128)(2,1)S(1)}, bf16[2,40,128]{2,1,0:T(8,128)(2,1)S(1)}, u32[]{:S(2)}, u32[]{:S(2)}) %collective-permute-start.7) | collective-permute-done | bytes 20512 | tf_op jit(solution)/shard_map/ppermute | solution.py:182
  22.2 1.6 %collective-permute-start.8 = (bf16[1,40,128]{2,1,0:T(8,128)(2,1)S(1)}, bf16[1,40,128]{2,1,0:T(8,128)(2,1)S(1)}, u32[]{:S(2)}, u32[]{:S(2)}) collective-permute-start(bf16[1,40,128]{2,1,0:T(8,128)(2,1)S(1)} %dynamic-slice_convert_fusion.1), channel_id=1, source_target_pairs={{0,2},{1,3},{2,0},{3,1},{4,6},{5,7},{6,4},{7,5},{8,10},{9,11},{10,... | collective-permute-start | bytes 30728 | tf_op jit(solution)/shard_map/ppermute | solution.py:182
  23.8 0.3 %collective-permute-done.10 = bf16[16,1280]{1,0:T(8,128)(2,1)S(1)} collective-permute-done((bf16[16,1280]{1,0:T(8,128)(2,1)S(1)}, bf16[16,1280]{1,0:T(8,128)(2,1)S(1)}, u32[]{:S(2)}, u32[]{:S(2)}) %collective-permute-start.10) | collective-permute-done | bytes 40992 | tf_op jit(solution)/shard_map/ppermute | solution.py:182
  24.2 1.0 %shard_map.105 = (f32[1,4,128,128]{3,2,1,0:T(8,128)}, f32[1,4,128,128]{3,2,1,0:T(8,128)}, f32[8,128]{1,0:T(8,128)S(1)}) custom-call(bf16[16,640]{1,0:T(8,128)(2,1)S(1)} %get-tuple-element.23.refs_0_, bf16[16,640]{1,0:T(8,128)(2,1)S(1)} %get-tuple-element.35.refs_1_, bf16[16,640]{1,0:T(8,128)(2,1)S(1)} %get-tuple-element.33.refs_2_, ...), custom_call_target="tpu_custom_call" | custom-call | flops 8388608 | bytes 524288 | tf_op jit(solution)/shard_map/pallas_call | solution.py:278
  25.2 0.7 %collective-permute-done.8.got = bf16[1,40,128]{2,1,0:T(8,128)(2,1)S(1)} collective-permute-done((bf16[1,40,128]{2,1,0:T(8,128)(2,1)S(1)}, bf16[1,40,128]{2,1,0:T(8,128)(2,1)S(1)}, u32[]{:S(2)}, u32[]{:S(2)}) %collective-permute-start.8) | collective-permute-done | bytes 10272 | tf_op jit(solution)/shard_map/ppermute | solution.py:182
  25.9 0.6 %shard_map.106 = (bf16[1,2560]{1,0:T(2,128)(2,1)}, bf16[1,2560]{1,0:T(2,128)(2,1)}) custom-call(f32[1,40,128]{2,1,0:T(8,128)S(1)} %constant_dynamic-slice_fusion.kept, bf16[1,40,128]{2,1,0:T(8,128)(2,1)S(1)} %collective-permute-done.8.got, f32[8,128]{1,0:T(8,128)S(1)} %get-tuple-element.27.order), custom_call_target="tpu_custom_call" | custom-call | flops 5120 | bytes 40960 | tf_op jit(solution)/shard_map/pallas_call | solution.py:286
  (16 shorter events, 0.1 us)
Async XLA Ops:
  0.6 7.2 %collective-permute-start = (bf16[1,4,128,128]{3,2,1,0:T(8,128)(2,1)}, bf16[1,4,128,128]{3,2,1,0:T(8,128)(2,1)S(1)}, u32[]{:S(2)}, u32[]{:S(2)}) collective-permute-start(bf16[1,4,128,128]{3,2,1,0:T(8,128)(2,1)} %refs_0_.3), channel_id=1, source_target_pairs={{0,8},{8,0},{16,24},{24,16},{1,9},{9,1},{17,25},{25,17},{2,10},{10... | collective-permute-start | bytes 393224 | tf_op jit(solution)/shard_map/ppermute | solution.py:182
  3.6 6.6 %collective-permute-start.1 = (bf16[1,4,128,128]{3,2,1,0:T(8,128)(2,1)}, bf16[1,4,128,128]{3,2,1,0:T(8,128)(2,1)S(1)}, u32[]{:S(2)}, u32[]{:S(2)}) collective-permute-start(bf16[1,4,128,128]{3,2,1,0:T(8,128)(2,1)} %refs_4_.1), channel_id=1, source_target_pairs={{0,16},{8,24},{16,0},{24,8},{1,17},{9,25},{17,1},{25,9},{2,18},{10... | collective-permute-start | bytes 393224 | tf_op jit(solution)/shard_map/ppermute | solution.py:182
  5.2 8.8 %collective-permute-start.2 = (bf16[4,128,128]{2,1,0:T(8,128)(2,1)}, bf16[4,128,128]{2,1,0:T(8,128)(2,1)S(1)}, u32[]{:S(2)}, u32[]{:S(2)}) collective-permute-start(bf16[4,128,128]{2,1,0:T(8,128)(2,1)} %bitcast.10), channel_id=1, source_target_pairs={{0,8},{8,0},{16,24},{24,16},{1,9},{9,1},{17,25},{25,17},{2,10},{10... | collective-permute-start | bytes 393224 | tf_op jit(solution)/shard_map/ppermute | solution.py:182
  5.7 6.1 %copy-start.2 = (s32[8]{0:T(128)S(1)}, s32[8]{0:T(128)}, u32[]{:S(2)}) copy-start(s32[8]{0:T(128)} %param.13) | copy-start | bytes 100
  5.7 7.5 %copy-start = (bf16[1,4,128,128]{3,2,1,0:T(8,128)(2,1)S(1)}, bf16[1,4,128,128]{3,2,1,0:T(8,128)(2,1)}, u32[]{:S(2)}) copy-start(bf16[1,4,128,128]{3,2,1,0:T(8,128)(2,1)} %refs_0_.3) | copy-start | bytes 393220
  5.7 7.5 %copy-start.1 = (bf16[1,4,128,128]{3,2,1,0:T(8,128)(2,1)S(1)}, bf16[1,4,128,128]{3,2,1,0:T(8,128)(2,1)}, u32[]{:S(2)}) copy-start(bf16[1,4,128,128]{3,2,1,0:T(8,128)(2,1)} %refs_4_.1) | copy-start | bytes 393220
  5.7 8.3 %collective-permute-start.3 = (bf16[4,128,128]{2,1,0:T(8,128)(2,1)}, bf16[4,128,128]{2,1,0:T(8,128)(2,1)S(1)}, u32[]{:S(2)}, u32[]{:S(2)}) collective-permute-start(bf16[4,128,128]{2,1,0:T(8,128)(2,1)} %bitcast.9), channel_id=1, source_target_pairs={{0,16},{8,24},{16,0},{24,8},{1,17},{9,25},{17,1},{25,9},{2,18},{10... | collective-permute-start | bytes 393224 | tf_op jit(solution)/shard_map/ppermute | solution.py:182
  7.9 6.6 %collective-permute-start.4 = (bf16[1,4,128,128]{3,2,1,0:T(8,128)(2,1)S(1)}, bf16[1,4,128,128]{3,2,1,0:T(8,128)(2,1)S(1)}, u32[]{:S(2)}, u32[]{:S(2)}) collective-permute-start(bf16[1,4,128,128]{3,2,1,0:T(8,128)(2,1)S(1)} %collective-permute-done.refs_1_), channel_id=1, source_target_pairs={{0,16},{8,24},{16,0},{24,8},{1,17},{9,25},{17,1},{25,9},{2,18},{10... | collective-permute-start | bytes 393224 | tf_op jit(solution)/shard_map/ppermute | solution.py:182
  10.3 5.0 %collective-permute-start.5 = (bf16[1,4,128,128]{3,2,1,0:T(8,128)(2,1)S(1)}, bf16[1,4,128,128]{3,2,1,0:T(8,128)(2,1)S(1)}, u32[]{:S(2)}, u32[]{:S(2)}) collective-permute-start(bf16[1,4,128,128]{3,2,1,0:T(8,128)(2,1)S(1)} %collective-permute-done.1.refs_3_.refs_6_), channel_id=1, source_target_pairs={{0,8},{8,0},{16,24},{24,16},{1,9},{9,1},{17,25},{25,17},{2,10},{10... | collective-permute-start | bytes 393224 | tf_op jit(solution)/shard_map/ppermute | solution.py:182
  12.5 0.7 %copy-start.3 = (s32[1,16]{1,0:T(1,128)S(1)}, s32[1,16]{1,0:T(1,128)}, u32[]{:S(2)}) copy-start(s32[1,16]{1,0:T(1,128)} %param.11) | copy-start | bytes 196
  15.7 1.7 %collective-permute-start.6 = (bf16[4,40,128]{2,1,0:T(8,128)(2,1)S(1)}, bf16[4,40,128]{2,1,0:T(8,128)(2,1)S(1)}, u32[]{:S(2)}, u32[]{:S(2)}) collective-permute-start(bf16[4,40,128]{2,1,0:T(8,128)(2,1)S(1)} %get-tuple-element.22), channel_id=1, source_target_pairs={{0,1},{1,0},{2,3},{3,2},{4,5},{5,4},{6,7},{7,6},{8,9},{9,8},{10,11... | collective-permute-start | bytes 122888 | tf_op jit(solution)/shard_map/ppermute | solution.py:182
  15.8 4.3 %collective-permute-start.9 = (bf16[16,1280]{1,0:T(8,128)(2,1)S(1)}, bf16[16,1280]{1,0:T(8,128)(2,1)S(1)}, u32[]{:S(2)}, u32[]{:S(2)}) collective-permute-start(bf16[16,1280]{1,0:T(8,128)(2,1)S(1)} %pad_maximum_fusion.1), channel_id=1, source_target_pairs={{0,8},{8,0},{16,24},{24,16},{1,9},{9,1},{17,25},{25,17},{2,10},{10... | collective-permute-start | bytes 122888 | tf_op jit(solution)/shard_map/ppermute | solution.py:182
  17.4 4.8 %collective-permute-start.7 = (bf16[2,40,128]{2,1,0:T(8,128)(2,1)S(1)}, bf16[2,40,128]{2,1,0:T(8,128)(2,1)S(1)}, u32[]{:S(2)}, u32[]{:S(2)}) collective-permute-start(bf16[2,40,128]{2,1,0:T(8,128)(2,1)S(1)} %dynamic-slice_convert_fusion), channel_id=1, source_target_pairs={{0,4},{1,5},{2,6},{3,7},{4,0},{5,1},{6,2},{7,3},{8,12},{9,13},{10,... | collective-permute-start | bytes 61448 | tf_op jit(solution)/shard_map/ppermute | solution.py:182
  20.1 4.1 %collective-permute-start.10 = (bf16[16,1280]{1,0:T(8,128)(2,1)S(1)}, bf16[16,1280]{1,0:T(8,128)(2,1)S(1)}, u32[]{:S(2)}, u32[]{:S(2)}) collective-permute-start(bf16[16,1280]{1,0:T(8,128)(2,1)S(1)} %pad_maximum_fusion.2), channel_id=1, source_target_pairs={{0,16},{8,24},{16,0},{24,8},{1,17},{9,25},{17,1},{25,9},{2,18},{10... | collective-permute-start | bytes 122888 | tf_op jit(solution)/shard_map/ppermute | solution.py:182
  22.2 3.7 %collective-permute-start.8 = (bf16[1,40,128]{2,1,0:T(8,128)(2,1)S(1)}, bf16[1,40,128]{2,1,0:T(8,128)(2,1)S(1)}, u32[]{:S(2)}, u32[]{:S(2)}) collective-permute-start(bf16[1,40,128]{2,1,0:T(8,128)(2,1)S(1)} %dynamic-slice_convert_fusion.1), channel_id=1, source_target_pairs={{0,2},{1,3},{2,0},{3,1},{4,6},{5,7},{6,4},{7,5},{8,10},{9,11},{10,... | collective-permute-start | bytes 30728 | tf_op jit(solution)/shard_map/ppermute | solution.py:182

commit v5 on v4

--- a/solution.py
+++ b/solution.py
@@ -107,6 +107,10 @@
     out[local:] = grad
 
 
+def bit_parity(number, size):
+    return functools.reduce(lambda found, i: found ^ number >> i & 1, range(1, size.bit_length()), number & 1)
+
+
 def hidden_kernel(slots, blocks, masks_in, masks_out, late, picks, table, keep, sums, *refs):
     count = len(masks_in)
     firsts = dict(zip(masks_in, refs[:count]))
@@ -115,7 +119,6 @@
     acc = refs[-1]
     local = keep.shape[0]
     half = local // 2
-    odd = lax.axis_index("mp") % 2
     acc[...] = jnp.zeros_like(acc)
     entries = table[...]
     pre, grad = add_slots(
@@ -134,9 +137,11 @@
             cut = slice(j * BS, (j + 1) * BS)
             acc[:, :, pl.ds(index, 1), :] = (out_row[:, cut] * used).reshape(half, 2, 1, BS)
             acc[:, :, pl.ds(blocks + index, 1), :] = (in_row[:, cut] * used).reshape(half, 2, 1, BS)
-    even_rows, odd_rows = acc[:, 0], acc[:, 1]
-    away[...] = jnp.where(odd == 1, even_rows, odd_rows).astype(BF16)
-    home[...] = jnp.where(odd == 1, odd_rows, even_rows)
+    odd = bit_parity(lax.axis_index("mp"), 2 * half)
+    for i in range(half):
+        even_row, odd_row = acc[i, bit_parity(i, half)], acc[i, 1 - bit_parity(i, half)]
+        away[i] = jnp.where(odd == 1, even_row, odd_row).astype(BF16)
+        home[i] = jnp.where(odd == 1, odd_row, even_row)
     hidden = jnp.concatenate([dropped_full, grad_full], axis=0).astype(BF16)
     for mask, message in enumerate(rows):
         message[:, :BS] = hidden
@@ -270,7 +275,7 @@
         cut = total.shape[0] // 2
         away = lax.dynamic_slice_in_dim(total, (1 - mine_bit) * cut, cut, 0)
         home = lax.dynamic_slice_in_dim(total, mine_bit * cut, cut, 0)
-        got = flip(away.astype(BF16), "mp", n_mp, bit)
+        got = flip(away.astype(BF16), "mp", n_mp, bit | 1)
         total = home + got.astype(F32)
         bit //= 2
 

time: 26.7 us -> 25.8 us (0.966)
  waiting for transfers between devices: 4.03 us -> 3.4 us
    ppermute x11, waiting for transfers between devices: 4.03 us -> 3.4 us  [flip(): lax.ppermute(value, axis, [(i, i ^ mask) for i in range(size)])]
    ppermute x11, starting transfers between devices: 16.3 us -> 16.1 us  [flip(): lax.ppermute(value, axis, [(i, i ^ mask) for i in range(size)])]
  transfers between devices with their start and end apart: 11 -> 11, of which waited for: 6 -> 6; matrix products, arithmetic and copies ran while one was open for 4% -> 4% of each run, Pallas kernels for 7% -> 8%
where the time goes in v5:
time: 25.8 us; the launch traced here: 25.7 us
  starting transfers between devices  16.1 us (62%)
  waiting for transfers between devices  3.4 us (13%)
  Pallas kernels  3.07 us (12%)
  between operations  1.38 us (5%)
  other arithmetic  1.07 us (4%)
  local copies, waits for them, and re-layouts  0.69 us (3%)
    ppermute x11, starting transfers between devices, flip(): lax.ppermute(value, axis, [(i, i ^ mask) for i in range(size)])  16.1 us
    ppermute x11, waiting for transfers between devices, flip(): lax.ppermute(value, axis, [(i, i ^ mask) for i in range(size)])  3.4 us
    pallas_call x1, Pallas kernels, body(): call(functools.partial(grad_kernel, slots), n_dp, [grad_shape, grad_shape...  1.04 us
    concatenate x1, other arithmetic, body(): jnp.concatenate([inputs, cotangent])  0.88 us
    pallas_call x1, Pallas kernels, body(): call(functools.partial(select_kernel, slots, *steps[0]), 1 + len(weights[...  0.75 us
    unnamed x8, local copies, waits for them, and re-layouts  0.66 us
    pallas_call x1, Pallas kernels, body(): call(functools.partial(last_kernel, blocks), 3, [shape((done, width), BF1...  0.62 us
  transfers between devices with their start and end apart: 11, of which 6 were waited for; matrix products, arithmetic and copies ran while one was open for 4% of the time, Pallas kernels for 8%

profile of v5, /device:TPU:0, one launch (start us, length us, event | category | flops | bytes accessed | tf_op | source)
XLA Modules:
  0.0 25.7 jit_solution(12992062271286308065)
XLA Ops:
  0.6 3.0 %collective-permute-start = (bf16[1,4,128,128]{3,2,1,0:T(8,128)(2,1)}, bf16[1,4,128,128]{3,2,1,0:T(8,128)(2,1)S(1)}, u32[]{:S(2)}, u32[]{:S(2)}) collective-permute-start(bf16[1,4,128,128]{3,2,1,0:T(8,128)(2,1)} %refs_0_.3), channel_id=1, source_target_pairs={{0,8},{8,0},{16,24},{24,16},{1,9},{9,1},{17,25},{25,17},{2,10},{10... | collective-permute-start | bytes 393224 | tf_op jit(solution)/shard_map/ppermute | solution.py:187
  3.6 1.5 %collective-permute-start.1 = (bf16[1,4,128,128]{3,2,1,0:T(8,128)(2,1)}, bf16[1,4,128,128]{3,2,1,0:T(8,128)(2,1)S(1)}, u32[]{:S(2)}, u32[]{:S(2)}) collective-permute-start(bf16[1,4,128,128]{3,2,1,0:T(8,128)(2,1)} %refs_4_.1), channel_id=1, source_target_pairs={{0,16},{8,24},{16,0},{24,8},{1,17},{9,25},{17,1},{25,9},{2,18},{10... | collective-permute-start | bytes 393224 | tf_op jit(solution)/shard_map/ppermute | solution.py:187
  5.2 0.5 %collective-permute-start.2 = (bf16[4,128,128]{2,1,0:T(8,128)(2,1)}, bf16[4,128,128]{2,1,0:T(8,128)(2,1)S(1)}, u32[]{:S(2)}, u32[]{:S(2)}) collective-permute-start(bf16[4,128,128]{2,1,0:T(8,128)(2,1)} %bitcast.10), channel_id=1, source_target_pairs={{0,8},{8,0},{16,24},{24,16},{1,9},{9,1},{17,25},{25,17},{2,10},{10... | collective-permute-start | bytes 393224 | tf_op jit(solution)/shard_map/ppermute | solution.py:187
  5.7 0.1 collective-permute-start.3
  5.8 0.9 %pad_maximum_fusion.tokens = bf16[16,2560]{1,0:T(8,128)(2,1)S(1)} fusion(bf16[8,2560]{1,0:T(8,128)(2,1)} %param.8, bf16[8,2560]{1,0:T(8,128)(2,1)} %param.7), kind=kLoop, calls=%fused_computation | loop fusion | flops 163840 | bytes 163840 | tf_op jit(solution)/shard_map/concatenate | solution.py:249
  6.6 1.2 %collective-permute-done.refs_1_ = bf16[1,4,128,128]{3,2,1,0:T(8,128)(2,1)S(1)} collective-permute-done((bf16[1,4,128,128]{3,2,1,0:T(8,128)(2,1)}, bf16[1,4,128,128]{3,2,1,0:T(8,128)(2,1)S(1)}, u32[]{:S(2)}, u32[]{:S(2)}) %collective-permute-start) | collective-permute-done | bytes 131104 | tf_op jit(solution)/shard_map/ppermute | solution.py:187
  7.9 2.4 %collective-permute-start.4 = (bf16[1,4,128,128]{3,2,1,0:T(8,128)(2,1)S(1)}, bf16[1,4,128,128]{3,2,1,0:T(8,128)(2,1)S(1)}, u32[]{:S(2)}, u32[]{:S(2)}) collective-permute-start(bf16[1,4,128,128]{3,2,1,0:T(8,128)(2,1)S(1)} %collective-permute-done.refs_1_), channel_id=1, source_target_pairs={{0,16},{8,24},{16,0},{24,8},{1,17},{9,25},{17,1},{25,9},{2,18},{10... | collective-permute-start | bytes 393224 | tf_op jit(solution)/shard_map/ppermute | solution.py:187
  10.3 0.0 collective-permute-done.1.refs_3_.refs_6_
  10.3 1.5 %collective-permute-start.5 = (bf16[1,4,128,128]{3,2,1,0:T(8,128)(2,1)S(1)}, bf16[1,4,128,128]{3,2,1,0:T(8,128)(2,1)S(1)}, u32[]{:S(2)}, u32[]{:S(2)}) collective-permute-start(bf16[1,4,128,128]{3,2,1,0:T(8,128)(2,1)S(1)} %collective-permute-done.1.refs_3_.refs_6_), channel_id=1, source_target_pairs={{0,8},{8,0},{16,24},{24,16},{1,9},{9,1},{17,25},{25,17},{2,10},{10... | collective-permute-start | bytes 393224 | tf_op jit(solution)/shard_map/ppermute | solution.py:187
  11.8 0.1 fusion.4.keep
  12.5 0.0 copy-start.3
  12.5 0.6 %copy-done.3 = s32[1,16]{1,0:T(1,128)S(1)} copy-done((s32[1,16]{1,0:T(1,128)S(1)}, s32[1,16]{1,0:T(1,128)}, u32[]{:S(2)}) %copy-start.3) | copy-done | bytes 88
  13.2 0.1 pad_add_fusion.listed
  13.2 0.7 %shard_map.102 = (bf16[16,2048]{1,0:T(8,128)(2,1)S(1)}, s32[8,128]{1,0:T(8,128)S(1)}, f32[16,128]{1,0:T(8,128)S(1)}) custom-call(s32[17]{0:T(128)S(1)} %pad_add_fusion.listed, bf16[16,2560]{1,0:T(8,128)(2,1)S(1)} %pad_maximum_fusion.tokens, bf16[1,4,128,128]{3,2,1,0:T(8,128)(2,1)S(1)} %copy-done, bf16[1,4,128,128]{3,2,1,0:T(8,128)(2,1)S(1)} %collective-permute-done.refs_1_, ...), custom_call_target="tpu_custom_call" | custom-call | tf_op jit(solution)/shard_map/pallas_call | solution.py:238
  14.0 0.0 collective-permute-done.2
  14.0 0.0 collective-permute-done.3
  14.0 0.2 shard_map.103.sums
  14.2 0.2 collective-permute-done.4.refs_3_
  14.4 0.8 %collective-permute-done.5.refs_7_ = bf16[1,4,128,128]{3,2,1,0:T(8,128)(2,1)S(1)} collective-permute-done((bf16[1,4,128,128]{3,2,1,0:T(8,128)(2,1)S(1)}, bf16[1,4,128,128]{3,2,1,0:T(8,128)(2,1)S(1)}, u32[]{:S(2)}, u32[]{:S(2)}) %collective-permute-start.5) | collective-permute-done | bytes 131104 | tf_op jit(solution)/shard_map/ppermute | solution.py:187
  15.2 0.5 %shard_map.104 = (bf16[4,40,128]{2,1,0:T(8,128)(2,1)S(1)}, f32[4,40,128]{2,1,0:T(8,128)S(1)}, bf16[16,640]{1,0:T(8,128)(2,1)S(1)}, bf16[16,640]{1,0:T(8,128)(2,1...) custom-call(bf16[16,2048]{1,0:T(8,128)(2,1)S(1)} %get-tuple-element.18.picks, ...), custom_call_target="tpu_custom_call" | custom-call | flops 10485760 | bytes 1048576 | tf_op jit(solution)/shard_map/pallas_call | solution.py:260
  15.7 0.1 collective-permute-start.6
  15.8 1.6 %collective-permute-start.9 = (bf16[16,1280]{1,0:T(8,128)(2,1)S(1)}, bf16[16,1280]{1,0:T(8,128)(2,1)S(1)}, u32[]{:S(2)}, u32[]{:S(2)}) collective-permute-start(bf16[16,1280]{1,0:T(8,128)(2,1)S(1)} %pad_maximum_fusion.1), channel_id=1, source_target_pairs={{0,8},{8,0},{16,24},{24,16},{1,9},{9,1},{17,25},{25,17},{2,10},{10... | collective-permute-start | bytes 122888 | tf_op jit(solution)/shard_map/ppermute | solution.py:187
  17.4 0.0 collective-permute-done.6
  17.4 2.4 %collective-permute-start.7 = (bf16[2,40,128]{2,1,0:T(8,128)(2,1)S(1)}, bf16[2,40,128]{2,1,0:T(8,128)(2,1)S(1)}, u32[]{:S(2)}, u32[]{:S(2)}) collective-permute-start(bf16[2,40,128]{2,1,0:T(8,128)(2,1)S(1)} %dynamic-slice_convert_fusion), channel_id=1, source_target_pairs={{0,5},{1,4},{2,7},{3,6},{4,1},{5,0},{6,3},{7,2},{8,13},{9,12},{10,... | collective-permute-start | bytes 61448 | tf_op jit(solution)/shard_map/ppermute | solution.py:187
  19.8 0.1 collective-permute-done.9
  19.9 1.6 %collective-permute-start.10 = (bf16[16,1280]{1,0:T(8,128)(2,1)S(1)}, bf16[16,1280]{1,0:T(8,128)(2,1)S(1)}, u32[]{:S(2)}, u32[]{:S(2)}) collective-permute-start(bf16[16,1280]{1,0:T(8,128)(2,1)S(1)} %pad_maximum_fusion.2), channel_id=1, source_target_pairs={{0,16},{8,24},{16,0},{24,8},{1,17},{9,25},{17,1},{25,9},{2,18},{10... | collective-permute-start | bytes 122888 | tf_op jit(solution)/shard_map/ppermute | solution.py:187
  21.5 0.1 collective-permute-done.7
  21.6 1.4 %collective-permute-start.8 = (bf16[1,40,128]{2,1,0:T(8,128)(2,1)S(1)}, bf16[1,40,128]{2,1,0:T(8,128)(2,1)S(1)}, u32[]{:S(2)}, u32[]{:S(2)}) collective-permute-start(bf16[1,40,128]{2,1,0:T(8,128)(2,1)S(1)} %dynamic-slice_convert_fusion.1), channel_id=1, source_target_pairs={{0,3},{1,2},{2,1},{3,0},{4,7},{5,6},{6,5},{7,4},{8,11},{9,10},{10,... | collective-permute-start | bytes 30728 | tf_op jit(solution)/shard_map/ppermute | solution.py:187
  23.0 1.0 %collective-permute-done.10 = bf16[16,1280]{1,0:T(8,128)(2,1)S(1)} collective-permute-done((bf16[16,1280]{1,0:T(8,128)(2,1)S(1)}, bf16[16,1280]{1,0:T(8,128)(2,1)S(1)}, u32[]{:S(2)}, u32[]{:S(2)}) %collective-permute-start.10) | collective-permute-done | bytes 40992 | tf_op jit(solution)/shard_map/ppermute | solution.py:187
  24.0 1.0 %shard_map.105 = (f32[1,4,128,128]{3,2,1,0:T(8,128)}, f32[1,4,128,128]{3,2,1,0:T(8,128)}, f32[8,128]{1,0:T(8,128)S(1)}) custom-call(bf16[16,640]{1,0:T(8,128)(2,1)S(1)} %get-tuple-element.23.refs_0_, bf16[16,640]{1,0:T(8,128)(2,1)S(1)} %get-tuple-element.35.refs_1_, bf16[16,640]{1,0:T(8,128)(2,1)S(1)} %get-tuple-element.33.refs_2_, ...), custom_call_target="tpu_custom_call" | custom-call | flops 8388608 | bytes 524288 | tf_op jit(solution)/shard_map/pallas_call | solution.py:283
  25.0 0.0 collective-permute-done.8.got
  25.0 0.6 %shard_map.106 = (bf16[1,2560]{1,0:T(2,128)(2,1)}, bf16[1,2560]{1,0:T(2,128)(2,1)}) custom-call(f32[1,40,128]{2,1,0:T(8,128)S(1)} %constant_dynamic-slice_fusion.kept, bf16[1,40,128]{2,1,0:T(8,128)(2,1)S(1)} %collective-permute-done.8.got, f32[8,128]{1,0:T(8,128)S(1)} %get-tuple-element.27.order), custom_call_target="tpu_custom_call" | custom-call | flops 5120 | bytes 40960 | tf_op jit(solution)/shard_map/pallas_call | solution.py:291
  (16 shorter events, 0.1 us)
Async XLA Ops:
  0.6 7.2 %collective-permute-start = (bf16[1,4,128,128]{3,2,1,0:T(8,128)(2,1)}, bf16[1,4,128,128]{3,2,1,0:T(8,128)(2,1)S(1)}, u32[]{:S(2)}, u32[]{:S(2)}) collective-permute-start(bf16[1,4,128,128]{3,2,1,0:T(8,128)(2,1)} %refs_0_.3), channel_id=1, source_target_pairs={{0,8},{8,0},{16,24},{24,16},{1,9},{9,1},{17,25},{25,17},{2,10},{10... | collective-permute-start | bytes 393224 | tf_op jit(solution)/shard_map/ppermute | solution.py:187
  3.6 6.6 %collective-permute-start.1 = (bf16[1,4,128,128]{3,2,1,0:T(8,128)(2,1)}, bf16[1,4,128,128]{3,2,1,0:T(8,128)(2,1)S(1)}, u32[]{:S(2)}, u32[]{:S(2)}) collective-permute-start(bf16[1,4,128,128]{3,2,1,0:T(8,128)(2,1)} %refs_4_.1), channel_id=1, source_target_pairs={{0,16},{8,24},{16,0},{24,8},{1,17},{9,25},{17,1},{25,9},{2,18},{10... | collective-permute-start | bytes 393224 | tf_op jit(solution)/shard_map/ppermute | solution.py:187
  5.2 8.8 %collective-permute-start.2 = (bf16[4,128,128]{2,1,0:T(8,128)(2,1)}, bf16[4,128,128]{2,1,0:T(8,128)(2,1)S(1)}, u32[]{:S(2)}, u32[]{:S(2)}) collective-permute-start(bf16[4,128,128]{2,1,0:T(8,128)(2,1)} %bitcast.10), channel_id=1, source_target_pairs={{0,8},{8,0},{16,24},{24,16},{1,9},{9,1},{17,25},{25,17},{2,10},{10... | collective-permute-start | bytes 393224 | tf_op jit(solution)/shard_map/ppermute | solution.py:187
  5.7 6.1 %copy-start.2 = (s32[8]{0:T(128)S(1)}, s32[8]{0:T(128)}, u32[]{:S(2)}) copy-start(s32[8]{0:T(128)} %param.13) | copy-start | bytes 100
  5.7 7.5 %copy-start = (bf16[1,4,128,128]{3,2,1,0:T(8,128)(2,1)S(1)}, bf16[1,4,128,128]{3,2,1,0:T(8,128)(2,1)}, u32[]{:S(2)}) copy-start(bf16[1,4,128,128]{3,2,1,0:T(8,128)(2,1)} %refs_0_.3) | copy-start | bytes 393220
  5.7 7.5 %copy-start.1 = (bf16[1,4,128,128]{3,2,1,0:T(8,128)(2,1)S(1)}, bf16[1,4,128,128]{3,2,1,0:T(8,128)(2,1)}, u32[]{:S(2)}) copy-start(bf16[1,4,128,128]{3,2,1,0:T(8,128)(2,1)} %refs_4_.1) | copy-start | bytes 393220
  5.7 8.3 %collective-permute-start.3 = (bf16[4,128,128]{2,1,0:T(8,128)(2,1)}, bf16[4,128,128]{2,1,0:T(8,128)(2,1)S(1)}, u32[]{:S(2)}, u32[]{:S(2)}) collective-permute-start(bf16[4,128,128]{2,1,0:T(8,128)(2,1)} %bitcast.9), channel_id=1, source_target_pairs={{0,16},{8,24},{16,0},{24,8},{1,17},{9,25},{17,1},{25,9},{2,18},{10... | collective-permute-start | bytes 393224 | tf_op jit(solution)/shard_map/ppermute | solution.py:187
  7.9 6.6 %collective-permute-start.4 = (bf16[1,4,128,128]{3,2,1,0:T(8,128)(2,1)S(1)}, bf16[1,4,128,128]{3,2,1,0:T(8,128)(2,1)S(1)}, u32[]{:S(2)}, u32[]{:S(2)}) collective-permute-start(bf16[1,4,128,128]{3,2,1,0:T(8,128)(2,1)S(1)} %collective-permute-done.refs_1_), channel_id=1, source_target_pairs={{0,16},{8,24},{16,0},{24,8},{1,17},{9,25},{17,1},{25,9},{2,18},{10... | collective-permute-start | bytes 393224 | tf_op jit(solution)/shard_map/ppermute | solution.py:187
  10.3 5.0 %collective-permute-start.5 = (bf16[1,4,128,128]{3,2,1,0:T(8,128)(2,1)S(1)}, bf16[1,4,128,128]{3,2,1,0:T(8,128)(2,1)S(1)}, u32[]{:S(2)}, u32[]{:S(2)}) collective-permute-start(bf16[1,4,128,128]{3,2,1,0:T(8,128)(2,1)S(1)} %collective-permute-done.1.refs_3_.refs_6_), channel_id=1, source_target_pairs={{0,8},{8,0},{16,24},{24,16},{1,9},{9,1},{17,25},{25,17},{2,10},{10... | collective-permute-start | bytes 393224 | tf_op jit(solution)/shard_map/ppermute | solution.py:187
  12.5 0.7 %copy-start.3 = (s32[1,16]{1,0:T(1,128)S(1)}, s32[1,16]{1,0:T(1,128)}, u32[]{:S(2)}) copy-start(s32[1,16]{1,0:T(1,128)} %param.11) | copy-start | bytes 196
  15.7 1.7 %collective-permute-start.6 = (bf16[4,40,128]{2,1,0:T(8,128)(2,1)S(1)}, bf16[4,40,128]{2,1,0:T(8,128)(2,1)S(1)}, u32[]{:S(2)}, u32[]{:S(2)}) collective-permute-start(bf16[4,40,128]{2,1,0:T(8,128)(2,1)S(1)} %get-tuple-element.22), channel_id=1, source_target_pairs={{0,1},{1,0},{2,3},{3,2},{4,5},{5,4},{6,7},{7,6},{8,9},{9,8},{10,11... | collective-permute-start | bytes 122888 | tf_op jit(solution)/shard_map/ppermute | solution.py:187
  15.8 4.1 %collective-permute-start.9 = (bf16[16,1280]{1,0:T(8,128)(2,1)S(1)}, bf16[16,1280]{1,0:T(8,128)(2,1)S(1)}, u32[]{:S(2)}, u32[]{:S(2)}) collective-permute-start(bf16[16,1280]{1,0:T(8,128)(2,1)S(1)} %pad_maximum_fusion.1), channel_id=1, source_target_pairs={{0,8},{8,0},{16,24},{24,16},{1,9},{9,1},{17,25},{25,17},{2,10},{10... | collective-permute-start | bytes 122888 | tf_op jit(solution)/shard_map/ppermute | solution.py:187
  17.4 4.2 %collective-permute-start.7 = (bf16[2,40,128]{2,1,0:T(8,128)(2,1)S(1)}, bf16[2,40,128]{2,1,0:T(8,128)(2,1)S(1)}, u32[]{:S(2)}, u32[]{:S(2)}) collective-permute-start(bf16[2,40,128]{2,1,0:T(8,128)(2,1)S(1)} %dynamic-slice_convert_fusion), channel_id=1, source_target_pairs={{0,5},{1,4},{2,7},{3,6},{4,1},{5,0},{6,3},{7,2},{8,13},{9,12},{10,... | collective-permute-start | bytes 61448 | tf_op jit(solution)/shard_map/ppermute | solution.py:187
  19.9 4.1 %collective-permute-start.10 = (bf16[16,1280]{1,0:T(8,128)(2,1)S(1)}, bf16[16,1280]{1,0:T(8,128)(2,1)S(1)}, u32[]{:S(2)}, u32[]{:S(2)}) collective-permute-start(bf16[16,1280]{1,0:T(8,128)(2,1)S(1)} %pad_maximum_fusion.2), channel_id=1, source_target_pairs={{0,16},{8,24},{16,0},{24,8},{1,17},{9,25},{17,1},{25,9},{2,18},{10... | collective-permute-start | bytes 122888 | tf_op jit(solution)/shard_map/ppermute | solution.py:187
  21.6 3.4 %collective-permute-start.8 = (bf16[1,40,128]{2,1,0:T(8,128)(2,1)S(1)}, bf16[1,40,128]{2,1,0:T(8,128)(2,1)S(1)}, u32[]{:S(2)}, u32[]{:S(2)}) collective-permute-start(bf16[1,40,128]{2,1,0:T(8,128)(2,1)S(1)} %dynamic-slice_convert_fusion.1), channel_id=1, source_target_pairs={{0,3},{1,2},{2,1},{3,0},{4,7},{5,6},{6,5},{7,4},{8,11},{9,10},{10,... | collective-permute-start | bytes 30728 | tf_op jit(solution)/shard_map/ppermute | solution.py:187

commit v6 on v5

--- a/solution.py
+++ b/solution.py
@@ -83,9 +83,12 @@
     row = lax.broadcasted_iota(jnp.int32, table.shape, 0)
     lane = lax.broadcasted_iota(jnp.int32, table.shape, 1)
     entries = jnp.zeros(table.shape, jnp.int32)
+    odd = lax.axis_index("mp") % 2
     count = picks.shape[1] // BS
     for place in range(count):
-        index, used = slot(listed, count, first, place)
+        mask = place // slots
+        turned = (mirrored(mask, count // slots) - mask) * slots
+        index, used = slot(listed, count, first, place + odd * turned)
         at = pl.ds(pl.multiple_of(index * BS, BS), BS)
         picks[:, place * BS : (place + 1) * BS] = (tokens[:, at].astype(F32) * used).astype(BF16)
         entry = jnp.where(row == 0, index, used.astype(jnp.int32))
@@ -187,11 +190,25 @@
     return lax.ppermute(value, axis, [(i, i ^ mask) for i in range(size)]) if mask else value
 
 
-def gather(values, held, n_dp, orders):
+def mirrored(mask, n_dp):
+    width = n_dp.bit_length() - 1
+    return sum(1 << (width - 1 - i) for i in range(width) if mask >> i & 1)
+
+
+def cross(value, n_dp, n_mp, mask):
+    pairs = []
+    for i in range(n_dp):
+        for j in range(n_mp):
+            other = i ^ (mirrored(mask, n_dp) if j % 2 else mask)
+            pairs.append((i * n_mp + j, other * n_mp + j))
+    return lax.ppermute(value, ("dp", "mp"), pairs)
+
+
+def gather(values, held, n_dp, n_mp, orders):
     pieces = [{0: value} for value in values]
     for step, bits in enumerate(zip(*orders)):
         pieces = [
-            {**parts, **{mask | bit: flip(part, "dp", n_dp, bit) for mask, part in parts.items()}}
+            {**parts, **{mask | bit: cross(part, n_dp, n_mp, bit) for mask, part in parts.items()}}
             for parts, bit in zip(pieces, bits)
         ]
         if step == 0:
@@ -204,11 +221,11 @@
     return pieces
 
 
-def exchange(messages, n_dp, bits):
+def exchange(messages, n_dp, n_mp, bits):
     for bit in bits:
         size = messages[0].shape[1]
         leaving = jnp.concatenate([message for mask, message in enumerate(messages) if mask & bit], axis=1)
-        arrived = flip(leaving, "dp", n_dp, bit)
+        arrived = cross(leaving, n_dp, n_mp, bit)
         place = 0
         for mask in range(len(messages)):
             if mask & bit:
@@ -226,7 +243,7 @@
     piece_bytes = slots * BS * BS * 2
 
     bits = [1 << i for i in range(n_dp.bit_length() - 1)]
-    firsts, seconds = gather([w_in, w_out], [w_in[0], w_out[0]], n_dp, [bits, bits[::-1]])
+    firsts, seconds = gather([w_in, w_out], [w_in[0], w_out[0]], n_dp, n_mp, [bits, bits[::-1]])
 
     rank = lax.axis_index("mp")
     keep = keep_factor(drop_seeds, rank * BS)
@@ -268,7 +285,7 @@
     )(picks, table, keep, sums, *[firsts[m] for m in masks_in], *[seconds[m] for m in masks_out])
 
     total = home + flip(away, "mp", n_mp, 1).astype(F32)
-    messages = exchange(rows, n_dp, bits)
+    messages = exchange(rows, n_dp, n_mp, bits)
     bit = n_mp // 2
     while bit > 1:
         mine_bit = (rank // bit) % 2

time: 25.8 us -> 25.6 us (level)
  starting transfers between devices: 16.1 us -> 14 us
  waiting for transfers between devices: 3.4 us -> 5.2 us
    ppermute x11 -> x3, starting transfers between devices: 16.1 us -> 3.3 us  [flip(): lax.ppermute(value, axis, [(i, i ^ mask) for i in range(size)])]
    ppermute x0 -> x8, starting transfers between devices: none -> 10.7 us  [cross(): return lax.ppermute(value, ('dp', 'mp'), pairs)]
    ppermute x0 -> x8, waiting for transfers between devices: none -> 3.9 us  [cross(): return lax.ppermute(value, ('dp', 'mp'), pairs)]
    ppermute x11 -> x3, waiting for transfers between devices: 3.4 us -> 1.31 us  [flip(): lax.ppermute(value, axis, [(i, i ^ mask) for i in range(size)])]
  transfers between devices with their start and end apart: 11 -> 11, of which waited for: 6 -> 7; matrix products, arithmetic and copies ran while one was open for 4% -> 4% of each run, Pallas kernels for 8% -> 8%
where the time goes in v6:
time: 25.6 us; the launch traced here: 25.4 us
  starting transfers between devices  14 us (55%)
  waiting for transfers between devices  5.2 us (20%)
  Pallas kernels  3.08 us (12%)
  between operations  1.38 us (5%)
  other arithmetic  1.07 us (4%)
  local copies, waits for them, and re-layouts  0.69 us (3%)
    ppermute x8, starting transfers between devices, cross(): return lax.ppermute(value, ('dp', 'mp'), pairs)  10.7 us
    ppermute x8, waiting for transfers between devices, cross(): return lax.ppermute(value, ('dp', 'mp'), pairs)  3.9 us
    ppermute x3, starting transfers between devices, flip(): lax.ppermute(value, axis, [(i, i ^ mask) for i in range(size)])  3.3 us
    ppermute x3, waiting for transfers between devices, flip(): lax.ppermute(value, axis, [(i, i ^ mask) for i in range(size)])  1.31 us
    pallas_call x1, Pallas kernels, body(): call(functools.partial(grad_kernel, slots), n_dp, [grad_shape, grad_shape...  1.04 us
    concatenate x1, other arithmetic, body(): jnp.concatenate([inputs, cotangent])  0.88 us
    pallas_call x1, Pallas kernels, body(): call(functools.partial(select_kernel, slots, *steps[0]), 1 + len(weights[...  0.75 us
    unnamed x8, local copies, waits for them, and re-layouts  0.66 us
  transfers between devices with their start and end apart: 11, of which 7 were waited for; matrix products, arithmetic and copies ran while one was open for 4% of the time, Pallas kernels for 8%

profile of v6, /device:TPU:0, one launch (start us, length us, event | category | flops | bytes accessed | tf_op | source)
XLA Modules:
  0.0 25.4 jit_solution(10007238796201011939)
XLA Ops:
  0.6 3.0 %collective-permute-start = (bf16[1,4,128,128]{3,2,1,0:T(8,128)(2,1)}, bf16[1,4,128,128]{3,2,1,0:T(8,128)(2,1)S(1)}, u32[]{:S(2)}, u32[]{:S(2)}) collective-permute-start(bf16[1,4,128,128]{3,2,1,0:T(8,128)(2,1)} %refs_0_.3), channel_id=1, source_target_pairs={{0,8},{1,17},{2,10},{3,19},{4,12},{5,21},{6,14},{7,23},{8,0},{9,25... | collective-permute-start | bytes 393224 | tf_op jit(solution)/shard_map/ppermute | solution.py:204
  3.6 1.5 %collective-permute-start.1 = (bf16[1,4,128,128]{3,2,1,0:T(8,128)(2,1)}, bf16[1,4,128,128]{3,2,1,0:T(8,128)(2,1)S(1)}, u32[]{:S(2)}, u32[]{:S(2)}) collective-permute-start(bf16[1,4,128,128]{3,2,1,0:T(8,128)(2,1)} %refs_4_.1), channel_id=1, source_target_pairs={{0,16},{1,9},{2,18},{3,11},{4,20},{5,13},{6,22},{7,15},{8,24},{9,1... | collective-permute-start | bytes 393224 | tf_op jit(solution)/shard_map/ppermute | solution.py:204
  5.2 0.5 %collective-permute-start.2 = (bf16[4,128,128]{2,1,0:T(8,128)(2,1)}, bf16[4,128,128]{2,1,0:T(8,128)(2,1)S(1)}, u32[]{:S(2)}, u32[]{:S(2)}) collective-permute-start(bf16[4,128,128]{2,1,0:T(8,128)(2,1)} %bitcast.10), channel_id=1, source_target_pairs={{0,8},{1,17},{2,10},{3,19},{4,12},{5,21},{6,14},{7,23},{8,0},{9,25... | collective-permute-start | bytes 393224 | tf_op jit(solution)/shard_map/ppermute | solution.py:204
  5.7 0.1 collective-permute-start.3
  5.8 0.9 %pad_maximum_fusion.tokens = bf16[16,2560]{1,0:T(8,128)(2,1)S(1)} fusion(bf16[8,2560]{1,0:T(8,128)(2,1)} %param.8, bf16[8,2560]{1,0:T(8,128)(2,1)} %param.7), kind=kLoop, calls=%fused_computation | loop fusion | flops 163840 | bytes 163840 | tf_op jit(solution)/shard_map/concatenate | solution.py:266
  6.6 1.1 %collective-permute-done.refs_1_ = bf16[1,4,128,128]{3,2,1,0:T(8,128)(2,1)S(1)} collective-permute-done((bf16[1,4,128,128]{3,2,1,0:T(8,128)(2,1)}, bf16[1,4,128,128]{3,2,1,0:T(8,128)(2,1)S(1)}, u32[]{:S(2)}, u32[]{:S(2)}) %collective-permute-start) | collective-permute-done | bytes 131104 | tf_op jit(solution)/shard_map/ppermute | solution.py:204
  7.7 1.6 %collective-permute-start.4 = (bf16[1,4,128,128]{3,2,1,0:T(8,128)(2,1)S(1)}, bf16[1,4,128,128]{3,2,1,0:T(8,128)(2,1)S(1)}, u32[]{:S(2)}, u32[]{:S(2)}) collective-permute-start(bf16[1,4,128,128]{3,2,1,0:T(8,128)(2,1)S(1)} %collective-permute-done.refs_1_), channel_id=1, source_target_pairs={{0,16},{1,9},{2,18},{3,11},{4,20},{5,13},{6,22},{7,15},{8,24},{9,1... | collective-permute-start | bytes 393224 | tf_op jit(solution)/shard_map/ppermute | solution.py:204
  9.3 0.7 %collective-permute-done.1.refs_3_.refs_6_ = bf16[1,4,128,128]{3,2,1,0:T(8,128)(2,1)S(1)} collective-permute-done((bf16[1,4,128,128]{3,2,1,0:T(8,128)(2,1)}, bf16[1,4,128,128]{3,2,1,0:T(8,128)(2,1)S(1)}, u32[]{:S(2)}, u32[]{:S(2)}) %collective-permute-start.1) | collective-permute-done | bytes 131104 | tf_op jit(solution)/shard_map/ppermute | solution.py:204
  10.0 1.7 %collective-permute-start.5 = (bf16[1,4,128,128]{3,2,1,0:T(8,128)(2,1)S(1)}, bf16[1,4,128,128]{3,2,1,0:T(8,128)(2,1)S(1)}, u32[]{:S(2)}, u32[]{:S(2)}) collective-permute-start(bf16[1,4,128,128]{3,2,1,0:T(8,128)(2,1)S(1)} %collective-permute-done.1.refs_3_.refs_6_), channel_id=1, source_target_pairs={{0,8},{1,17},{2,10},{3,19},{4,12},{5,21},{6,14},{7,23},{8,0},{9,25... | collective-permute-start | bytes 393224 | tf_op jit(solution)/shard_map/ppermute | solution.py:204
  11.7 0.1 fusion.4.keep
  12.5 0.0 copy-start.3
  12.5 0.6 %copy-done.3 = s32[1,16]{1,0:T(1,128)S(1)} copy-done((s32[1,16]{1,0:T(1,128)S(1)}, s32[1,16]{1,0:T(1,128)}, u32[]{:S(2)}) %copy-start.3) | copy-done | bytes 88
  13.1 0.1 pad_add_fusion.listed
  13.2 0.8 %shard_map.102 = (bf16[16,2048]{1,0:T(8,128)(2,1)S(1)}, s32[8,128]{1,0:T(8,128)S(1)}, f32[16,128]{1,0:T(8,128)S(1)}) custom-call(s32[17]{0:T(128)S(1)} %pad_add_fusion.listed, bf16[16,2560]{1,0:T(8,128)(2,1)S(1)} %pad_maximum_fusion.tokens, bf16[1,4,128,128]{3,2,1,0:T(8,128)(2,1)S(1)} %copy-done, bf16[1,4,128,128]{3,2,1,0:T(8,128)(2,1)S(1)} %collective-permute-done.refs_1_, ...), custom_call_target="tpu_custom_call" | custom-call | tf_op jit(solution)/shard_map/pallas_call | solution.py:255
  14.0 0.0 collective-permute-done.2
  14.0 0.0 collective-permute-done.3
  14.0 0.2 shard_map.103.sums
  14.2 0.1 collective-permute-done.4.refs_3_
  14.3 0.8 %collective-permute-done.5.refs_7_ = bf16[1,4,128,128]{3,2,1,0:T(8,128)(2,1)S(1)} collective-permute-done((bf16[1,4,128,128]{3,2,1,0:T(8,128)(2,1)S(1)}, bf16[1,4,128,128]{3,2,1,0:T(8,128)(2,1)S(1)}, u32[]{:S(2)}, u32[]{:S(2)}) %collective-permute-start.5) | collective-permute-done | bytes 131104 | tf_op jit(solution)/shard_map/ppermute | solution.py:204
  15.0 0.5 %shard_map.104 = (bf16[4,40,128]{2,1,0:T(8,128)(2,1)S(1)}, f32[4,40,128]{2,1,0:T(8,128)S(1)}, bf16[16,640]{1,0:T(8,128)(2,1)S(1)}, bf16[16,640]{1,0:T(8,128)(2,1...) custom-call(bf16[16,2048]{1,0:T(8,128)(2,1)S(1)} %get-tuple-element.18.picks, ...), custom_call_target="tpu_custom_call" | custom-call | flops 10485760 | bytes 1048576 | tf_op jit(solution)/shard_map/pallas_call | solution.py:277
  15.5 0.1 collective-permute-start.6
  15.6 1.7 %collective-permute-start.9 = (bf16[16,1280]{1,0:T(8,128)(2,1)S(1)}, bf16[16,1280]{1,0:T(8,128)(2,1)S(1)}, u32[]{:S(2)}, u32[]{:S(2)}) collective-permute-start(bf16[16,1280]{1,0:T(8,128)(2,1)S(1)} %pad_maximum_fusion.1), channel_id=1, source_target_pairs={{0,8},{1,17},{2,10},{3,19},{4,12},{5,21},{6,14},{7,23},{8,0},{9,25... | collective-permute-start | bytes 122888 | tf_op jit(solution)/shard_map/ppermute | solution.py:204
  17.4 0.0 collective-permute-done.6
  17.4 1.9 %collective-permute-start.7 = (bf16[2,40,128]{2,1,0:T(8,128)(2,1)S(1)}, bf16[2,40,128]{2,1,0:T(8,128)(2,1)S(1)}, u32[]{:S(2)}, u32[]{:S(2)}) collective-permute-start(bf16[2,40,128]{2,1,0:T(8,128)(2,1)S(1)} %dynamic-slice_convert_fusion), channel_id=1, source_target_pairs={{0,5},{1,4},{2,7},{3,6},{4,1},{5,0},{6,3},{7,2},{8,13},{9,12},{10,... | collective-permute-start | bytes 61448 | tf_op jit(solution)/shard_map/ppermute | solution.py:190
  19.3 0.4 %collective-permute-done.9 = bf16[16,1280]{1,0:T(8,128)(2,1)S(1)} collective-permute-done((bf16[16,1280]{1,0:T(8,128)(2,1)S(1)}, bf16[16,1280]{1,0:T(8,128)(2,1)S(1)}, u32[]{:S(2)}, u32[]{:S(2)}) %collective-permute-start.9) | collective-permute-done | bytes 40992 | tf_op jit(solution)/shard_map/ppermute | solution.py:204
  19.7 0.6 %collective-permute-start.10 = (bf16[16,1280]{1,0:T(8,128)(2,1)S(1)}, bf16[16,1280]{1,0:T(8,128)(2,1)S(1)}, u32[]{:S(2)}, u32[]{:S(2)}) collective-permute-start(bf16[16,1280]{1,0:T(8,128)(2,1)S(1)} %pad_maximum_fusion.2), channel_id=1, source_target_pairs={{0,16},{1,9},{2,18},{3,11},{4,20},{5,13},{6,22},{7,15},{8,24},{9,1... | collective-permute-start | bytes 122888 | tf_op jit(solution)/shard_map/ppermute | solution.py:204
  20.3 1.3 %collective-permute-done.7 = bf16[2,40,128]{2,1,0:T(8,128)(2,1)S(1)} collective-permute-done((bf16[2,40,128]{2,1,0:T(8,128)(2,1)S(1)}, bf16[2,40,128]{2,1,0:T(8,128)(2,1)S(1)}, u32[]{:S(2)}, u32[]{:S(2)}) %collective-permute-start.7) | collective-permute-done | bytes 20512 | tf_op jit(solution)/shard_map/ppermute | solution.py:190
  21.6 1.4 %collective-permute-start.8 = (bf16[1,40,128]{2,1,0:T(8,128)(2,1)S(1)}, bf16[1,40,128]{2,1,0:T(8,128)(2,1)S(1)}, u32[]{:S(2)}, u32[]{:S(2)}) collective-permute-start(bf16[1,40,128]{2,1,0:T(8,128)(2,1)S(1)} %dynamic-slice_convert_fusion.1), channel_id=1, source_target_pairs={{0,3},{1,2},{2,1},{3,0},{4,7},{5,6},{6,5},{7,4},{8,11},{9,10},{10,... | collective-permute-start | bytes 30728 | tf_op jit(solution)/shard_map/ppermute | solution.py:190
  23.0 0.8 %collective-permute-done.10 = bf16[16,1280]{1,0:T(8,128)(2,1)S(1)} collective-permute-done((bf16[16,1280]{1,0:T(8,128)(2,1)S(1)}, bf16[16,1280]{1,0:T(8,128)(2,1)S(1)}, u32[]{:S(2)}, u32[]{:S(2)}) %collective-permute-start.10) | collective-permute-done | bytes 40992 | tf_op jit(solution)/shard_map/ppermute | solution.py:204
  23.8 1.0 %shard_map.105 = (f32[1,4,128,128]{3,2,1,0:T(8,128)}, f32[1,4,128,128]{3,2,1,0:T(8,128)}, f32[8,128]{1,0:T(8,128)S(1)}) custom-call(bf16[16,640]{1,0:T(8,128)(2,1)S(1)} %get-tuple-element.23.refs_0_, bf16[16,640]{1,0:T(8,128)(2,1)S(1)} %get-tuple-element.35.refs_1_, bf16[16,640]{1,0:T(8,128)(2,1)S(1)} %get-tuple-element.33.refs_2_, ...), custom_call_target="tpu_custom_call" | custom-call | flops 8388608 | bytes 524288 | tf_op jit(solution)/shard_map/pallas_call | solution.py:300
  24.8 0.0 collective-permute-done.8.got
  24.8 0.6 %shard_map.106 = (bf16[1,2560]{1,0:T(2,128)(2,1)}, bf16[1,2560]{1,0:T(2,128)(2,1)}) custom-call(f32[1,40,128]{2,1,0:T(8,128)S(1)} %constant_dynamic-slice_fusion.kept, bf16[1,40,128]{2,1,0:T(8,128)(2,1)S(1)} %collective-permute-done.8.got, f32[8,128]{1,0:T(8,128)S(1)} %get-tuple-element.27.order), custom_call_target="tpu_custom_call" | custom-call | flops 5120 | bytes 40960 | tf_op jit(solution)/shard_map/pallas_call | solution.py:308
  (16 shorter events, 0.1 us)
Async XLA Ops:
  0.6 7.1 %collective-permute-start = (bf16[1,4,128,128]{3,2,1,0:T(8,128)(2,1)}, bf16[1,4,128,128]{3,2,1,0:T(8,128)(2,1)S(1)}, u32[]{:S(2)}, u32[]{:S(2)}) collective-permute-start(bf16[1,4,128,128]{3,2,1,0:T(8,128)(2,1)} %refs_0_.3), channel_id=1, source_target_pairs={{0,8},{1,17},{2,10},{3,19},{4,12},{5,21},{6,14},{7,23},{8,0},{9,25... | collective-permute-start | bytes 393224 | tf_op jit(solution)/shard_map/ppermute | solution.py:204
  3.6 6.4 %collective-permute-start.1 = (bf16[1,4,128,128]{3,2,1,0:T(8,128)(2,1)}, bf16[1,4,128,128]{3,2,1,0:T(8,128)(2,1)S(1)}, u32[]{:S(2)}, u32[]{:S(2)}) collective-permute-start(bf16[1,4,128,128]{3,2,1,0:T(8,128)(2,1)} %refs_4_.1), channel_id=1, source_target_pairs={{0,16},{1,9},{2,18},{3,11},{4,20},{5,13},{6,22},{7,15},{8,24},{9,1... | collective-permute-start | bytes 393224 | tf_op jit(solution)/shard_map/ppermute | solution.py:204
  5.2 8.8 %collective-permute-start.2 = (bf16[4,128,128]{2,1,0:T(8,128)(2,1)}, bf16[4,128,128]{2,1,0:T(8,128)(2,1)S(1)}, u32[]{:S(2)}, u32[]{:S(2)}) collective-permute-start(bf16[4,128,128]{2,1,0:T(8,128)(2,1)} %bitcast.10), channel_id=1, source_target_pairs={{0,8},{1,17},{2,10},{3,19},{4,12},{5,21},{6,14},{7,23},{8,0},{9,25... | collective-permute-start | bytes 393224 | tf_op jit(solution)/shard_map/ppermute | solution.py:204
  5.7 6.0 %copy-start.2 = (s32[8]{0:T(128)S(1)}, s32[8]{0:T(128)}, u32[]{:S(2)}) copy-start(s32[8]{0:T(128)} %param.13) | copy-start | bytes 100
  5.7 7.5 %copy-start = (bf16[1,4,128,128]{3,2,1,0:T(8,128)(2,1)S(1)}, bf16[1,4,128,128]{3,2,1,0:T(8,128)(2,1)}, u32[]{:S(2)}) copy-start(bf16[1,4,128,128]{3,2,1,0:T(8,128)(2,1)} %refs_0_.3) | copy-start | bytes 393220
  5.7 7.5 %copy-start.1 = (bf16[1,4,128,128]{3,2,1,0:T(8,128)(2,1)S(1)}, bf16[1,4,128,128]{3,2,1,0:T(8,128)(2,1)}, u32[]{:S(2)}) copy-start(bf16[1,4,128,128]{3,2,1,0:T(8,128)(2,1)} %refs_4_.1) | copy-start | bytes 393220
  5.7 8.3 %collective-permute-start.3 = (bf16[4,128,128]{2,1,0:T(8,128)(2,1)}, bf16[4,128,128]{2,1,0:T(8,128)(2,1)S(1)}, u32[]{:S(2)}, u32[]{:S(2)}) collective-permute-start(bf16[4,128,128]{2,1,0:T(8,128)(2,1)} %bitcast.9), channel_id=1, source_target_pairs={{0,16},{1,9},{2,18},{3,11},{4,20},{5,13},{6,22},{7,15},{8,24},{9,1... | collective-permute-start | bytes 393224 | tf_op jit(solution)/shard_map/ppermute | solution.py:204
  7.7 6.5 %collective-permute-start.4 = (bf16[1,4,128,128]{3,2,1,0:T(8,128)(2,1)S(1)}, bf16[1,4,128,128]{3,2,1,0:T(8,128)(2,1)S(1)}, u32[]{:S(2)}, u32[]{:S(2)}) collective-permute-start(bf16[1,4,128,128]{3,2,1,0:T(8,128)(2,1)S(1)} %collective-permute-done.refs_1_), channel_id=1, source_target_pairs={{0,16},{1,9},{2,18},{3,11},{4,20},{5,13},{6,22},{7,15},{8,24},{9,1... | collective-permute-start | bytes 393224 | tf_op jit(solution)/shard_map/ppermute | solution.py:204
  10.0 5.0 %collective-permute-start.5 = (bf16[1,4,128,128]{3,2,1,0:T(8,128)(2,1)S(1)}, bf16[1,4,128,128]{3,2,1,0:T(8,128)(2,1)S(1)}, u32[]{:S(2)}, u32[]{:S(2)}) collective-permute-start(bf16[1,4,128,128]{3,2,1,0:T(8,128)(2,1)S(1)} %collective-permute-done.1.refs_3_.refs_6_), channel_id=1, source_target_pairs={{0,8},{1,17},{2,10},{3,19},{4,12},{5,21},{6,14},{7,23},{8,0},{9,25... | collective-permute-start | bytes 393224 | tf_op jit(solution)/shard_map/ppermute | solution.py:204
  12.5 0.7 %copy-start.3 = (s32[1,16]{1,0:T(1,128)S(1)}, s32[1,16]{1,0:T(1,128)}, u32[]{:S(2)}) copy-start(s32[1,16]{1,0:T(1,128)} %param.11) | copy-start | bytes 196
  15.5 1.8 %collective-permute-start.6 = (bf16[4,40,128]{2,1,0:T(8,128)(2,1)S(1)}, bf16[4,40,128]{2,1,0:T(8,128)(2,1)S(1)}, u32[]{:S(2)}, u32[]{:S(2)}) collective-permute-start(bf16[4,40,128]{2,1,0:T(8,128)(2,1)S(1)} %get-tuple-element.22), channel_id=1, source_target_pairs={{0,1},{1,0},{2,3},{3,2},{4,5},{5,4},{6,7},{7,6},{8,9},{9,8},{10,11... | collective-permute-start | bytes 122888 | tf_op jit(solution)/shard_map/ppermute | solution.py:190
  15.6 4.1 %collective-permute-start.9 = (bf16[16,1280]{1,0:T(8,128)(2,1)S(1)}, bf16[16,1280]{1,0:T(8,128)(2,1)S(1)}, u32[]{:S(2)}, u32[]{:S(2)}) collective-permute-start(bf16[16,1280]{1,0:T(8,128)(2,1)S(1)} %pad_maximum_fusion.1), channel_id=1, source_target_pairs={{0,8},{1,17},{2,10},{3,19},{4,12},{5,21},{6,14},{7,23},{8,0},{9,25... | collective-permute-start | bytes 122888 | tf_op jit(solution)/shard_map/ppermute | solution.py:204
  17.4 4.2 %collective-permute-start.7 = (bf16[2,40,128]{2,1,0:T(8,128)(2,1)S(1)}, bf16[2,40,128]{2,1,0:T(8,128)(2,1)S(1)}, u32[]{:S(2)}, u32[]{:S(2)}) collective-permute-start(bf16[2,40,128]{2,1,0:T(8,128)(2,1)S(1)} %dynamic-slice_convert_fusion), channel_id=1, source_target_pairs={{0,5},{1,4},{2,7},{3,6},{4,1},{5,0},{6,3},{7,2},{8,13},{9,12},{10,... | collective-permute-start | bytes 61448 | tf_op jit(solution)/shard_map/ppermute | solution.py:190
  19.7 4.1 %collective-permute-start.10 = (bf16[16,1280]{1,0:T(8,128)(2,1)S(1)}, bf16[16,1280]{1,0:T(8,128)(2,1)S(1)}, u32[]{:S(2)}, u32[]{:S(2)}) collective-permute-start(bf16[16,1280]{1,0:T(8,128)(2,1)S(1)} %pad_maximum_fusion.2), channel_id=1, source_target_pairs={{0,16},{1,9},{2,18},{3,11},{4,20},{5,13},{6,22},{7,15},{8,24},{9,1... | collective-permute-start | bytes 122888 | tf_op jit(solution)/shard_map/ppermute | solution.py:204
  21.6 3.2 %collective-permute-start.8 = (bf16[1,40,128]{2,1,0:T(8,128)(2,1)S(1)}, bf16[1,40,128]{2,1,0:T(8,128)(2,1)S(1)}, u32[]{:S(2)}, u32[]{:S(2)}) collective-permute-start(bf16[1,40,128]{2,1,0:T(8,128)(2,1)S(1)} %dynamic-slice_convert_fusion.1), channel_id=1, source_target_pairs={{0,3},{1,2},{2,1},{3,0},{4,7},{5,6},{6,5},{7,4},{8,11},{9,10},{10,... | collective-permute-start | bytes 30728 | tf_op jit(solution)/shard_map/ppermute | solution.py:190

commit v7 on v6

--- a/solution.py
+++ b/solution.py
@@ -114,40 +114,51 @@
     return functools.reduce(lambda found, i: found ^ number >> i & 1, range(1, size.bit_length()), number & 1)
 
 
-def hidden_kernel(slots, blocks, masks_in, masks_out, late, picks, table, keep, sums, *refs):
-    count = len(masks_in)
-    firsts = dict(zip(masks_in, refs[:count]))
-    seconds = dict(zip(masks_out, refs[count : 2 * count]))
-    away, home, *rows = refs[2 * count : -1]
+def place(acc, rows, entries, start, slots, mask):
+    half = acc.shape[0]
+    for j in range(slots):
+        at = mask * slots + j
+        index, used = entries[0, at], entries[1, at].astype(F32)
+        block = rows[:, j * BS : (j + 1) * BS] * used
+        acc[:, :, pl.ds(start + index, 1), :] = block.reshape(half, 2, 1, BS)
+
+
+def activation_kernel(slots, early, late, picks, table, keep, sums, first, *refs):
+    *seconds, hidden, out = refs
+    local = keep.shape[0]
+    out[...] = jnp.zeros_like(out)
+    entries = table[...]
+    pre, _ = add_slots(slots, picks, sums[:local], None, [late], [], [first], [])
+    activation, slope = gelu_parts(pre)
+    dropped = activation * keep[...]
+    hidden[:local] = dropped
+    hidden[local:] = keep[...] * slope
+    for mask, second in zip(early, seconds):
+        place(out, dot(dropped.astype(BF16), side_by_side(second, slots), ((1,), (0,))), entries, 0, slots, mask)
+
+
+def hidden_kernel(slots, late, picks, table, sums, hidden, out, second, *refs):
     acc = refs[-1]
-    local = keep.shape[0]
-    half = local // 2
-    acc[...] = jnp.zeros_like(acc)
+    firsts, (away, home, *rows) = refs[: late + 1], refs[late + 1 : -1]
+    local = hidden.shape[0] // 2
+    half, blocks = local // 2, out.shape[2]
     entries = table[...]
-    pre, grad = add_slots(
-        slots, picks, sums[:local], sums[local:], late, late, [firsts[m] for m in late], [seconds[m] for m in late]
-    )
-    activation, slope = gelu_parts(pre)
-    dropped_full = activation * keep[...]
-    grad_full = grad * keep[...] * slope
-    dropped, grad_pre = dropped_full.astype(BF16), grad_full.astype(BF16)
-    for mask in range(count):
-        out_row = dot(dropped, side_by_side(seconds[mask], slots), ((1,), (0,)))
-        in_row = dot(grad_pre, stacked(firsts[mask], slots), ((1,), (1,)))
-        for j in range(slots):
-            at = mask * slots + j
-            index, used = entries[0, at], entries[1, at].astype(F32)
-            cut = slice(j * BS, (j + 1) * BS)
-            acc[:, :, pl.ds(index, 1), :] = (out_row[:, cut] * used).reshape(half, 2, 1, BS)
-            acc[:, :, pl.ds(blocks + index, 1), :] = (in_row[:, cut] * used).reshape(half, 2, 1, BS)
+    _, grad = add_slots(slots, picks, None, sums[local:], [], [late], [], [second])
+    dropped, grad_pre = hidden[:local], grad * hidden[local:]
+    acc[:, :, :blocks] = out[...]
+    acc[:, :, blocks:] = jnp.zeros_like(out)
+    place(acc, dot(dropped.astype(BF16), side_by_side(second, slots), ((1,), (0,))), entries, 0, slots, late)
+    for mask, first in enumerate(firsts):
+        in_rows = dot(grad_pre.astype(BF16), stacked(first, slots), ((1,), (1,)))
+        place(acc, in_rows, entries, blocks, slots, mask)
     odd = bit_parity(lax.axis_index("mp"), 2 * half)
     for i in range(half):
         even_row, odd_row = acc[i, bit_parity(i, half)], acc[i, 1 - bit_parity(i, half)]
         away[i] = jnp.where(odd == 1, even_row, odd_row).astype(BF16)
         home[i] = jnp.where(odd == 1, odd_row, even_row)
-    hidden = jnp.concatenate([dropped_full, grad_full], axis=0).astype(BF16)
+    both = jnp.concatenate([dropped, grad_pre], axis=0).astype(BF16)
     for mask, message in enumerate(rows):
-        message[:, :BS] = hidden
+        message[:, :BS] = both
         message[:, BS:] = picks[:, mask * slots * BS : (mask + 1) * slots * BS]
 
 
@@ -248,7 +259,6 @@
     rank = lax.axis_index("mp")
     keep = keep_factor(drop_seeds, rank * BS)
     steps = [([0, bits[0]], [0, bits[-1]])]
-    late = [n_dp - 1]
     steps.append([[mask for mask in range(n_dp - 1) if mask not in done] for done in steps[0]])
     weights = [[firsts[m] for m in masks_in] + [seconds[m] for m in masks_out] for masks_in, masks_out in steps[:1]]
     weights.append([seconds[m] for m in steps[1][1]] + [firsts[m] for m in steps[1][0]])
@@ -273,16 +283,23 @@
     )(picks, *weights[1], sums)
 
     half = local // 2
-    masks_in, masks_out = sorted(firsts), sorted(seconds)
+    early, late = list(range(n_dp - 1)), n_dp - 1
+    hidden, out = call(
+        functools.partial(activation_kernel, slots, early, late),
+        5 + len(early),
+        [shape((2 * local, BS), F32), shape((half, 2, blocks, BS), F32)],
+        0,
+        0,
+    )(picks, table, keep, sums, firsts[late], *[seconds[m] for m in early])
     away, home, *rows = call(
-        functools.partial(hidden_kernel, slots, blocks, masks_in, masks_out, late),
-        4 + 2 * n_dp,
+        functools.partial(hidden_kernel, slots, late),
+        6 + n_dp,
         [shape((half, 2 * blocks, BS), BF16), shape((half, 2 * blocks, BS), F32)]
         + [shape((2 * local, (1 + slots) * BS), BF16)] * n_dp,
-        (2 * n_dp + 2) * piece_flops,
-        2 * n_dp * piece_bytes,
+        (n_dp + 2) * piece_flops,
+        (n_dp + 1) * piece_bytes,
         scratch=[pltpu.VMEM((half, 2, 2 * blocks, BS), F32)],
-    )(picks, table, keep, sums, *[firsts[m] for m in masks_in], *[seconds[m] for m in masks_out])
+    )(picks, table, sums, hidden, out, seconds[late], *[firsts[m] for m in range(n_dp)])
 
     total = home + flip(away, "mp", n_mp, 1).astype(F32)
     messages = exchange(rows, n_dp, n_mp, bits)

time: 25.6 us -> 25.5 us (level)
  waiting for transfers between devices: 5.2 us -> 4.88 us
    ppermute x8, waiting for transfers between devices: 3.9 us -> 3.57 us  [cross(): return lax.ppermute(value, ('dp', 'mp'), pairs)]
    pallas_call x1 -> x2, Pallas kernels: 0.5 us -> 0.73 us  [the longest x1 0.41 us: body(): call(functools.partial(hidden_kernel, slots, late), 6 + n_dp, [shape((hal...]
  transfers between devices with their start and end apart: 11 -> 11, of which waited for: 7 -> 7; matrix products, arithmetic and copies ran while one was open for 4% -> 4% of each run, Pallas kernels for 8% -> 9%
where the time goes in v7:
time: 25.5 us; the launch traced here: 25.3 us
  starting transfers between devices  14 us (55%)
  waiting for transfers between devices  4.88 us (19%)
  Pallas kernels  3.31 us (13%)
  between operations  1.38 us (5%)
  other arithmetic  1.07 us (4%)
  local copies, waits for them, and re-layouts  0.69 us (3%)
    ppermute x8, starting transfers between devices, cross(): return lax.ppermute(value, ('dp', 'mp'), pairs)  10.7 us
    ppermute x8, waiting for transfers between devices, cross(): return lax.ppermute(value, ('dp', 'mp'), pairs)  3.57 us
    ppermute x3, starting transfers between devices, flip(): lax.ppermute(value, axis, [(i, i ^ mask) for i in range(size)])  3.3 us
    ppermute x3, waiting for transfers between devices, flip(): lax.ppermute(value, axis, [(i, i ^ mask) for i in range(size)])  1.31 us
    pallas_call x1, Pallas kernels, body(): call(functools.partial(grad_kernel, slots), n_dp, [grad_shape, grad_shape...  1.05 us
    concatenate x1, other arithmetic, body(): jnp.concatenate([inputs, cotangent])  0.88 us
    pallas_call x1, Pallas kernels, body(): call(functools.partial(select_kernel, slots, *steps[0]), 1 + len(weights[...  0.75 us
    unnamed x8, local copies, waits for them, and re-layouts  0.66 us
  transfers between devices with their start and end apart: 11, of which 7 were waited for; matrix products, arithmetic and copies ran while one was open for 4% of the time, Pallas kernels for 9%

profile of v7, /device:TPU:0, one launch (start us, length us, event | category | flops | bytes accessed | tf_op | source)
XLA Modules:
  0.0 25.3 jit_solution(17097401805905217675)
XLA Ops:
  0.6 3.0 %collective-permute-start = (bf16[1,4,128,128]{3,2,1,0:T(8,128)(2,1)}, bf16[1,4,128,128]{3,2,1,0:T(8,128)(2,1)S(1)}, u32[]{:S(2)}, u32[]{:S(2)}) collective-permute-start(bf16[1,4,128,128]{3,2,1,0:T(8,128)(2,1)} %refs_0_.5), channel_id=1, source_target_pairs={{0,8},{1,17},{2,10},{3,19},{4,12},{5,21},{6,14},{7,23},{8,0},{9,25... | collective-permute-start | bytes 393224 | tf_op jit(solution)/shard_map/ppermute | solution.py:215
  3.6 1.5 %collective-permute-start.1 = (bf16[1,4,128,128]{3,2,1,0:T(8,128)(2,1)}, bf16[1,4,128,128]{3,2,1,0:T(8,128)(2,1)S(1)}, u32[]{:S(2)}, u32[]{:S(2)}) collective-permute-start(bf16[1,4,128,128]{3,2,1,0:T(8,128)(2,1)} %refs_0_.4), channel_id=1, source_target_pairs={{0,16},{1,9},{2,18},{3,11},{4,20},{5,13},{6,22},{7,15},{8,24},{9,1... | collective-permute-start | bytes 393224 | tf_op jit(solution)/shard_map/ppermute | solution.py:215
  5.2 0.5 %collective-permute-start.2 = (bf16[4,128,128]{2,1,0:T(8,128)(2,1)}, bf16[4,128,128]{2,1,0:T(8,128)(2,1)S(1)}, u32[]{:S(2)}, u32[]{:S(2)}) collective-permute-start(bf16[4,128,128]{2,1,0:T(8,128)(2,1)} %bitcast.9), channel_id=1, source_target_pairs={{0,8},{1,17},{2,10},{3,19},{4,12},{5,21},{6,14},{7,23},{8,0},{9,25... | collective-permute-start | bytes 393224 | tf_op jit(solution)/shard_map/ppermute | solution.py:215
  5.7 0.1 collective-permute-start.3
  5.8 0.9 %pad_maximum_fusion.tokens = bf16[16,2560]{1,0:T(8,128)(2,1)S(1)} fusion(bf16[8,2560]{1,0:T(8,128)(2,1)} %param.8, bf16[8,2560]{1,0:T(8,128)(2,1)} %param.7), kind=kLoop, calls=%fused_computation | loop fusion | flops 163840 | bytes 163840 | tf_op jit(solution)/shard_map/concatenate | solution.py:276
  6.6 1.1 %collective-permute-done.refs_1_ = bf16[1,4,128,128]{3,2,1,0:T(8,128)(2,1)S(1)} collective-permute-done((bf16[1,4,128,128]{3,2,1,0:T(8,128)(2,1)}, bf16[1,4,128,128]{3,2,1,0:T(8,128)(2,1)S(1)}, u32[]{:S(2)}, u32[]{:S(2)}) %collective-permute-start) | collective-permute-done | bytes 131104 | tf_op jit(solution)/shard_map/ppermute | solution.py:215
  7.7 1.6 %collective-permute-start.4 = (bf16[1,4,128,128]{3,2,1,0:T(8,128)(2,1)S(1)}, bf16[1,4,128,128]{3,2,1,0:T(8,128)(2,1)S(1)}, u32[]{:S(2)}, u32[]{:S(2)}) collective-permute-start(bf16[1,4,128,128]{3,2,1,0:T(8,128)(2,1)S(1)} %collective-permute-done.refs_1_), channel_id=1, source_target_pairs={{0,16},{1,9},{2,18},{3,11},{4,20},{5,13},{6,22},{7,15},{8,24},{9,1... | collective-permute-start | bytes 393224 | tf_op jit(solution)/shard_map/ppermute | solution.py:215
  9.3 0.7 %collective-permute-done.1.refs_3_.refs_2_ = bf16[1,4,128,128]{3,2,1,0:T(8,128)(2,1)S(1)} collective-permute-done((bf16[1,4,128,128]{3,2,1,0:T(8,128)(2,1)}, bf16[1,4,128,128]{3,2,1,0:T(8,128)(2,1)S(1)}, u32[]{:S(2)}, u32[]{:S(2)}) %collective-permute-start.1) | collective-permute-done | bytes 131104 | tf_op jit(solution)/shard_map/ppermute | solution.py:215
  10.0 1.7 %collective-permute-start.5 = (bf16[1,4,128,128]{3,2,1,0:T(8,128)(2,1)S(1)}, bf16[1,4,128,128]{3,2,1,0:T(8,128)(2,1)S(1)}, u32[]{:S(2)}, u32[]{:S(2)}) collective-permute-start(bf16[1,4,128,128]{3,2,1,0:T(8,128)(2,1)S(1)} %collective-permute-done.1.refs_3_.refs_2_), channel_id=1, source_target_pairs={{0,8},{1,17},{2,10},{3,19},{4,12},{5,21},{6,14},{7,23},{8,0},{9,25... | collective-permute-start | bytes 393224 | tf_op jit(solution)/shard_map/ppermute | solution.py:215
  11.7 0.1 fusion.4.keep
  12.5 0.0 copy-start.3
  12.5 0.6 %copy-done.3 = s32[1,16]{1,0:T(1,128)S(1)} copy-done((s32[1,16]{1,0:T(1,128)S(1)}, s32[1,16]{1,0:T(1,128)}, u32[]{:S(2)}) %copy-start.3) | copy-done | bytes 88
  13.1 0.1 pad_add_fusion.listed
  13.2 0.8 %shard_map.102 = (bf16[16,2048]{1,0:T(8,128)(2,1)S(1)}, s32[8,128]{1,0:T(8,128)S(1)}, f32[16,128]{1,0:T(8,128)S(1)}) custom-call(s32[17]{0:T(128)S(1)} %pad_add_fusion.listed, bf16[16,2560]{1,0:T(8,128)(2,1)S(1)} %pad_maximum_fusion.tokens, bf16[1,4,128,128]{3,2,1,0:T(8,128)(2,1)S(1)} %copy-done.1, ...), custom_call_target="tpu_custom_call" | custom-call | tf_op jit(solution)/shard_map/pallas_call | solution.py:265
  14.0 0.0 collective-permute-done.2
  14.0 0.0 collective-permute-done.3
  14.0 0.2 shard_map.103.sums
  14.2 0.1 collective-permute-done.4.first.refs_3_
  14.3 0.3 %shard_map.104 = (f32[16,128]{1,0:T(8,128)S(1)}, f32[4,2,20,128]{3,2,1,0:T(8,128)S(1)}) custom-call(bf16[16,2048]{1,0:T(8,128)(2,1)S(1)} %get-tuple-element.20.picks, s32[8,128]{1,0:T(8,128)S(1)} %get-tuple-element.21.table, f32[8,128]{1,0:T(8,128)S(1)} %fusion.4.keep, f32[16,128]{1,0:T(8,128)S(1)} %shard_map.103.sums, ...), custom_call_target="tpu_custom_call" | custom-call | tf_op jit(solution)/shard_map/pallas_call | solution.py:287
  14.6 0.4 %collective-permute-done.5.second = bf16[1,4,128,128]{3,2,1,0:T(8,128)(2,1)S(1)} collective-permute-done((bf16[1,4,128,128]{3,2,1,0:T(8,128)(2,1)S(1)}, bf16[1,4,128,128]{3,2,1,0:T(8,128)(2,1)S(1)}, u32[]{:S(2)}, u32[]{:S(2)}) %collective-permute-start.5) | collective-permute-done | bytes 131104 | tf_op jit(solution)/shard_map/ppermute | solution.py:215
  15.0 0.4 %shard_map.105 = (bf16[4,40,128]{2,1,0:T(8,128)(2,1)S(1)}, f32[4,40,128]{2,1,0:T(8,128)S(1)}, bf16[16,640]{1,0:T(8,128)(2,1)S(1)}, bf16[16,640]{1,0:T(8,128)(2,1...) custom-call(bf16[16,2048]{1,0:T(8,128)(2,1)S(1)} %get-tuple-element.20.picks, ...), custom_call_target="tpu_custom_call" | custom-call | flops 6291456 | bytes 655360 | tf_op jit(solution)/shard_map/pallas_call | solution.py:294
  15.4 0.1 collective-permute-start.6
  15.5 1.7 %collective-permute-start.9 = (bf16[16,1280]{1,0:T(8,128)(2,1)S(1)}, bf16[16,1280]{1,0:T(8,128)(2,1)S(1)}, u32[]{:S(2)}, u32[]{:S(2)}) collective-permute-start(bf16[16,1280]{1,0:T(8,128)(2,1)S(1)} %pad_maximum_fusion.1), channel_id=1, source_target_pairs={{0,8},{1,17},{2,10},{3,19},{4,12},{5,21},{6,14},{7,23},{8,0},{9,25... | collective-permute-start | bytes 122888 | tf_op jit(solution)/shard_map/ppermute | solution.py:215
  17.3 1.9 %collective-permute-start.7 = (bf16[2,40,128]{2,1,0:T(8,128)(2,1)S(1)}, bf16[2,40,128]{2,1,0:T(8,128)(2,1)S(1)}, u32[]{:S(2)}, u32[]{:S(2)}) collective-permute-start(bf16[2,40,128]{2,1,0:T(8,128)(2,1)S(1)} %dynamic-slice_convert_fusion), channel_id=1, source_target_pairs={{0,5},{1,4},{2,7},{3,6},{4,1},{5,0},{6,3},{7,2},{8,13},{9,12},{10,... | collective-permute-start | bytes 61448 | tf_op jit(solution)/shard_map/ppermute | solution.py:201
  19.2 0.4 %collective-permute-done.9 = bf16[16,1280]{1,0:T(8,128)(2,1)S(1)} collective-permute-done((bf16[16,1280]{1,0:T(8,128)(2,1)S(1)}, bf16[16,1280]{1,0:T(8,128)(2,1)S(1)}, u32[]{:S(2)}, u32[]{:S(2)}) %collective-permute-start.9) | collective-permute-done | bytes 40992 | tf_op jit(solution)/shard_map/ppermute | solution.py:215
  19.6 0.6 %collective-permute-start.10 = (bf16[16,1280]{1,0:T(8,128)(2,1)S(1)}, bf16[16,1280]{1,0:T(8,128)(2,1)S(1)}, u32[]{:S(2)}, u32[]{:S(2)}) collective-permute-start(bf16[16,1280]{1,0:T(8,128)(2,1)S(1)} %pad_maximum_fusion.2), channel_id=1, source_target_pairs={{0,16},{1,9},{2,18},{3,11},{4,20},{5,13},{6,22},{7,15},{8,24},{9,1... | collective-permute-start | bytes 122888 | tf_op jit(solution)/shard_map/ppermute | solution.py:215
  20.2 1.3 %collective-permute-done.7 = bf16[2,40,128]{2,1,0:T(8,128)(2,1)S(1)} collective-permute-done((bf16[2,40,128]{2,1,0:T(8,128)(2,1)S(1)}, bf16[2,40,128]{2,1,0:T(8,128)(2,1)S(1)}, u32[]{:S(2)}, u32[]{:S(2)}) %collective-permute-start.7) | collective-permute-done | bytes 20512 | tf_op jit(solution)/shard_map/ppermute | solution.py:201
  21.5 1.4 %collective-permute-start.8 = (bf16[1,40,128]{2,1,0:T(8,128)(2,1)S(1)}, bf16[1,40,128]{2,1,0:T(8,128)(2,1)S(1)}, u32[]{:S(2)}, u32[]{:S(2)}) collective-permute-start(bf16[1,40,128]{2,1,0:T(8,128)(2,1)S(1)} %dynamic-slice_convert_fusion.1), channel_id=1, source_target_pairs={{0,3},{1,2},{2,1},{3,0},{4,7},{5,6},{6,5},{7,4},{8,11},{9,10},{10,... | collective-permute-start | bytes 30728 | tf_op jit(solution)/shard_map/ppermute | solution.py:201
  22.9 0.8 %collective-permute-done.10 = bf16[16,1280]{1,0:T(8,128)(2,1)S(1)} collective-permute-done((bf16[16,1280]{1,0:T(8,128)(2,1)S(1)}, bf16[16,1280]{1,0:T(8,128)(2,1)S(1)}, u32[]{:S(2)}, u32[]{:S(2)}) %collective-permute-start.10) | collective-permute-done | bytes 40992 | tf_op jit(solution)/shard_map/ppermute | solution.py:215
  23.7 1.0 %shard_map.106 = (f32[1,4,128,128]{3,2,1,0:T(8,128)}, f32[1,4,128,128]{3,2,1,0:T(8,128)}, f32[8,128]{1,0:T(8,128)S(1)}) custom-call(bf16[16,640]{1,0:T(8,128)(2,1)S(1)} %get-tuple-element.27.refs_0_, bf16[16,640]{1,0:T(8,128)(2,1)S(1)} %get-tuple-element.39.refs_1_, bf16[16,640]{1,0:T(8,128)(2,1)S(1)} %get-tuple-element.37.refs_2_, ...), custom_call_target="tpu_custom_call" | custom-call | flops 8388608 | bytes 524288 | tf_op jit(solution)/shard_map/pallas_call | solution.py:317
  24.7 0.0 collective-permute-done.8.got
  24.7 0.6 %shard_map.107 = (bf16[1,2560]{1,0:T(2,128)(2,1)}, bf16[1,2560]{1,0:T(2,128)(2,1)}) custom-call(f32[1,40,128]{2,1,0:T(8,128)S(1)} %constant_dynamic-slice_fusion.kept, bf16[1,40,128]{2,1,0:T(8,128)(2,1)S(1)} %collective-permute-done.8.got, f32[8,128]{1,0:T(8,128)S(1)} %get-tuple-element.31.order), custom_call_target="tpu_custom_call" | custom-call | flops 5120 | bytes 40960 | tf_op jit(solution)/shard_map/pallas_call | solution.py:325
  (17 shorter events, 0.1 us)
Async XLA Ops:
  0.6 7.1 %collective-permute-start = (bf16[1,4,128,128]{3,2,1,0:T(8,128)(2,1)}, bf16[1,4,128,128]{3,2,1,0:T(8,128)(2,1)S(1)}, u32[]{:S(2)}, u32[]{:S(2)}) collective-permute-start(bf16[1,4,128,128]{3,2,1,0:T(8,128)(2,1)} %refs_0_.5), channel_id=1, source_target_pairs={{0,8},{1,17},{2,10},{3,19},{4,12},{5,21},{6,14},{7,23},{8,0},{9,25... | collective-permute-start | bytes 393224 | tf_op jit(solution)/shard_map/ppermute | solution.py:215
  3.6 6.4 %collective-permute-start.1 = (bf16[1,4,128,128]{3,2,1,0:T(8,128)(2,1)}, bf16[1,4,128,128]{3,2,1,0:T(8,128)(2,1)S(1)}, u32[]{:S(2)}, u32[]{:S(2)}) collective-permute-start(bf16[1,4,128,128]{3,2,1,0:T(8,128)(2,1)} %refs_0_.4), channel_id=1, source_target_pairs={{0,16},{1,9},{2,18},{3,11},{4,20},{5,13},{6,22},{7,15},{8,24},{9,1... | collective-permute-start | bytes 393224 | tf_op jit(solution)/shard_map/ppermute | solution.py:215
  5.2 8.8 %collective-permute-start.2 = (bf16[4,128,128]{2,1,0:T(8,128)(2,1)}, bf16[4,128,128]{2,1,0:T(8,128)(2,1)S(1)}, u32[]{:S(2)}, u32[]{:S(2)}) collective-permute-start(bf16[4,128,128]{2,1,0:T(8,128)(2,1)} %bitcast.9), channel_id=1, source_target_pairs={{0,8},{1,17},{2,10},{3,19},{4,12},{5,21},{6,14},{7,23},{8,0},{9,25... | collective-permute-start | bytes 393224 | tf_op jit(solution)/shard_map/ppermute | solution.py:215
  5.7 6.0 %copy-start.2 = (s32[8]{0:T(128)S(1)}, s32[8]{0:T(128)}, u32[]{:S(2)}) copy-start(s32[8]{0:T(128)} %param.13) | copy-start | bytes 100
  5.7 7.5 %copy-start = (bf16[1,4,128,128]{3,2,1,0:T(8,128)(2,1)S(1)}, bf16[1,4,128,128]{3,2,1,0:T(8,128)(2,1)}, u32[]{:S(2)}) copy-start(bf16[1,4,128,128]{3,2,1,0:T(8,128)(2,1)} %refs_0_.4) | copy-start | bytes 393220
  5.7 7.5 %copy-start.1 = (bf16[1,4,128,128]{3,2,1,0:T(8,128)(2,1)S(1)}, bf16[1,4,128,128]{3,2,1,0:T(8,128)(2,1)}, u32[]{:S(2)}) copy-start(bf16[1,4,128,128]{3,2,1,0:T(8,128)(2,1)} %refs_0_.5) | copy-start | bytes 393220
  5.7 8.3 %collective-permute-start.3 = (bf16[4,128,128]{2,1,0:T(8,128)(2,1)}, bf16[4,128,128]{2,1,0:T(8,128)(2,1)S(1)}, u32[]{:S(2)}, u32[]{:S(2)}) collective-permute-start(bf16[4,128,128]{2,1,0:T(8,128)(2,1)} %bitcast.10), channel_id=1, source_target_pairs={{0,16},{1,9},{2,18},{3,11},{4,20},{5,13},{6,22},{7,15},{8,24},{9,1... | collective-permute-start | bytes 393224 | tf_op jit(solution)/shard_map/ppermute | solution.py:215
  7.7 6.5 %collective-permute-start.4 = (bf16[1,4,128,128]{3,2,1,0:T(8,128)(2,1)S(1)}, bf16[1,4,128,128]{3,2,1,0:T(8,128)(2,1)S(1)}, u32[]{:S(2)}, u32[]{:S(2)}) collective-permute-start(bf16[1,4,128,128]{3,2,1,0:T(8,128)(2,1)S(1)} %collective-permute-done.refs_1_), channel_id=1, source_target_pairs={{0,16},{1,9},{2,18},{3,11},{4,20},{5,13},{6,22},{7,15},{8,24},{9,1... | collective-permute-start | bytes 393224 | tf_op jit(solution)/shard_map/ppermute | solution.py:215
  10.0 5.0 %collective-permute-start.5 = (bf16[1,4,128,128]{3,2,1,0:T(8,128)(2,1)S(1)}, bf16[1,4,128,128]{3,2,1,0:T(8,128)(2,1)S(1)}, u32[]{:S(2)}, u32[]{:S(2)}) collective-permute-start(bf16[1,4,128,128]{3,2,1,0:T(8,128)(2,1)S(1)} %collective-permute-done.1.refs_3_.refs_2_), channel_id=1, source_target_pairs={{0,8},{1,17},{2,10},{3,19},{4,12},{5,21},{6,14},{7,23},{8,0},{9,25... | collective-permute-start | bytes 393224 | tf_op jit(solution)/shard_map/ppermute | solution.py:215
  12.5 0.7 %copy-start.3 = (s32[1,16]{1,0:T(1,128)S(1)}, s32[1,16]{1,0:T(1,128)}, u32[]{:S(2)}) copy-start(s32[1,16]{1,0:T(1,128)} %param.11) | copy-start | bytes 196
  15.4 1.8 %collective-permute-start.6 = (bf16[4,40,128]{2,1,0:T(8,128)(2,1)S(1)}, bf16[4,40,128]{2,1,0:T(8,128)(2,1)S(1)}, u32[]{:S(2)}, u32[]{:S(2)}) collective-permute-start(bf16[4,40,128]{2,1,0:T(8,128)(2,1)S(1)} %get-tuple-element.26), channel_id=1, source_target_pairs={{0,1},{1,0},{2,3},{3,2},{4,5},{5,4},{6,7},{7,6},{8,9},{9,8},{10,11... | collective-permute-start | bytes 122888 | tf_op jit(solution)/shard_map/ppermute | solution.py:201
  15.5 4.1 %collective-permute-start.9 = (bf16[16,1280]{1,0:T(8,128)(2,1)S(1)}, bf16[16,1280]{1,0:T(8,128)(2,1)S(1)}, u32[]{:S(2)}, u32[]{:S(2)}) collective-permute-start(bf16[16,1280]{1,0:T(8,128)(2,1)S(1)} %pad_maximum_fusion.1), channel_id=1, source_target_pairs={{0,8},{1,17},{2,10},{3,19},{4,12},{5,21},{6,14},{7,23},{8,0},{9,25... | collective-permute-start | bytes 122888 | tf_op jit(solution)/shard_map/ppermute | solution.py:215
  17.3 4.2 %collective-permute-start.7 = (bf16[2,40,128]{2,1,0:T(8,128)(2,1)S(1)}, bf16[2,40,128]{2,1,0:T(8,128)(2,1)S(1)}, u32[]{:S(2)}, u32[]{:S(2)}) collective-permute-start(bf16[2,40,128]{2,1,0:T(8,128)(2,1)S(1)} %dynamic-slice_convert_fusion), channel_id=1, source_target_pairs={{0,5},{1,4},{2,7},{3,6},{4,1},{5,0},{6,3},{7,2},{8,13},{9,12},{10,... | collective-permute-start | bytes 61448 | tf_op jit(solution)/shard_map/ppermute | solution.py:201
  19.6 4.1 %collective-permute-start.10 = (bf16[16,1280]{1,0:T(8,128)(2,1)S(1)}, bf16[16,1280]{1,0:T(8,128)(2,1)S(1)}, u32[]{:S(2)}, u32[]{:S(2)}) collective-permute-start(bf16[16,1280]{1,0:T(8,128)(2,1)S(1)} %pad_maximum_fusion.2), channel_id=1, source_target_pairs={{0,16},{1,9},{2,18},{3,11},{4,20},{5,13},{6,22},{7,15},{8,24},{9,1... | collective-permute-start | bytes 122888 | tf_op jit(solution)/shard_map/ppermute | solution.py:215
  21.5 3.2 %collective-permute-start.8 = (bf16[1,40,128]{2,1,0:T(8,128)(2,1)S(1)}, bf16[1,40,128]{2,1,0:T(8,128)(2,1)S(1)}, u32[]{:S(2)}, u32[]{:S(2)}) collective-permute-start(bf16[1,40,128]{2,1,0:T(8,128)(2,1)S(1)} %dynamic-slice_convert_fusion.1), channel_id=1, source_target_pairs={{0,3},{1,2},{2,1},{3,0},{4,7},{5,6},{6,5},{7,4},{8,11},{9,10},{10,... | collective-permute-start | bytes 30728 | tf_op jit(solution)/shard_map/ppermute | solution.py:201

commit v8 on v7

--- a/solution.py
+++ b/solution.py
@@ -254,7 +254,9 @@
     piece_bytes = slots * BS * BS * 2
 
     bits = [1 << i for i in range(n_dp.bit_length() - 1)]
-    firsts, seconds = gather([w_in, w_out], [w_in[0], w_out[0]], n_dp, n_mp, [bits, bits[::-1]])
+    tokens = jnp.concatenate([inputs, cotangent])
+    *held, tokens = lax.optimization_barrier((w_in[0], w_out[0], tokens))
+    firsts, seconds = gather([w_in, w_out], held, n_dp, n_mp, [bits, bits[::-1]])
 
     rank = lax.axis_index("mp")
     keep = keep_factor(drop_seeds, rank * BS)
@@ -273,7 +275,7 @@
         0,
         0,
         scalars=1,
-    )(jnp.concatenate([block_index[0], block_count]), jnp.concatenate([inputs, cotangent]), *weights[0])
+    )(jnp.concatenate([block_index[0], block_count]), tokens, *weights[0])
     sums = call(
         functools.partial(partial_kernel, slots, *steps[1]),
         2 + len(weights[1]),

time: 25.5 us -> 25.4 us (level)
  waiting for transfers between devices: 4.88 us -> 3.6 us
  starting transfers between devices: 14 us -> 14.6 us
  other arithmetic: 1.07 us -> 1.65 us
    ppermute x3, waiting for transfers between devices: 1.31 us -> 0.33 us  [flip(): lax.ppermute(value, axis, [(i, i ^ mask) for i in range(size)])]
    mul x1, other arithmetic: 0.08 us -> 0.73 us  [keep_factor(): return kept.astype(F32) * jnp.float32(8.0 / 7.0)]
    ppermute x3, starting transfers between devices: 3.3 us -> 3.64 us  [flip(): lax.ppermute(value, axis, [(i, i ^ mask) for i in range(size)])]
    ppermute x8, waiting for transfers between devices: 3.57 us -> 3.27 us  [cross(): return lax.ppermute(value, ('dp', 'mp'), pairs)]
    unnamed x8 -> x6, local copies, waits for them, and re-layouts: 0.66 us -> 0.66 us
  transfers between devices with their start and end apart: 11 -> 11, of which waited for: 7 -> 6; matrix products, arithmetic and copies ran while one was open for 4% -> 7% of each run, Pallas kernels for 9% -> 9%
where the time goes in v8:
time: 25.4 us; the launch traced here: 25.2 us
  starting transfers between devices  14.6 us (57%)
  waiting for transfers between devices  3.6 us (14%)
  Pallas kernels  3.31 us (13%)
  other arithmetic  1.65 us (6%)
  between operations  1.4 us (6%)
  local copies, waits for them, and re-layouts  0.69 us (3%)
    ppermute x8, starting transfers between devices, cross(): return lax.ppermute(value, ('dp', 'mp'), pairs)  11 us
    ppermute x3, starting transfers between devices, flip(): lax.ppermute(value, axis, [(i, i ^ mask) for i in range(size)])  3.64 us
    ppermute x8, waiting for transfers between devices, cross(): return lax.ppermute(value, ('dp', 'mp'), pairs)  3.27 us
    pallas_call x1, Pallas kernels, body(): call(functools.partial(grad_kernel, slots), n_dp, [grad_shape, grad_shape...  1.04 us
    concatenate x1, other arithmetic, body(): tokens = jnp.concatenate([inputs, cotangent])  0.8 us
    pallas_call x1, Pallas kernels, body(): call(functools.partial(select_kernel, slots, *steps[0]), 1 + len(weights[...  0.75 us
    mul x1, other arithmetic, keep_factor(): return kept.astype(F32) * jnp.float32(8.0 / 7.0)  0.73 us
    unnamed x6, local copies, waits for them, and re-layouts  0.66 us
  transfers between devices with their start and end apart: 11, of which 6 were waited for; matrix products, arithmetic and copies ran while one was open for 7% of the time, Pallas kernels for 9%

profile of v8, /device:TPU:0, one launch (start us, length us, event | category | flops | bytes accessed | tf_op | source)
XLA Modules:
  0.0 25.2 jit_solution(18307512996294749766)
XLA Ops:
  0.6 0.0 copy-start.1
  0.7 3.0 %collective-permute-start = (bf16[1,4,128,128]{3,2,1,0:T(8,128)(2,1)}, bf16[1,4,128,128]{3,2,1,0:T(8,128)(2,1)S(1)}, u32[]{:S(2)}, u32[]{:S(2)}) collective-permute-start(bf16[1,4,128,128]{3,2,1,0:T(8,128)(2,1)} %refs_0_.5), channel_id=1, source_target_pairs={{0,8},{1,17},{2,10},{3,19},{4,12},{5,21},{6,14},{7,23},{8,0},{9,25... | collective-permute-start | bytes 393224 | tf_op jit(solution)/shard_map/ppermute | solution.py:215
  3.7 1.5 %collective-permute-start.1 = (bf16[1,4,128,128]{3,2,1,0:T(8,128)(2,1)}, bf16[1,4,128,128]{3,2,1,0:T(8,128)(2,1)S(1)}, u32[]{:S(2)}, u32[]{:S(2)}) collective-permute-start(bf16[1,4,128,128]{3,2,1,0:T(8,128)(2,1)} %refs_0_.4), channel_id=1, source_target_pairs={{0,16},{1,9},{2,18},{3,11},{4,20},{5,13},{6,22},{7,15},{8,24},{9,1... | collective-permute-start | bytes 393224 | tf_op jit(solution)/shard_map/ppermute | solution.py:215
  5.2 0.8 %pad_maximum_fusion.tokens = bf16[16,2560]{1,0:T(8,128)(2,1)S(1)} fusion(bf16[8,2560]{1,0:T(8,128)(2,1)} %param.8, bf16[8,2560]{1,0:T(8,128)(2,1)} %param.7), kind=kLoop, calls=%fused_computation | loop fusion | flops 163840 | bytes 163840 | tf_op jit(solution)/shard_map/concatenate | solution.py:257
  6.0 0.6 %collective-permute-start.2 = (bf16[4,128,128]{2,1,0:T(8,128)(2,1)S(1)}, bf16[4,128,128]{2,1,0:T(8,128)(2,1)S(1)}, u32[]{:S(2)}, u32[]{:S(2)}) collective-permute-start(bf16[4,128,128]{2,1,0:T(8,128)(2,1)S(1)} %bitcast.9), channel_id=1, source_target_pairs={{0,8},{1,17},{2,10},{3,19},{4,12},{5,21},{6,14},{7,23},{8,0},{9,25... | collective-permute-start | bytes 393224 | tf_op jit(solution)/shard_map/ppermute | solution.py:215
  6.6 0.1 collective-permute-start.3
  6.6 1.1 %collective-permute-done.refs_1_ = bf16[1,4,128,128]{3,2,1,0:T(8,128)(2,1)S(1)} collective-permute-done((bf16[1,4,128,128]{3,2,1,0:T(8,128)(2,1)}, bf16[1,4,128,128]{3,2,1,0:T(8,128)(2,1)S(1)}, u32[]{:S(2)}, u32[]{:S(2)}) %collective-permute-start) | collective-permute-done | bytes 131104 | tf_op jit(solution)/shard_map/ppermute | solution.py:215
  7.8 1.5 %collective-permute-start.4 = (bf16[1,4,128,128]{3,2,1,0:T(8,128)(2,1)S(1)}, bf16[1,4,128,128]{3,2,1,0:T(8,128)(2,1)S(1)}, u32[]{:S(2)}, u32[]{:S(2)}) collective-permute-start(bf16[1,4,128,128]{3,2,1,0:T(8,128)(2,1)S(1)} %collective-permute-done.refs_1_), channel_id=1, source_target_pairs={{0,16},{1,9},{2,18},{3,11},{4,20},{5,13},{6,22},{7,15},{8,24},{9,1... | collective-permute-start | bytes 393224 | tf_op jit(solution)/shard_map/ppermute | solution.py:215
  9.2 0.6 %collective-permute-done.1.refs_3_.refs_2_ = bf16[1,4,128,128]{3,2,1,0:T(8,128)(2,1)S(1)} collective-permute-done((bf16[1,4,128,128]{3,2,1,0:T(8,128)(2,1)}, bf16[1,4,128,128]{3,2,1,0:T(8,128)(2,1)S(1)}, u32[]{:S(2)}, u32[]{:S(2)}) %collective-permute-start.1) | collective-permute-done | bytes 131104 | tf_op jit(solution)/shard_map/ppermute | solution.py:215
  9.8 1.4 %collective-permute-start.5 = (bf16[1,4,128,128]{3,2,1,0:T(8,128)(2,1)S(1)}, bf16[1,4,128,128]{3,2,1,0:T(8,128)(2,1)S(1)}, u32[]{:S(2)}, u32[]{:S(2)}) collective-permute-start(bf16[1,4,128,128]{3,2,1,0:T(8,128)(2,1)S(1)} %collective-permute-done.1.refs_3_.refs_2_), channel_id=1, source_target_pairs={{0,8},{1,17},{2,10},{3,19},{4,12},{5,21},{6,14},{7,23},{8,0},{9,25... | collective-permute-start | bytes 393224 | tf_op jit(solution)/shard_map/ppermute | solution.py:215
  11.2 0.7 %fusion.4.keep = f32[8,128]{1,0:T(8,128)S(1)} fusion(s32[128]{0:T(128)S(1)} %add_multiply_fusion, s32[8]{0:T(128)} %param.13), kind=kLoop, calls=%fused_computation.14 | loop fusion | flops 12288 | bytes 4640 | tf_op jit(solution)/shard_map/mul | solution.py:30
  12.6 0.0 copy-start.2
  12.6 0.6 %copy-done.2 = s32[1,16]{1,0:T(1,128)S(1)} copy-done((s32[1,16]{1,0:T(1,128)S(1)}, s32[1,16]{1,0:T(1,128)}, u32[]{:S(2)}) %copy-start.2) | copy-done | bytes 88
  13.3 0.1 pad_add_fusion.listed
  13.4 0.8 %shard_map.102 = (bf16[16,2048]{1,0:T(8,128)(2,1)S(1)}, s32[8,128]{1,0:T(8,128)S(1)}, f32[16,128]{1,0:T(8,128)S(1)}) custom-call(s32[17]{0:T(128)S(1)} %pad_add_fusion.listed, bf16[16,2560]{1,0:T(8,128)(2,1)S(1)} %pad_maximum_fusion.tokens, bf16[1,4,128,128]{3,2,1,0:T(8,128)(2,1)S(1)} %copy-done.1, ...), custom_call_target="tpu_custom_call" | custom-call | tf_op jit(solution)/shard_map/pallas_call | solution.py:267
  14.1 0.0 collective-permute-done.3
  14.2 0.2 shard_map.103.sums
  14.3 0.3 %collective-permute-done.4.first.refs_3_ = bf16[1,4,128,128]{3,2,1,0:T(8,128)(2,1)S(1)} collective-permute-done((bf16[1,4,128,128]{3,2,1,0:T(8,128)(2,1)S(1)}, bf16[1,4,128,128]{3,2,1,0:T(8,128)(2,1)S(1)}, u32[]{:S(2)}, u32[]{:S(2)}) %collective-permute-start.4) | collective-permute-done | bytes 131104 | tf_op jit(solution)/shard_map/ppermute | solution.py:215
  14.6 0.3 %shard_map.104 = (f32[16,128]{1,0:T(8,128)S(1)}, f32[4,2,20,128]{3,2,1,0:T(8,128)S(1)}) custom-call(bf16[16,2048]{1,0:T(8,128)(2,1)S(1)} %get-tuple-element.24.picks, s32[8,128]{1,0:T(8,128)S(1)} %get-tuple-element.25.table, f32[8,128]{1,0:T(8,128)S(1)} %fusion.4.keep, f32[16,128]{1,0:T(8,128)S(1)} %shard_map.103.sums, ...), custom_call_target="tpu_custom_call" | custom-call | tf_op jit(solution)/shard_map/pallas_call | solution.py:289
  14.9 0.0 collective-permute-done.5.second
  14.9 0.4 %shard_map.105 = (bf16[4,40,128]{2,1,0:T(8,128)(2,1)S(1)}, f32[4,40,128]{2,1,0:T(8,128)S(1)}, bf16[16,640]{1,0:T(8,128)(2,1)S(1)}, bf16[16,640]{1,0:T(8,128)(2,1...) custom-call(bf16[16,2048]{1,0:T(8,128)(2,1)S(1)} %get-tuple-element.24.picks, ...), custom_call_target="tpu_custom_call" | custom-call | flops 6291456 | bytes 655360 | tf_op jit(solution)/shard_map/pallas_call | solution.py:296
  15.3 0.1 collective-permute-start.6
  15.4 1.6 %collective-permute-start.9 = (bf16[16,1280]{1,0:T(8,128)(2,1)S(1)}, bf16[16,1280]{1,0:T(8,128)(2,1)S(1)}, u32[]{:S(2)}, u32[]{:S(2)}) collective-permute-start(bf16[16,1280]{1,0:T(8,128)(2,1)S(1)} %pad_maximum_fusion.1), channel_id=1, source_target_pairs={{0,8},{1,17},{2,10},{3,19},{4,12},{5,21},{6,14},{7,23},{8,0},{9,25... | collective-permute-start | bytes 122888 | tf_op jit(solution)/shard_map/ppermute | solution.py:215
  17.0 2.2 %collective-permute-start.7 = (bf16[2,40,128]{2,1,0:T(8,128)(2,1)S(1)}, bf16[2,40,128]{2,1,0:T(8,128)(2,1)S(1)}, u32[]{:S(2)}, u32[]{:S(2)}) collective-permute-start(bf16[2,40,128]{2,1,0:T(8,128)(2,1)S(1)} %dynamic-slice_convert_fusion), channel_id=1, source_target_pairs={{0,5},{1,4},{2,7},{3,6},{4,1},{5,0},{6,3},{7,2},{8,13},{9,12},{10,... | collective-permute-start | bytes 61448 | tf_op jit(solution)/shard_map/ppermute | solution.py:201
  19.2 0.3 %collective-permute-done.9 = bf16[16,1280]{1,0:T(8,128)(2,1)S(1)} collective-permute-done((bf16[16,1280]{1,0:T(8,128)(2,1)S(1)}, bf16[16,1280]{1,0:T(8,128)(2,1)S(1)}, u32[]{:S(2)}, u32[]{:S(2)}) %collective-permute-start.9) | collective-permute-done | bytes 40992 | tf_op jit(solution)/shard_map/ppermute | solution.py:215
  19.5 1.4 %collective-permute-start.10 = (bf16[16,1280]{1,0:T(8,128)(2,1)S(1)}, bf16[16,1280]{1,0:T(8,128)(2,1)S(1)}, u32[]{:S(2)}, u32[]{:S(2)}) collective-permute-start(bf16[16,1280]{1,0:T(8,128)(2,1)S(1)} %pad_maximum_fusion.2), channel_id=1, source_target_pairs={{0,16},{1,9},{2,18},{3,11},{4,20},{5,13},{6,22},{7,15},{8,24},{9,1... | collective-permute-start | bytes 122888 | tf_op jit(solution)/shard_map/ppermute | solution.py:215
  20.9 0.3 %collective-permute-done.7 = bf16[2,40,128]{2,1,0:T(8,128)(2,1)S(1)} collective-permute-done((bf16[2,40,128]{2,1,0:T(8,128)(2,1)S(1)}, bf16[2,40,128]{2,1,0:T(8,128)(2,1)S(1)}, u32[]{:S(2)}, u32[]{:S(2)}) %collective-permute-start.7) | collective-permute-done | bytes 20512 | tf_op jit(solution)/shard_map/ppermute | solution.py:201
  21.2 1.4 %collective-permute-start.8 = (bf16[1,40,128]{2,1,0:T(8,128)(2,1)S(1)}, bf16[1,40,128]{2,1,0:T(8,128)(2,1)S(1)}, u32[]{:S(2)}, u32[]{:S(2)}) collective-permute-start(bf16[1,40,128]{2,1,0:T(8,128)(2,1)S(1)} %dynamic-slice_convert_fusion.1), channel_id=1, source_target_pairs={{0,3},{1,2},{2,1},{3,0},{4,7},{5,6},{6,5},{7,4},{8,11},{9,10},{10,... | collective-permute-start | bytes 30728 | tf_op jit(solution)/shard_map/ppermute | solution.py:201
  22.6 1.0 %collective-permute-done.10 = bf16[16,1280]{1,0:T(8,128)(2,1)S(1)} collective-permute-done((bf16[16,1280]{1,0:T(8,128)(2,1)S(1)}, bf16[16,1280]{1,0:T(8,128)(2,1)S(1)}, u32[]{:S(2)}, u32[]{:S(2)}) %collective-permute-start.10) | collective-permute-done | bytes 40992 | tf_op jit(solution)/shard_map/ppermute | solution.py:215
  23.6 1.0 %shard_map.106 = (f32[1,4,128,128]{3,2,1,0:T(8,128)}, f32[1,4,128,128]{3,2,1,0:T(8,128)}, f32[8,128]{1,0:T(8,128)S(1)}) custom-call(bf16[16,640]{1,0:T(8,128)(2,1)S(1)} %get-tuple-element.33.refs_0_, bf16[16,640]{1,0:T(8,128)(2,1)S(1)} %get-tuple-element.45.refs_1_, bf16[16,640]{1,0:T(8,128)(2,1)S(1)} %get-tuple-element.43.refs_2_, ...), custom_call_target="tpu_custom_call" | custom-call | flops 8388608 | bytes 524288 | tf_op jit(solution)/shard_map/pallas_call | solution.py:319
  24.6 0.0 collective-permute-done.8.got
  24.6 0.6 %shard_map.107 = (bf16[1,2560]{1,0:T(2,128)(2,1)}, bf16[1,2560]{1,0:T(2,128)(2,1)}) custom-call(f32[1,40,128]{2,1,0:T(8,128)S(1)} %constant_dynamic-slice_fusion.kept, bf16[1,40,128]{2,1,0:T(8,128)(2,1)S(1)} %collective-permute-done.8.got, f32[8,128]{1,0:T(8,128)S(1)} %get-tuple-element.37.order), custom_call_target="tpu_custom_call" | custom-call | flops 5120 | bytes 40960 | tf_op jit(solution)/shard_map/pallas_call | solution.py:327
  (15 shorter events, 0.1 us)
Async XLA Ops:
  0.6 5.4 %copy-start = (bf16[1,4,128,128]{3,2,1,0:T(8,128)(2,1)S(1)}, bf16[1,4,128,128]{3,2,1,0:T(8,128)(2,1)}, u32[]{:S(2)}) copy-start(bf16[1,4,128,128]{3,2,1,0:T(8,128)(2,1)} %refs_0_.4) | copy-start | bytes 393220
  0.6 12.7 %copy-start.1 = (bf16[1,4,128,128]{3,2,1,0:T(8,128)(2,1)S(1)}, bf16[1,4,128,128]{3,2,1,0:T(8,128)(2,1)}, u32[]{:S(2)}) copy-start(bf16[1,4,128,128]{3,2,1,0:T(8,128)(2,1)} %refs_0_.5) | copy-start | bytes 393220
  0.7 7.1 %collective-permute-start = (bf16[1,4,128,128]{3,2,1,0:T(8,128)(2,1)}, bf16[1,4,128,128]{3,2,1,0:T(8,128)(2,1)S(1)}, u32[]{:S(2)}, u32[]{:S(2)}) collective-permute-start(bf16[1,4,128,128]{3,2,1,0:T(8,128)(2,1)} %refs_0_.5), channel_id=1, source_target_pairs={{0,8},{1,17},{2,10},{3,19},{4,12},{5,21},{6,14},{7,23},{8,0},{9,25... | collective-permute-start | bytes 393224 | tf_op jit(solution)/shard_map/ppermute | solution.py:215
  3.7 6.2 %collective-permute-start.1 = (bf16[1,4,128,128]{3,2,1,0:T(8,128)(2,1)}, bf16[1,4,128,128]{3,2,1,0:T(8,128)(2,1)S(1)}, u32[]{:S(2)}, u32[]{:S(2)}) collective-permute-start(bf16[1,4,128,128]{3,2,1,0:T(8,128)(2,1)} %refs_0_.4), channel_id=1, source_target_pairs={{0,16},{1,9},{2,18},{3,11},{4,20},{5,13},{6,22},{7,15},{8,24},{9,1... | collective-permute-start | bytes 393224 | tf_op jit(solution)/shard_map/ppermute | solution.py:215
  6.0 8.1 %collective-permute-start.2 = (bf16[4,128,128]{2,1,0:T(8,128)(2,1)S(1)}, bf16[4,128,128]{2,1,0:T(8,128)(2,1)S(1)}, u32[]{:S(2)}, u32[]{:S(2)}) collective-permute-start(bf16[4,128,128]{2,1,0:T(8,128)(2,1)S(1)} %bitcast.9), channel_id=1, source_target_pairs={{0,8},{1,17},{2,10},{3,19},{4,12},{5,21},{6,14},{7,23},{8,0},{9,25... | collective-permute-start | bytes 393224 | tf_op jit(solution)/shard_map/ppermute | solution.py:215
  6.6 7.6 %collective-permute-start.3 = (bf16[4,128,128]{2,1,0:T(8,128)(2,1)}, bf16[4,128,128]{2,1,0:T(8,128)(2,1)S(1)}, u32[]{:S(2)}, u32[]{:S(2)}) collective-permute-start(bf16[4,128,128]{2,1,0:T(8,128)(2,1)} %bitcast.10), channel_id=1, source_target_pairs={{0,16},{1,9},{2,18},{3,11},{4,20},{5,13},{6,22},{7,15},{8,24},{9,1... | collective-permute-start | bytes 393224 | tf_op jit(solution)/shard_map/ppermute | solution.py:215
  7.8 6.8 %collective-permute-start.4 = (bf16[1,4,128,128]{3,2,1,0:T(8,128)(2,1)S(1)}, bf16[1,4,128,128]{3,2,1,0:T(8,128)(2,1)S(1)}, u32[]{:S(2)}, u32[]{:S(2)}) collective-permute-start(bf16[1,4,128,128]{3,2,1,0:T(8,128)(2,1)S(1)} %collective-permute-done.refs_1_), channel_id=1, source_target_pairs={{0,16},{1,9},{2,18},{3,11},{4,20},{5,13},{6,22},{7,15},{8,24},{9,1... | collective-permute-start | bytes 393224 | tf_op jit(solution)/shard_map/ppermute | solution.py:215
  9.8 5.1 %collective-permute-start.5 = (bf16[1,4,128,128]{3,2,1,0:T(8,128)(2,1)S(1)}, bf16[1,4,128,128]{3,2,1,0:T(8,128)(2,1)S(1)}, u32[]{:S(2)}, u32[]{:S(2)}) collective-permute-start(bf16[1,4,128,128]{3,2,1,0:T(8,128)(2,1)S(1)} %collective-permute-done.1.refs_3_.refs_2_), channel_id=1, source_target_pairs={{0,8},{1,17},{2,10},{3,19},{4,12},{5,21},{6,14},{7,23},{8,0},{9,25... | collective-permute-start | bytes 393224 | tf_op jit(solution)/shard_map/ppermute | solution.py:215
  12.6 0.7 %copy-start.2 = (s32[1,16]{1,0:T(1,128)S(1)}, s32[1,16]{1,0:T(1,128)}, u32[]{:S(2)}) copy-start(s32[1,16]{1,0:T(1,128)} %param.11) | copy-start | bytes 196
  15.3 1.7 %collective-permute-start.6 = (bf16[4,40,128]{2,1,0:T(8,128)(2,1)S(1)}, bf16[4,40,128]{2,1,0:T(8,128)(2,1)S(1)}, u32[]{:S(2)}, u32[]{:S(2)}) collective-permute-start(bf16[4,40,128]{2,1,0:T(8,128)(2,1)S(1)} %get-tuple-element.32), channel_id=1, source_target_pairs={{0,1},{1,0},{2,3},{3,2},{4,5},{5,4},{6,7},{7,6},{8,9},{9,8},{10,11... | collective-permute-start | bytes 122888 | tf_op jit(solution)/shard_map/ppermute | solution.py:201
  15.4 4.1 %collective-permute-start.9 = (bf16[16,1280]{1,0:T(8,128)(2,1)S(1)}, bf16[16,1280]{1,0:T(8,128)(2,1)S(1)}, u32[]{:S(2)}, u32[]{:S(2)}) collective-permute-start(bf16[16,1280]{1,0:T(8,128)(2,1)S(1)} %pad_maximum_fusion.1), channel_id=1, source_target_pairs={{0,8},{1,17},{2,10},{3,19},{4,12},{5,21},{6,14},{7,23},{8,0},{9,25... | collective-permute-start | bytes 122888 | tf_op jit(solution)/shard_map/ppermute | solution.py:215
  17.0 4.2 %collective-permute-start.7 = (bf16[2,40,128]{2,1,0:T(8,128)(2,1)S(1)}, bf16[2,40,128]{2,1,0:T(8,128)(2,1)S(1)}, u32[]{:S(2)}, u32[]{:S(2)}) collective-permute-start(bf16[2,40,128]{2,1,0:T(8,128)(2,1)S(1)} %dynamic-slice_convert_fusion), channel_id=1, source_target_pairs={{0,5},{1,4},{2,7},{3,6},{4,1},{5,0},{6,3},{7,2},{8,13},{9,12},{10,... | collective-permute-start | bytes 61448 | tf_op jit(solution)/shard_map/ppermute | solution.py:201
  19.5 4.1 %collective-permute-start.10 = (bf16[16,1280]{1,0:T(8,128)(2,1)S(1)}, bf16[16,1280]{1,0:T(8,128)(2,1)S(1)}, u32[]{:S(2)}, u32[]{:S(2)}) collective-permute-start(bf16[16,1280]{1,0:T(8,128)(2,1)S(1)} %pad_maximum_fusion.2), channel_id=1, source_target_pairs={{0,16},{1,9},{2,18},{3,11},{4,20},{5,13},{6,22},{7,15},{8,24},{9,1... | collective-permute-start | bytes 122888 | tf_op jit(solution)/shard_map/ppermute | solution.py:215
  21.2 3.4 %collective-permute-start.8 = (bf16[1,40,128]{2,1,0:T(8,128)(2,1)S(1)}, bf16[1,40,128]{2,1,0:T(8,128)(2,1)S(1)}, u32[]{:S(2)}, u32[]{:S(2)}) collective-permute-start(bf16[1,40,128]{2,1,0:T(8,128)(2,1)S(1)} %dynamic-slice_convert_fusion.1), channel_id=1, source_target_pairs={{0,3},{1,2},{2,1},{3,0},{4,7},{5,6},{6,5},{7,4},{8,11},{9,10},{10,... | collective-permute-start | bytes 30728 | tf_op jit(solution)/shard_map/ppermute | solution.py:201

commit v9 on v6

--- a/solution.py
+++ b/solution.py
@@ -243,7 +243,9 @@
     piece_bytes = slots * BS * BS * 2
 
     bits = [1 << i for i in range(n_dp.bit_length() - 1)]
-    firsts, seconds = gather([w_in, w_out], [w_in[0], w_out[0]], n_dp, n_mp, [bits, bits[::-1]])
+    tokens = jnp.concatenate([inputs, cotangent])
+    *held, tokens = lax.optimization_barrier((w_in[0], w_out[0], tokens))
+    firsts, seconds = gather([w_in, w_out], held, n_dp, n_mp, [bits, bits[::-1]])
 
     rank = lax.axis_index("mp")
     keep = keep_factor(drop_seeds, rank * BS)
@@ -263,7 +265,7 @@
         0,
         0,
         scalars=1,
-    )(jnp.concatenate([block_index[0], block_count]), jnp.concatenate([inputs, cotangent]), *weights[0])
+    )(jnp.concatenate([block_index[0], block_count]), tokens, *weights[0])
     sums = call(
         functools.partial(partial_kernel, slots, *steps[1]),
         2 + len(weights[1]),

time: 25.6 us -> 25.4 us (level)
  waiting for transfers between devices: 5.2 us -> 2.73 us
  starting transfers between devices: 14 us -> 15.6 us
  other arithmetic: 1.07 us -> 1.65 us
    ppermute x8, waiting for transfers between devices: 3.9 us -> 2.43 us  [cross(): return lax.ppermute(value, ('dp', 'mp'), pairs)]
    ppermute x8, starting transfers between devices: 10.7 us -> 12 us  [cross(): return lax.ppermute(value, ('dp', 'mp'), pairs)]
    ppermute x3, waiting for transfers between devices: 1.31 us -> 0.31 us  [flip(): lax.ppermute(value, axis, [(i, i ^ mask) for i in range(size)])]
    mul x1, other arithmetic: 0.08 us -> 0.73 us  [keep_factor(): return kept.astype(F32) * jnp.float32(8.0 / 7.0)]
    ppermute x3, starting transfers between devices: 3.3 us -> 3.66 us  [flip(): lax.ppermute(value, axis, [(i, i ^ mask) for i in range(size)])]
    unnamed x8 -> x6, local copies, waits for them, and re-layouts: 0.66 us -> 0.66 us
  transfers between devices with their start and end apart: 11 -> 11, of which waited for: 7 -> 4; matrix products, arithmetic and copies ran while one was open for 4% -> 7% of each run, Pallas kernels for 8% -> 8%
where the time goes in v9:
time: 25.4 us; the launch traced here: 25.2 us
  starting transfers between devices  15.6 us (61%)
  Pallas kernels  3.08 us (12%)
  waiting for transfers between devices  2.73 us (11%)
  other arithmetic  1.65 us (6%)
  between operations  1.4 us (6%)
  local copies, waits for them, and re-layouts  0.69 us (3%)
    ppermute x8, starting transfers between devices, cross(): return lax.ppermute(value, ('dp', 'mp'), pairs)  12 us
    ppermute x3, starting transfers between devices, flip(): lax.ppermute(value, axis, [(i, i ^ mask) for i in range(size)])  3.66 us
    ppermute x8, waiting for transfers between devices, cross(): return lax.ppermute(value, ('dp', 'mp'), pairs)  2.43 us
    pallas_call x1, Pallas kernels, body(): call(functools.partial(grad_kernel, slots), n_dp, [grad_shape, grad_shape...  1.04 us
    concatenate x1, other arithmetic, body(): tokens = jnp.concatenate([inputs, cotangent])  0.8 us
    pallas_call x1, Pallas kernels, body(): call(functools.partial(select_kernel, slots, *steps[0]), 1 + len(weights[...  0.75 us
    mul x1, other arithmetic, keep_factor(): return kept.astype(F32) * jnp.float32(8.0 / 7.0)  0.73 us
    unnamed x6, local copies, waits for them, and re-layouts  0.66 us
  transfers between devices with their start and end apart: 11, of which 4 were waited for; matrix products, arithmetic and copies ran while one was open for 7% of the time, Pallas kernels for 8%

profile of v9, /device:TPU:0, one launch (start us, length us, event | category | flops | bytes accessed | tf_op | source)
XLA Modules:
  0.0 25.2 jit_solution(11669048538421458528)
XLA Ops:
  0.6 0.0 copy-start.1
  0.7 3.0 %collective-permute-start = (bf16[1,4,128,128]{3,2,1,0:T(8,128)(2,1)}, bf16[1,4,128,128]{3,2,1,0:T(8,128)(2,1)S(1)}, u32[]{:S(2)}, u32[]{:S(2)}) collective-permute-start(bf16[1,4,128,128]{3,2,1,0:T(8,128)(2,1)} %refs_0_.3), channel_id=1, source_target_pairs={{0,8},{1,17},{2,10},{3,19},{4,12},{5,21},{6,14},{7,23},{8,0},{9,25... | collective-permute-start | bytes 393224 | tf_op jit(solution)/shard_map/ppermute | solution.py:204
  3.7 1.5 %collective-permute-start.1 = (bf16[1,4,128,128]{3,2,1,0:T(8,128)(2,1)}, bf16[1,4,128,128]{3,2,1,0:T(8,128)(2,1)S(1)}, u32[]{:S(2)}, u32[]{:S(2)}) collective-permute-start(bf16[1,4,128,128]{3,2,1,0:T(8,128)(2,1)} %refs_4_.1), channel_id=1, source_target_pairs={{0,16},{1,9},{2,18},{3,11},{4,20},{5,13},{6,22},{7,15},{8,24},{9,1... | collective-permute-start | bytes 393224 | tf_op jit(solution)/shard_map/ppermute | solution.py:204
  5.2 0.8 %pad_maximum_fusion.tokens = bf16[16,2560]{1,0:T(8,128)(2,1)S(1)} fusion(bf16[8,2560]{1,0:T(8,128)(2,1)} %param.8, bf16[8,2560]{1,0:T(8,128)(2,1)} %param.7), kind=kLoop, calls=%fused_computation | loop fusion | flops 163840 | bytes 163840 | tf_op jit(solution)/shard_map/concatenate | solution.py:246
  6.0 0.5 %collective-permute-start.2 = (bf16[4,128,128]{2,1,0:T(8,128)(2,1)}, bf16[4,128,128]{2,1,0:T(8,128)(2,1)S(1)}, u32[]{:S(2)}, u32[]{:S(2)}) collective-permute-start(bf16[4,128,128]{2,1,0:T(8,128)(2,1)} %bitcast.10), channel_id=1, source_target_pairs={{0,8},{1,17},{2,10},{3,19},{4,12},{5,21},{6,14},{7,23},{8,0},{9,25... | collective-permute-start | bytes 393224 | tf_op jit(solution)/shard_map/ppermute | solution.py:204
  6.5 0.0 collective-permute-start.3
  6.6 1.2 %collective-permute-done.refs_1_ = bf16[1,4,128,128]{3,2,1,0:T(8,128)(2,1)S(1)} collective-permute-done((bf16[1,4,128,128]{3,2,1,0:T(8,128)(2,1)}, bf16[1,4,128,128]{3,2,1,0:T(8,128)(2,1)S(1)}, u32[]{:S(2)}, u32[]{:S(2)}) %collective-permute-start) | collective-permute-done | bytes 131104 | tf_op jit(solution)/shard_map/ppermute | solution.py:204
  7.8 1.5 %collective-permute-start.4 = (bf16[1,4,128,128]{3,2,1,0:T(8,128)(2,1)S(1)}, bf16[1,4,128,128]{3,2,1,0:T(8,128)(2,1)S(1)}, u32[]{:S(2)}, u32[]{:S(2)}) collective-permute-start(bf16[1,4,128,128]{3,2,1,0:T(8,128)(2,1)S(1)} %collective-permute-done.refs_1_), channel_id=1, source_target_pairs={{0,16},{1,9},{2,18},{3,11},{4,20},{5,13},{6,22},{7,15},{8,24},{9,1... | collective-permute-start | bytes 393224 | tf_op jit(solution)/shard_map/ppermute | solution.py:204
  9.2 0.5 %collective-permute-done.1.refs_3_.refs_6_ = bf16[1,4,128,128]{3,2,1,0:T(8,128)(2,1)S(1)} collective-permute-done((bf16[1,4,128,128]{3,2,1,0:T(8,128)(2,1)}, bf16[1,4,128,128]{3,2,1,0:T(8,128)(2,1)S(1)}, u32[]{:S(2)}, u32[]{:S(2)}) %collective-permute-start.1) | collective-permute-done | bytes 131104 | tf_op jit(solution)/shard_map/ppermute | solution.py:204
  9.7 1.9 %collective-permute-start.5 = (bf16[1,4,128,128]{3,2,1,0:T(8,128)(2,1)S(1)}, bf16[1,4,128,128]{3,2,1,0:T(8,128)(2,1)S(1)}, u32[]{:S(2)}, u32[]{:S(2)}) collective-permute-start(bf16[1,4,128,128]{3,2,1,0:T(8,128)(2,1)S(1)} %collective-permute-done.1.refs_3_.refs_6_), channel_id=1, source_target_pairs={{0,8},{1,17},{2,10},{3,19},{4,12},{5,21},{6,14},{7,23},{8,0},{9,25... | collective-permute-start | bytes 393224 | tf_op jit(solution)/shard_map/ppermute | solution.py:204
  11.5 0.7 %fusion.4.keep = f32[8,128]{1,0:T(8,128)S(1)} fusion(s32[128]{0:T(128)S(1)} %add_multiply_fusion, s32[8]{0:T(128)} %param.13), kind=kLoop, calls=%fused_computation.14 | loop fusion | flops 12288 | bytes 4640 | tf_op jit(solution)/shard_map/mul | solution.py:30
  12.9 0.0 copy-start.2
  13.0 0.6 %copy-done.2 = s32[1,16]{1,0:T(1,128)S(1)} copy-done((s32[1,16]{1,0:T(1,128)S(1)}, s32[1,16]{1,0:T(1,128)}, u32[]{:S(2)}) %copy-start.2) | copy-done | bytes 88
  13.6 0.1 pad_add_fusion.listed
  13.7 0.8 %shard_map.102 = (bf16[16,2048]{1,0:T(8,128)(2,1)S(1)}, s32[8,128]{1,0:T(8,128)S(1)}, f32[16,128]{1,0:T(8,128)S(1)}) custom-call(s32[17]{0:T(128)S(1)} %pad_add_fusion.listed, bf16[16,2560]{1,0:T(8,128)(2,1)S(1)} %pad_maximum_fusion.tokens, bf16[1,4,128,128]{3,2,1,0:T(8,128)(2,1)S(1)} %copy-done, bf16[1,4,128,128]{3,2,1,0:T(8,128)(2,1)S(1)} %collective-permute-done.refs_1_, ...), custom_call_target="tpu_custom_call" | custom-call | tf_op jit(solution)/shard_map/pallas_call | solution.py:257
  14.4 0.0 collective-permute-done.2
  14.4 0.0 collective-permute-done.3
  14.5 0.2 shard_map.103.sums
  14.6 0.0 collective-permute-done.4.refs_3_
  14.7 0.5 %shard_map.104 = (bf16[4,40,128]{2,1,0:T(8,128)(2,1)S(1)}, f32[4,40,128]{2,1,0:T(8,128)S(1)}, bf16[16,640]{1,0:T(8,128)(2,1)S(1)}, bf16[16,640]{1,0:T(8,128)(2,1...) custom-call(bf16[16,2048]{1,0:T(8,128)(2,1)S(1)} %get-tuple-element.22.picks, ...), custom_call_target="tpu_custom_call" | custom-call | flops 10485760 | bytes 1048576 | tf_op jit(solution)/shard_map/pallas_call | solution.py:279
  15.2 0.1 collective-permute-start.6
  15.3 1.9 %collective-permute-start.9 = (bf16[16,1280]{1,0:T(8,128)(2,1)S(1)}, bf16[16,1280]{1,0:T(8,128)(2,1)S(1)}, u32[]{:S(2)}, u32[]{:S(2)}) collective-permute-start(bf16[16,1280]{1,0:T(8,128)(2,1)S(1)} %pad_maximum_fusion.1), channel_id=1, source_target_pairs={{0,8},{1,17},{2,10},{3,19},{4,12},{5,21},{6,14},{7,23},{8,0},{9,25... | collective-permute-start | bytes 122888 | tf_op jit(solution)/shard_map/ppermute | solution.py:204
  17.2 0.0 collective-permute-done.6
  17.2 2.2 %collective-permute-start.7 = (bf16[2,40,128]{2,1,0:T(8,128)(2,1)S(1)}, bf16[2,40,128]{2,1,0:T(8,128)(2,1)S(1)}, u32[]{:S(2)}, u32[]{:S(2)}) collective-permute-start(bf16[2,40,128]{2,1,0:T(8,128)(2,1)S(1)} %dynamic-slice_convert_fusion), channel_id=1, source_target_pairs={{0,5},{1,4},{2,7},{3,6},{4,1},{5,0},{6,3},{7,2},{8,13},{9,12},{10,... | collective-permute-start | bytes 61448 | tf_op jit(solution)/shard_map/ppermute | solution.py:190
  19.5 0.0 collective-permute-done.9
  19.5 1.6 %collective-permute-start.10 = (bf16[16,1280]{1,0:T(8,128)(2,1)S(1)}, bf16[16,1280]{1,0:T(8,128)(2,1)S(1)}, u32[]{:S(2)}, u32[]{:S(2)}) collective-permute-start(bf16[16,1280]{1,0:T(8,128)(2,1)S(1)} %pad_maximum_fusion.2), channel_id=1, source_target_pairs={{0,16},{1,9},{2,18},{3,11},{4,20},{5,13},{6,22},{7,15},{8,24},{9,1... | collective-permute-start | bytes 122888 | tf_op jit(solution)/shard_map/ppermute | solution.py:204
  21.1 0.3 %collective-permute-done.7 = bf16[2,40,128]{2,1,0:T(8,128)(2,1)S(1)} collective-permute-done((bf16[2,40,128]{2,1,0:T(8,128)(2,1)S(1)}, bf16[2,40,128]{2,1,0:T(8,128)(2,1)S(1)}, u32[]{:S(2)}, u32[]{:S(2)}) %collective-permute-start.7) | collective-permute-done | bytes 20512 | tf_op jit(solution)/shard_map/ppermute | solution.py:190
  21.4 1.4 %collective-permute-start.8 = (bf16[1,40,128]{2,1,0:T(8,128)(2,1)S(1)}, bf16[1,40,128]{2,1,0:T(8,128)(2,1)S(1)}, u32[]{:S(2)}, u32[]{:S(2)}) collective-permute-start(bf16[1,40,128]{2,1,0:T(8,128)(2,1)S(1)} %dynamic-slice_convert_fusion.1), channel_id=1, source_target_pairs={{0,3},{1,2},{2,1},{3,0},{4,7},{5,6},{6,5},{7,4},{8,11},{9,10},{10,... | collective-permute-start | bytes 30728 | tf_op jit(solution)/shard_map/ppermute | solution.py:190
  22.8 0.8 %collective-permute-done.10 = bf16[16,1280]{1,0:T(8,128)(2,1)S(1)} collective-permute-done((bf16[16,1280]{1,0:T(8,128)(2,1)S(1)}, bf16[16,1280]{1,0:T(8,128)(2,1)S(1)}, u32[]{:S(2)}, u32[]{:S(2)}) %collective-permute-start.10) | collective-permute-done | bytes 40992 | tf_op jit(solution)/shard_map/ppermute | solution.py:204
  23.5 1.0 %shard_map.105 = (f32[1,4,128,128]{3,2,1,0:T(8,128)}, f32[1,4,128,128]{3,2,1,0:T(8,128)}, f32[8,128]{1,0:T(8,128)S(1)}) custom-call(bf16[16,640]{1,0:T(8,128)(2,1)S(1)} %get-tuple-element.29.refs_0_, bf16[16,640]{1,0:T(8,128)(2,1)S(1)} %get-tuple-element.41.refs_1_, bf16[16,640]{1,0:T(8,128)(2,1)S(1)} %get-tuple-element.39.refs_2_, ...), custom_call_target="tpu_custom_call" | custom-call | flops 8388608 | bytes 524288 | tf_op jit(solution)/shard_map/pallas_call | solution.py:302
  24.6 0.0 collective-permute-done.8.got
  24.6 0.6 %shard_map.106 = (bf16[1,2560]{1,0:T(2,128)(2,1)}, bf16[1,2560]{1,0:T(2,128)(2,1)}) custom-call(f32[1,40,128]{2,1,0:T(8,128)S(1)} %constant_dynamic-slice_fusion.kept, bf16[1,40,128]{2,1,0:T(8,128)(2,1)S(1)} %collective-permute-done.8.got, f32[8,128]{1,0:T(8,128)S(1)} %get-tuple-element.33.order), custom_call_target="tpu_custom_call" | custom-call | flops 5120 | bytes 40960 | tf_op jit(solution)/shard_map/pallas_call | solution.py:310
  (14 shorter events, 0.1 us)
Async XLA Ops:
  0.6 5.9 %copy-start = (bf16[1,4,128,128]{3,2,1,0:T(8,128)(2,1)S(1)}, bf16[1,4,128,128]{3,2,1,0:T(8,128)(2,1)}, u32[]{:S(2)}) copy-start(bf16[1,4,128,128]{3,2,1,0:T(8,128)(2,1)} %refs_0_.3) | copy-start | bytes 393220
  0.6 13.0 %copy-start.1 = (bf16[1,4,128,128]{3,2,1,0:T(8,128)(2,1)S(1)}, bf16[1,4,128,128]{3,2,1,0:T(8,128)(2,1)}, u32[]{:S(2)}) copy-start(bf16[1,4,128,128]{3,2,1,0:T(8,128)(2,1)} %refs_4_.1) | copy-start | bytes 393220
  0.7 7.1 %collective-permute-start = (bf16[1,4,128,128]{3,2,1,0:T(8,128)(2,1)}, bf16[1,4,128,128]{3,2,1,0:T(8,128)(2,1)S(1)}, u32[]{:S(2)}, u32[]{:S(2)}) collective-permute-start(bf16[1,4,128,128]{3,2,1,0:T(8,128)(2,1)} %refs_0_.3), channel_id=1, source_target_pairs={{0,8},{1,17},{2,10},{3,19},{4,12},{5,21},{6,14},{7,23},{8,0},{9,25... | collective-permute-start | bytes 393224 | tf_op jit(solution)/shard_map/ppermute | solution.py:204
  3.7 6.0 %collective-permute-start.1 = (bf16[1,4,128,128]{3,2,1,0:T(8,128)(2,1)}, bf16[1,4,128,128]{3,2,1,0:T(8,128)(2,1)S(1)}, u32[]{:S(2)}, u32[]{:S(2)}) collective-permute-start(bf16[1,4,128,128]{3,2,1,0:T(8,128)(2,1)} %refs_4_.1), channel_id=1, source_target_pairs={{0,16},{1,9},{2,18},{3,11},{4,20},{5,13},{6,22},{7,15},{8,24},{9,1... | collective-permute-start | bytes 393224 | tf_op jit(solution)/shard_map/ppermute | solution.py:204
  6.0 8.5 %collective-permute-start.2 = (bf16[4,128,128]{2,1,0:T(8,128)(2,1)}, bf16[4,128,128]{2,1,0:T(8,128)(2,1)S(1)}, u32[]{:S(2)}, u32[]{:S(2)}) collective-permute-start(bf16[4,128,128]{2,1,0:T(8,128)(2,1)} %bitcast.10), channel_id=1, source_target_pairs={{0,8},{1,17},{2,10},{3,19},{4,12},{5,21},{6,14},{7,23},{8,0},{9,25... | collective-permute-start | bytes 393224 | tf_op jit(solution)/shard_map/ppermute | solution.py:204
  6.5 8.0 %collective-permute-start.3 = (bf16[4,128,128]{2,1,0:T(8,128)(2,1)S(1)}, bf16[4,128,128]{2,1,0:T(8,128)(2,1)S(1)}, u32[]{:S(2)}, u32[]{:S(2)}) collective-permute-start(bf16[4,128,128]{2,1,0:T(8,128)(2,1)S(1)} %bitcast.9), channel_id=1, source_target_pairs={{0,16},{1,9},{2,18},{3,11},{4,20},{5,13},{6,22},{7,15},{8,24},{9,1... | collective-permute-start | bytes 393224 | tf_op jit(solution)/shard_map/ppermute | solution.py:204
  7.8 6.9 %collective-permute-start.4 = (bf16[1,4,128,128]{3,2,1,0:T(8,128)(2,1)S(1)}, bf16[1,4,128,128]{3,2,1,0:T(8,128)(2,1)S(1)}, u32[]{:S(2)}, u32[]{:S(2)}) collective-permute-start(bf16[1,4,128,128]{3,2,1,0:T(8,128)(2,1)S(1)} %collective-permute-done.refs_1_), channel_id=1, source_target_pairs={{0,16},{1,9},{2,18},{3,11},{4,20},{5,13},{6,22},{7,15},{8,24},{9,1... | collective-permute-start | bytes 393224 | tf_op jit(solution)/shard_map/ppermute | solution.py:204
  9.7 5.0 %collective-permute-start.5 = (bf16[1,4,128,128]{3,2,1,0:T(8,128)(2,1)S(1)}, bf16[1,4,128,128]{3,2,1,0:T(8,128)(2,1)S(1)}, u32[]{:S(2)}, u32[]{:S(2)}) collective-permute-start(bf16[1,4,128,128]{3,2,1,0:T(8,128)(2,1)S(1)} %collective-permute-done.1.refs_3_.refs_6_), channel_id=1, source_target_pairs={{0,8},{1,17},{2,10},{3,19},{4,12},{5,21},{6,14},{7,23},{8,0},{9,25... | collective-permute-start | bytes 393224 | tf_op jit(solution)/shard_map/ppermute | solution.py:204
  12.9 0.7 %copy-start.2 = (s32[1,16]{1,0:T(1,128)S(1)}, s32[1,16]{1,0:T(1,128)}, u32[]{:S(2)}) copy-start(s32[1,16]{1,0:T(1,128)} %param.11) | copy-start | bytes 196
  15.2 2.0 %collective-permute-start.6 = (bf16[4,40,128]{2,1,0:T(8,128)(2,1)S(1)}, bf16[4,40,128]{2,1,0:T(8,128)(2,1)S(1)}, u32[]{:S(2)}, u32[]{:S(2)}) collective-permute-start(bf16[4,40,128]{2,1,0:T(8,128)(2,1)S(1)} %get-tuple-element.28), channel_id=1, source_target_pairs={{0,1},{1,0},{2,3},{3,2},{4,5},{5,4},{6,7},{7,6},{8,9},{9,8},{10,11... | collective-permute-start | bytes 122888 | tf_op jit(solution)/shard_map/ppermute | solution.py:190
  15.3 4.2 %collective-permute-start.9 = (bf16[16,1280]{1,0:T(8,128)(2,1)S(1)}, bf16[16,1280]{1,0:T(8,128)(2,1)S(1)}, u32[]{:S(2)}, u32[]{:S(2)}) collective-permute-start(bf16[16,1280]{1,0:T(8,128)(2,1)S(1)} %pad_maximum_fusion.1), channel_id=1, source_target_pairs={{0,8},{1,17},{2,10},{3,19},{4,12},{5,21},{6,14},{7,23},{8,0},{9,25... | collective-permute-start | bytes 122888 | tf_op jit(solution)/shard_map/ppermute | solution.py:204
  17.2 4.2 %collective-permute-start.7 = (bf16[2,40,128]{2,1,0:T(8,128)(2,1)S(1)}, bf16[2,40,128]{2,1,0:T(8,128)(2,1)S(1)}, u32[]{:S(2)}, u32[]{:S(2)}) collective-permute-start(bf16[2,40,128]{2,1,0:T(8,128)(2,1)S(1)} %dynamic-slice_convert_fusion), channel_id=1, source_target_pairs={{0,5},{1,4},{2,7},{3,6},{4,1},{5,0},{6,3},{7,2},{8,13},{9,12},{10,... | collective-permute-start | bytes 61448 | tf_op jit(solution)/shard_map/ppermute | solution.py:190
  19.5 4.1 %collective-permute-start.10 = (bf16[16,1280]{1,0:T(8,128)(2,1)S(1)}, bf16[16,1280]{1,0:T(8,128)(2,1)S(1)}, u32[]{:S(2)}, u32[]{:S(2)}) collective-permute-start(bf16[16,1280]{1,0:T(8,128)(2,1)S(1)} %pad_maximum_fusion.2), channel_id=1, source_target_pairs={{0,16},{1,9},{2,18},{3,11},{4,20},{5,13},{6,22},{7,15},{8,24},{9,1... | collective-permute-start | bytes 122888 | tf_op jit(solution)/shard_map/ppermute | solution.py:204
  21.4 3.2 %collective-permute-start.8 = (bf16[1,40,128]{2,1,0:T(8,128)(2,1)S(1)}, bf16[1,40,128]{2,1,0:T(8,128)(2,1)S(1)}, u32[]{:S(2)}, u32[]{:S(2)}) collective-permute-start(bf16[1,40,128]{2,1,0:T(8,128)(2,1)S(1)} %dynamic-slice_convert_fusion.1), channel_id=1, source_target_pairs={{0,3},{1,2},{2,1},{3,0},{4,7},{5,6},{6,5},{7,4},{8,11},{9,10},{10,... | collective-permute-start | bytes 30728 | tf_op jit(solution)/shard_map/ppermute | solution.py:190
